TPU v7x, 32 devices: a whole 2x2x4 slice. The times are simulated.
32 devices in a mesh: shard: 4 (over y, x), context: 4 (over z), tensor: 2 (over core).
Axes of the slice: x: 2, y: 2, z: 4, core: 2. Of those that a mesh axis runs over, the one named last changes fastest.
Arguments:
- clips_in: bfloat16 [32, 8, 196, 768], P(('shard', 'tensor'), 'context'), may hold values from -6 to 6
- valid_clips: int32 [32], P(('shard', 'tensor')), may hold values 0 or 1
- norm_gains: float32 [3, 768], replicated, may hold values from 0.25 to 1.75
- norm_shifts: float32 [3, 768], replicated, may hold values from -4 to 4
- temporal_qkv: float32 [768, 3, 768], P(('shard', 'context', 'tensor')), may hold values from -0.21875 to 0.21875
- temporal_proj: float32 [768, 768], P(('shard', 'context', 'tensor')), may hold values from -0.4375 to 0.4375
- temporal_fc: float32 [768, 768], P(('shard', 'context', 'tensor')), may hold values from -0.21875 to 0.21875
- spatial_qkv: float32 [768, 3, 768], P(('shard', 'context', 'tensor')), may hold values from -0.21875 to 0.21875
- spatial_proj: float32 [768, 768], P(('shard', 'context', 'tensor')), may hold values from -1.75 to 1.75
- mlp_in: float32 [768, 3072], P(('shard', 'context'), 'tensor'), may hold values from -0.21875 to 0.21875
- mlp_out: float32 [768, 3072], P(('shard', 'context'), 'tensor'), may hold values from -0.3125 to 0.3125
- head_bias: float32 [2, 2, 768], replicated, may hold values from -6 to 6
- width_bias: float32 [3, 768], replicated, may hold values from -6 to 6
- fc_bias: float32 [768], replicated, may hold values from -6 to 6
- hidden_bias: float32 [3072], replicated, may hold values from -6 to 6
- cotangent: bfloat16 [32, 8, 196, 768], P(('shard', 'tensor'), 'context'), may hold values from -6 to 6
Outputs:
- output: bfloat16 [32, 8, 196, 768], P(('shard', 'tensor'), 'context')
- input_grad: bfloat16 [32, 8, 196, 768], P(('shard', 'tensor'), 'context')
- norm_gains_grad: float32 [3, 768], replicated
- norm_shifts_grad: float32 [3, 768], replicated
- temporal_qkv_grad: float32 [768, 3, 768], P(('shard', 'context', 'tensor'))
- temporal_proj_grad: float32 [768, 768], P(('shard', 'context', 'tensor'))
- temporal_fc_grad: float32 [768, 768], P(('shard', 'context', 'tensor'))
- spatial_qkv_grad: float32 [768, 3, 768], P(('shard', 'context', 'tensor'))
- spatial_proj_grad: float32 [768, 768], P(('shard', 'context', 'tensor'))
- mlp_in_grad: float32 [768, 3072], P(('shard', 'context'), 'tensor')
- mlp_out_grad: float32 [768, 3072], P(('shard', 'context'), 'tensor')
- head_bias_grad: float32 [2, 2, 768], replicated
- width_bias_grad: float32 [3, 768], replicated
- fc_bias_grad: float32 [768], replicated
- hidden_bias_grad: float32 [3072], replicated
Inputs may be any that keep to these rules, and one draw needn't show every extreme that they name: `valid_clips`: 1 marks a real clip, 0 a padding clip.
All inputs are finite; a program needn't handle non-finite values. No bound on the sum of `valid_clips` on one device may be relied on, other than what follows from the above.
Results may differ from a plain program's by a relative error of at most 0.02.
Values may be sent and summed in bfloat16 or wider, within the bound.
No kernel may reach another device: no remote copies, remote signals or barrier semaphores. Data moves between devices by JAX's collectives and lax.ppermute only.
A program may use at most 384 MiB of HBM per device.

v0:
```python
from functools import partial

import jax
import jax.numpy as jnp
from jax import lax
from jax.experimental import pallas as pl
from jax.experimental.pallas import tpu as pltpu
from jax.sharding import PartitionSpec as P

HEADS = 12
EPS = 1e-05
ALL = ("shard", "context", "tensor")
BF = jnp.bfloat16
F32 = jnp.float32
VMEM = 60 * 2**20

def mm(left, right, left_dim, right_dim):
    return lax.dot_general(left, right, (((left_dim,), (right_dim,)), ((), ())), preferred_element_type=F32)

def norm_stats(rows):
    centered = rows - jnp.mean(rows, axis=-1, keepdims=True)
    inv = lax.rsqrt(jnp.mean(centered * centered, axis=-1, keepdims=True) + EPS)
    return centered * inv, inv

def mlp_kernel(x_ref, cot_ref, keep_ref, gain_ref, shift_ref, w_ref, hb_ref, wb_ref,
               out_ref, g2_ref, db_ref, dw_ref, dhb_ref, sums_ref,
               a_ref, at_ref, dm_ref, dmt_ref, m_ref, da_ref, h_ref, du_ref, *, rb, chunks):
    step = pl.program_id(0)
    T, D = x_ref.shape
    nb = T // rb
    blocks, _, both, hc = w_ref.shape
    half = both // 2

    @pl.when(step == 0)
    def _():
        def body(i, c):
            r = pl.ds(pl.multiple_of(i * rb, 16), rb)
            unit, _ = norm_stats(x_ref[r, :])
            a = (unit * gain_ref[...] + shift_ref[...]).astype(BF)
            a_ref[r, :] = a
            dm = (keep_ref[0, 0] * cot_ref[r, :].astype(F32)).astype(BF)
            dm_ref[r, :] = dm
            return c
        lax.fori_loop(0, nb, body, 0)
        at_ref[...] = a_ref[...].T
        dmt_ref[...] = dm_ref[...].T

    win = w_ref[:, 0, :half, :].reshape(D, hc)
    wout = w_ref[:, 0, half:, :].reshape(D, hc)
    hb = hb_ref[...]
    tot = jnp.zeros((1, hc), F32)
    for i in range(nb):
        r = slice(i * rb, (i + 1) * rb)
        u = mm(a_ref[r, :], win, 1, 0) + hb
        cdf = 0.5 * (1.0 + lax.erf(u * (2 ** -0.5)))
        h = (u * cdf).astype(BF)
        pdf = jnp.exp(-0.5 * u * u) * ((2 * jnp.pi) ** -0.5)
        dh = mm(dm_ref[r, :], wout, 1, 0)
        du = ((cdf + u * pdf) * dh).astype(BF)
        h_ref[r, :] = h
        du_ref[r, :] = du
        tot += jnp.sum(du.astype(F32), axis=0, keepdims=True)
        m = mm(h, wout, 1, 1)
        da = mm(du, win, 1, 1)
        @pl.when(step == 0)
        def _():
            m_ref[r, :] = m
            da_ref[r, :] = da
        @pl.when(step > 0)
        def _():
            m_ref[r, :] += m
            da_ref[r, :] += da
    dhb_ref[...] = tot
    dw_ref[0, :, :half, :] = mm(at_ref[...], du_ref[...], 1, 0).astype(BF).reshape(blocks, half, hc)
    dw_ref[0, :, half:, :] = mm(dmt_ref[...], h_ref[...], 1, 0).astype(BF).reshape(blocks, half, hc)

    @pl.when(step == chunks - 1)
    def _():
        k = keep_ref[0, 0]
        def body(i, c):
            r = pl.ds(pl.multiple_of(i * rb, 16), rb)
            x = x_ref[r, :]
            out_ref[r, :] = (k * (x + (m_ref[r, :] + wb_ref[...]))).astype(BF)
            g3 = k * cot_ref[r, :].astype(F32)
            da = da_ref[r, :]
            unit, inv = norm_stats(x)
            sc = da * gain_ref[...]
            into = inv * (sc - jnp.mean(sc, axis=-1, keepdims=True) - unit * jnp.mean(sc * unit, axis=-1, keepdims=True))
            g2 = g3 + into
            g2_ref[r, :] = g2
            low = g2.astype(BF)
            db_ref[r, :] = low
            return (c[0] + jnp.sum(da * unit, axis=0, keepdims=True),
                    c[1] + jnp.sum(da, axis=0, keepdims=True),
                    c[2] + jnp.sum(dm_ref[r, :].astype(F32), axis=0, keepdims=True),
                    c[3] + jnp.sum(low.astype(F32), axis=0, keepdims=True))
        z = jnp.zeros((1, D), F32)
        c = lax.fori_loop(0, nb, body, (z, z, z, z))
        for j in range(4):
            sums_ref[j:j+1, :] = c[j]

def mlp(x2, cot, keep, gain, shift, w4, hb, wb):
    T, D = x2.shape
    B, H2, R, C = w4.shape
    rb = T // 4 if T % 64 == 0 else T
    hc = next(w for w in (768, 512, 384, 256, 128) if C % w == 0)
    per = C // hc
    chunks = H2 * per
    full = lambda *s: pl.BlockSpec(s, lambda j: (0,) * len(s), pipeline_mode=pl.Buffered(1))
    wspec = pl.BlockSpec((B, 1, R, hc), lambda j: (0, j // per, 0, j % per))
    dspec = pl.BlockSpec((1, B, R, hc), lambda j: (j // per, 0, 0, j % per))
    hspec = pl.BlockSpec((1, hc), lambda j: (0, j))
    return pl.pallas_call(
        partial(mlp_kernel, rb=rb, chunks=chunks),
        grid=(chunks,),
        in_specs=[full(T, D), full(T, D), pl.BlockSpec(memory_space=pltpu.SMEM), full(1, D), full(1, D), wspec, hspec, full(1, D)],
        out_specs=[full(T, D), full(T, D), full(T, D), dspec, hspec, full(8, D)],
        out_shape=(sds(T, D), sds(T, D, t=F32), sds(T, D), sds(H2, B, R, C), sds(1, H2 * C, t=F32), sds(8, D, t=F32)),
        scratch_shapes=[pltpu.VMEM((T, D), BF), pltpu.VMEM((D, T), BF), pltpu.VMEM((T, D), BF), pltpu.VMEM((D, T), BF),
                        pltpu.VMEM((T, D), F32), pltpu.VMEM((T, D), F32), pltpu.VMEM((T, hc), BF), pltpu.VMEM((T, hc), BF)],
        compiler_params=pltpu.CompilerParams(vmem_limit_bytes=VMEM),
        cost_estimate=cost(75),
    )(x2, cot, keep, gain, shift, w4, hb, wb)
LANES = 128
LOW = -1e30

def once(*s):
    return pl.BlockSpec(s, lambda j: (0,) * len(s), pipeline_mode=pl.Buffered(1))

def column(rows, cols, at):
    return pl.BlockSpec((rows, cols), lambda j: (0, at), pipeline_mode=pl.Buffered(1))

def sds(*s, t=BF):
    return jax.ShapeDtypeStruct(s, t)

def cost(us):
    return pl.CostEstimate(flops=us * 10**9, bytes_accessed=0, transcendentals=0)

def call(body, us, grid, ins, outs, shapes, scratch=()):
    return pl.pallas_call(body, grid=(grid,), in_specs=ins, out_specs=outs, out_shape=shapes, scratch_shapes=list(scratch),
                          compiler_params=pltpu.CompilerParams(vmem_limit_bytes=VMEM), cost_estimate=cost(us))

def qkv_store(a, wqkv, hb_ref, dst, rows, D):
    packed = mm(a, wqkv, 1, 0)
    dst[rows, :D] = (packed[:, :D] + hb_ref[0:1, :]).astype(BF)
    dst[rows, D:2 * D] = packed[:, D:2 * D].astype(BF)
    dst[rows, 2 * D:] = (packed[:, 2 * D:] + hb_ref[1:2, :]).astype(BF)

def lane_masks(head, value):
    lane = lax.broadcasted_iota(jnp.int32, (1, LANES), 1)
    return [jnp.where(lane // head == i, value, 0.0).astype(BF) for i in range(LANES // head)]

def sf_kernel(x_ref, gain_ref, shift_ref, wqkv_ref, wproj_ref, hb_ref, wb_ref, a_ref, qkv_ref, o_ref, x2_ref, *, fb, real, head, scale):
    M, D = x_ref.shape
    P = M // fb
    unit, _ = norm_stats(x_ref[...])
    a = (unit * gain_ref[...] + shift_ref[...]).astype(BF)
    a_ref[...] = a
    qkv_store(a, wqkv_ref[...], hb_ref, qkv_ref, slice(0, M), D)
    col = lax.broadcasted_iota(jnp.int32, (1, P), 1)
    hide = jnp.where(col < real, 0.0, LOW)
    ones = lane_masks(head, 1.0)
    for f in range(fb):
        r = slice(f * P, (f + 1) * P)
        for j in range(D // LANES):
            q = qkv_ref[r, j * LANES:(j + 1) * LANES]
            k = qkv_ref[r, D + j * LANES:D + (j + 1) * LANES]
            v = qkv_ref[r, 2 * D + j * LANES:2 * D + (j + 1) * LANES]
            o = None
            for m in ones:
                s = mm(q * m, k, 1, 1) * scale + hide
                p = jnp.exp(s - jnp.max(s, axis=-1, keepdims=True))
                p = (p * (1.0 / jnp.sum(p, axis=-1, keepdims=True))).astype(BF)
                part = mm(p, v * m, 1, 0)
                o = part if o is None else o + part
            o_ref[r, j * LANES:(j + 1) * LANES] = o.astype(BF)
    x2_ref[...] = x_ref[...] + (mm(o_ref[...], wproj_ref[...], 1, 1) + wb_ref[...])

def spatial_forward(x1, gain, shift, w, hb, wb, *, frames, real, head, scale, fb=2):
    T, D = x1.shape
    M = T // frames * fb
    blk = lambda w: pl.BlockSpec((M, w), lambda j: (j, 0))
    return call(partial(sf_kernel, fb=fb, real=real, head=head, scale=scale), 30, frames // fb,
        [blk(D), once(1, D), once(1, D), column(D, 3 * D, 0), column(D, D, 3), once(2, D), once(1, D)],
        [blk(D), blk(3 * D), blk(D), blk(D)], (sds(T, D), sds(T, 3 * D), sds(T, D), sds(T, D, t=F32)))(
        x1, gain, shift, w, w, hb, wb)

def norm_back_store(x, gain, da, base, sums_ref, at):
    unit, inv = norm_stats(x)
    sc = da * gain
    into = inv * (sc - jnp.mean(sc, axis=-1, keepdims=True) - unit * jnp.mean(sc * unit, axis=-1, keepdims=True))
    sums_ref[at:at + 1, :] += jnp.sum(da * unit, axis=0, keepdims=True)
    sums_ref[at + 1:at + 2, :] += jnp.sum(da, axis=0, keepdims=True)
    return base + into

def add_sum(sums_ref, at, rows):
    sums_ref[at:at + 1, :] += jnp.sum(rows.astype(F32), axis=0, keepdims=True)

def sb_kernel(g2_ref, db_ref, qkv_ref, x_ref, gain_ref, wqkv_ref, wproj_ref, *rest, fb, real, head, scale):
    dqkv_ref, g1_ref, dz_ref, sums_ref, do_ref = rest[-5:]
    M, D = x_ref.shape
    P = M // fb
    @pl.when(pl.program_id(0) == 0)
    def _():
        sums_ref[...] = jnp.zeros_like(sums_ref)
    do_ref[...] = mm(db_ref[...], wproj_ref[...], 1, 0).astype(BF)
    row = lax.broadcasted_iota(jnp.int32, (P, 1), 0)
    hide = jnp.where(row < real, 0.0, LOW)
    ones = lane_masks(head, 1.0)
    for f in range(fb):
        r = slice(f * P, (f + 1) * P)
        for j in range(D // LANES):
            ls = [slice(i * D + j * LANES, i * D + (j + 1) * LANES) for i in range(3)]
            q, k, v = [qkv_ref[r, l] for l in ls]
            do = do_ref[r, ls[0]]
            dq = dk = dv = 0.0
            for m in ones:
                qm = q * m
                dom = do * m
                s = mm(k, qm, 1, 1) * scale + hide
                p = jnp.exp(s - jnp.max(s, axis=0, keepdims=True))
                p = p * (1.0 / jnp.sum(p, axis=0, keepdims=True))
                dp = mm(v, dom, 1, 1)
                ds = (p * (dp - jnp.sum(p * dp, axis=0, keepdims=True))).astype(BF)
                dv = dv + mm(p.astype(BF), dom, 1, 0)
                dk = dk + mm(ds, qm, 1, 0)
                dq = dq + mm(ds, k * m, 0, 0)
            dqkv_ref[r, ls[0]] = (dq * scale).astype(BF)
            dqkv_ref[r, ls[1]] = (dk * scale).astype(BF)
            dqkv_ref[r, ls[2]] = dv.astype(BF)
    add_sum(sums_ref, 2, dqkv_ref[:, :D])
    add_sum(sums_ref, 3, dqkv_ref[:, 2 * D:])
    da = mm(dqkv_ref[...], wqkv_ref[...], 1, 1)
    g1 = norm_back_store(x_ref[...], gain_ref[...], da, g2_ref[...], sums_ref, 0)
    g1_ref[...] = g1
    low = g1.astype(BF)
    dz_ref[...] = low
    add_sum(sums_ref, 4, low)

def spatial_backward(g2, db, qkv, x1, *, gain, w, frames, real, head, scale, part, held=None, fb=2):
    T, D = x1.shape
    M = T // frames * fb
    nb = frames // fb // 2
    blk = lambda w: pl.BlockSpec((M, w), lambda j: (j + part * nb, 0))
    kept = [] if held is None else list(held[:3])
    return pl.pallas_call(
        partial(sb_kernel, fb=fb, real=real, head=head, scale=scale), grid=(nb,),
        in_specs=[blk(D), blk(D), blk(3 * D), blk(D), once(1, D), column(D, 3 * D, 0), column(D, D, 3)]
        + [pl.BlockSpec(memory_space=pl.ANY)] * len(kept),
        out_specs=[blk(3 * D), blk(D), blk(D), once(8, D)],
        out_shape=(sds(T, 3 * D), sds(T, D, t=F32), sds(T, D), sds(8, D, t=F32)),
        scratch_shapes=[pltpu.VMEM((M, D), BF)],
        input_output_aliases={7 + i: i for i in range(len(kept))},
        compiler_params=pltpu.CompilerParams(vmem_limit_bytes=VMEM), cost_estimate=cost(24),
    )(g2, db, qkv, x1, gain, w, w, *kept)

def over_frames(op, rows, slot):
    shift = slot
    while shift < LANES:
        rows = op(rows, pltpu.roll(rows, shift, 1))
        shift *= 2
    return rows

def tf_kernel(x_ref, gain_ref, shift_ref, wqkv_ref, wproj_ref, wfc_ref, hb_ref, wb_ref, fcb_ref, e_ref, b_ref,
              a_ref, qkv_ref, p_ref, o_ref, y_ref, x1_ref, all_ref, prod_ref, xs_ref, *, fb, nb, frames, slot, scale):
    M, D = x_ref.shape
    P = M // fb
    step = pl.program_id(0)
    @pl.when(step < nb)
    def _():
        x = x_ref[...].astype(F32)
        unit, _ = norm_stats(x)
        a = (unit * gain_ref[...] + shift_ref[...]).astype(BF)
        a_ref[...] = a
        qkv_store(a, wqkv_ref[...], hb_ref, qkv_ref, slice(0, M), D)
        all_ref[pl.ds(pl.multiple_of(step * M, M), M), :] = qkv_ref[...]
        xs_ref[pl.ds(pl.multiple_of(step * M, M), M), :] = x_ref[...]
    @pl.when(step >= nb)
    def _():
        base = pl.multiple_of((step - nb) * M, M)
        for f in range(fb):
            q = all_ref[pl.ds(base + f * P, P), :D]
            for g in range(frames):
                prod_ref[f * P:(f + 1) * P, g * D:(g + 1) * D] = q * all_ref[g * P:(g + 1) * P, D:2 * D]
        s = mm(prod_ref[...], e_ref[...], 1, 0) * scale
        p = jnp.exp(s - over_frames(jnp.maximum, s, slot))
        p = p * (1.0 / over_frames(jnp.add, p, slot))
        p_ref[...] = p
        low = p.astype(BF)
        o = [None] * fb
        for g in range(frames):
            wide = mm(low, b_ref[:, g * D:(g + 1) * D], 1, 0)
            v = all_ref[g * P:(g + 1) * P, 2 * D:].astype(F32)
            for f in range(fb):
                part = wide[f * P:(f + 1) * P] * v
                o[f] = part if g == 0 else o[f] + part
        for f in range(fb):
            o_ref[f * P:(f + 1) * P, :] = o[f].astype(BF)
        y = (mm(o_ref[...], wproj_ref[...], 1, 1) + wb_ref[...]).astype(BF)
        y_ref[...] = y
        z = (mm(y, wfc_ref[...], 1, 0) + fcb_ref[...]).astype(BF)
        x1_ref[...] = xs_ref[pl.ds(base, M), :].astype(F32) + z.astype(F32)

def temporal_tables(D, head, frames):
    slot = LANES // frames
    lane = jnp.arange(LANES)
    feat = jnp.arange(frames * D)
    e = ((feat[:, None] // D == lane[None, :] // slot) & ((feat[:, None] % D) // head == lane[None, :] % slot)).astype(BF)
    return e, e.T

def temporal_forward(x, gain, shift, w, hb, wb, fcb, e, b, *, frames, scale, fb=2):
    T, D = x.shape
    M = T // frames * fb
    nb = frames // fb
    first = lambda w: pl.BlockSpec((M, w), lambda j: (jnp.minimum(j, nb - 1), 0))
    last = lambda w: pl.BlockSpec((M, w), lambda j: (jnp.maximum(j - nb, 0), 0))
    return call(partial(tf_kernel, fb=fb, nb=nb, frames=frames, slot=LANES // frames, scale=scale), 44, 2 * nb,
        [first(D), once(1, D), once(1, D), column(D, 3 * D, 0), column(D, D, 3), column(D, D, 4), once(2, D), once(1, D), once(1, D), once(*e.shape), once(*b.shape)],
        [first(D), first(3 * D), last(LANES), last(D), last(D), last(D)],
        (sds(T, D), sds(T, 3 * D), sds(T, LANES, t=F32), sds(T, D), sds(T, D), sds(T, D, t=F32)),
        [pltpu.VMEM((T, 3 * D), BF), pltpu.VMEM((M, frames * D), BF), pltpu.VMEM((T, D), BF)])(
        x, gain, shift, w, w, w, hb, wb, fcb, e, b)

def zero_first(*refs):
    @pl.when(pl.program_id(0) == 0)
    def _():
        for ref in refs:
            ref[...] = jnp.zeros_like(ref)

def pull_kernel(dz_ref, wproj_ref, wfc_ref, dy_ref, do_ref, sums_ref):
    zero_first(sums_ref)
    dy = mm(dz_ref[...], wfc_ref[...], 1, 1).astype(BF)
    dy_ref[...] = dy
    add_sum(sums_ref, 4, dy)
    do_ref[...] = mm(dy, wproj_ref[...], 1, 0).astype(BF)

def temporal_pull(dz, w, *, blocks=4):
    T, D = dz.shape
    blk = pl.BlockSpec((T // blocks, D), lambda j: (j, 0))
    return call(pull_kernel, 8, blocks, [blk, column(D, D, 3), column(D, D, 4)], [blk, blk, once(8, D)],
                (sds(T, D), sds(T, D), sds(8, D, t=F32)))(dz, w, w)

def tb_kernel(do_ref, qkv_ref, p_ref, e_ref, b_ref, dqkv_ref, sums_ref, dk_ref, dv_ref, prod_ref, *, fb, nb, frames, slot, scale):
    M = p_ref.shape[0]
    T, D = do_ref.shape
    P = M // fb
    step = pl.program_id(0)
    zero_first(sums_ref, dk_ref, dv_ref)
    base = pl.multiple_of(step * M, M)
    for f in range(fb):
        do = do_ref[pl.ds(base + f * P, P), :]
        for g in range(frames):
            prod_ref[f * P:(f + 1) * P, g * D:(g + 1) * D] = do * qkv_ref[g * P:(g + 1) * P, 2 * D:]
    dp = mm(prod_ref[...], e_ref[...], 1, 0)
    p = p_ref[...]
    ds = (p * (dp - over_frames(jnp.add, p * dp, slot))).astype(BF)
    low = p.astype(BF)
    dq = [0.0] * fb
    for g in range(frames):
        gr = slice(g * P, (g + 1) * P)
        wide_p = mm(low, b_ref[:, g * D:(g + 1) * D], 1, 0)
        wide_s = mm(ds, b_ref[:, g * D:(g + 1) * D], 1, 0)
        k = qkv_ref[gr, D:2 * D].astype(F32)
        dk, dv = dk_ref[gr, :], dv_ref[gr, :]
        for f in range(fb):
            fr = pl.ds(base + f * P, P)
            wp, ws = wide_p[f * P:(f + 1) * P], wide_s[f * P:(f + 1) * P]
            dv = dv + wp * do_ref[fr, :].astype(F32)
            dk = dk + ws * qkv_ref[fr, :D].astype(F32)
            dq[f] = dq[f] + ws * k
        dk_ref[gr, :] = dk
        dv_ref[gr, :] = dv
    for f in range(fb):
        low = (dq[f] * scale).astype(BF)
        add_sum(sums_ref, 2, low)
        dqkv_ref[pl.ds(base + f * P, P), :D] = low
    @pl.when(step == nb - 1)
    def _():
        for g in range(frames):
            gr = slice(g * P, (g + 1) * P)
            dqkv_ref[gr, D:2 * D] = (dk_ref[gr, :] * scale).astype(BF)
            low = dv_ref[gr, :].astype(BF)
            add_sum(sums_ref, 3, low)
            dqkv_ref[gr, 2 * D:] = low

def temporal_backward(do, qkv, p, e, b, *, frames, scale, fb=2):
    T, D = do.shape
    M = T // frames * fb
    nb = frames // fb
    return call(partial(tb_kernel, fb=fb, nb=nb, frames=frames, slot=LANES // frames, scale=scale), 40, nb,
        [once(T, D), once(T, 3 * D), pl.BlockSpec((M, LANES), lambda j: (j, 0)), once(*e.shape), once(*b.shape)],
        [once(T, 3 * D), once(8, D)], (sds(T, 3 * D), sds(8, D, t=F32)),
        [pltpu.VMEM((T, D), F32), pltpu.VMEM((T, D), F32), pltpu.VMEM((M, frames * D), BF)])(do, qkv, p, e, b)

def end_kernel(dqkv_ref, x_ref, g1_ref, gain_ref, wqkv_ref, out_ref, sums_ref):
    zero_first(sums_ref)
    da = mm(dqkv_ref[...], wqkv_ref[...], 1, 1)
    out = norm_back_store(x_ref[...].astype(F32), gain_ref[...], da, g1_ref[...], sums_ref, 0)
    out_ref[...] = out.astype(BF)

def temporal_end(dqkv, x, g1, gain, w, *, blocks=4):
    T, D = x.shape
    blk = lambda w: pl.BlockSpec((T // blocks, w), lambda j: (j, 0))
    return call(end_kernel, 12, blocks, [blk(3 * D), blk(D), blk(D), once(1, D), column(D, 3 * D, 0)], [blk(D), once(8, D)],
                (sds(T, D), sds(8, D, t=F32)))(dqkv, x, g1, gain, w)

def wg_kernel(*refs, starts, halves, rows):
    n = len(starts)
    a_refs, b_refs, out_ref, t_ref = refs[:n], refs[n:2 * n], refs[2 * n], refs[2 * n + 1]
    step = pl.program_id(0)
    for i in range(n):
        @pl.when(step == starts[i])
        def _():
            t_ref[...] = a_refs[i][...].T
        stop = starts[i + 1] if i + 1 < n else step + 1
        @pl.when((step >= starts[i]) & (step < stop))
        def _():
            res = mm(t_ref[...], b_refs[i][...], 1, 0)
            if rows:
                parts = res.reshape(-1, halves, rows, res.shape[-1])
                for h in range(halves):
                    out_ref[h] = parts[:, h].reshape(-1, res.shape[-1]).astype(BF)
            else:
                out_ref[0] = res.astype(BF)

def weight_grads(pairs, halves, rows, us):
    T, D = pairs[0][0].shape
    starts, steps = [], 0
    for a, b in pairs:
        starts.append(steps)
        steps += b.shape[1] // D
    cols = steps * D
    fits = rows % 8 == 0
    def chunk(i):
        many = pairs[i][1].shape[1] // D
        return pl.BlockSpec((T, D), lambda j: (0, jnp.clip(j - starts[i], 0, many - 1)))
    groups = halves if fits else 1
    out = call(partial(wg_kernel, starts=starts, halves=halves, rows=rows if fits else 0), us, steps,
        [once(T, D)] * len(pairs) + [chunk(i) for i in range(len(pairs))],
        [pl.BlockSpec((groups, D // groups, D), lambda j: (0, 0, j))], (sds(groups, D // groups, cols),),
        [pltpu.VMEM((D, T), BF)])(*[a for a, _ in pairs], *[b for _, b in pairs])[0]
    if fits:
        return out.reshape(halves, -1, rows, cols)
    return jnp.swapaxes(out.reshape(-1, halves, rows, cols), 0, 1)


def exchange(pieces, axis):
    size = len(pieces)
    return [pieces[0]] + [
        lax.ppermute(pieces[d], axis, [(i, i ^ d) for i in range(size)]) for d in range(1, size)
    ]


def in_order(pieces, axis, step=1):
    while step < len(pieces):
        swap = (lax.axis_index(axis) // step) % 2 == 1
        pieces = [jnp.where(swap, pieces[c ^ step], pieces[c]) for c in range(len(pieces))]
        step *= 2
    return pieces


def collect(array, axis, at=0, hold=()):
    pieces = exchange([array] * lax.axis_size(axis), axis)
    pieces = pieces[:1] + [after(piece, *hold) for piece in pieces[1:]]
    return jnp.stack(in_order(pieces, axis), axis=at)


def partner(array, axis, step):
    size = lax.axis_size(axis)
    return lax.ppermute(array, axis, [(i, i ^ step) for i in range(size)])


def far_first(array, axis):
    size = lax.axis_size(axis)
    step = size // 2
    out = array[None]
    while step:
        other = partner(out, axis, step)
        low = (lax.axis_index(axis) // step) % 2 == 0
        out = jnp.stack((jnp.where(low, out, other), jnp.where(low, other, out)), axis=1)
        out = out.reshape((-1,) + array.shape)
        step //= 2
    return out


def near_first(array, axis):
    size = lax.axis_size(axis)
    step = 1
    while step < size:
        blocks = array.reshape((-1, 2) + array.shape[1:])
        mine = (lax.axis_index(axis) // step) % 2
        send = lax.dynamic_index_in_dim(blocks, 1 - mine, 1, keepdims=False).astype(BF)
        keep = lax.dynamic_index_in_dim(blocks, mine, 1, keepdims=False)
        array = keep.astype(F32) + partner(send, axis, step).astype(F32)
        step *= 2
    return array[0]


def split_off(array, axis):
    place = lax.axis_index(axis)
    pieces = [
        lax.dynamic_index_in_dim(array, place ^ d, 0, keepdims=False)
        for d in range(lax.axis_size(axis))
    ]
    return exchange(pieces[:1] + [piece.astype(BF) for piece in pieces[1:]], axis)


def added(pieces, *hold):
    out = pieces[0].astype(F32)
    for piece in pieces[1:]:
        out = out + after(piece, *hold).astype(F32)
    return out


def shed(array, axis, hold=()):
    return added(split_off(array, axis), *hold)


def shed_at_once(array, axis):
    came = lax.all_to_all(array.astype(BF), axis, split_axis=0, concat_axis=0, tiled=True)
    return jnp.sum(came.astype(F32), axis=0)


def after(array, *others):
    return lax.optimization_barrier((array,) + others)[0]


def plus_others(array, axis):
    came = exchange([array] * lax.axis_size(axis), axis)
    return sum(came[1:], came[0])


def local(
    clips_in,
    valid_clips,
    norm_gains,
    norm_shifts,
    temporal_qkv,
    temporal_proj,
    temporal_fc,
    spatial_qkv,
    spatial_proj,
    mlp_in,
    mlp_out,
    head_bias,
    width_bias,
    fc_bias,
    hidden_bias,
    cotangent,
):
    held, frames_held, places, width = clips_in.shape
    head = width // HEADS
    scale = head ** (-0.5)
    across = lax.axis_size("context")
    halves = lax.axis_size("tensor")
    place = lax.axis_index("context")
    own_rows = temporal_qkv.shape[0]
    in_rows, in_cols = mlp_in.shape
    spread = held % across == 0
    clips = held // across if spread else held
    share = 1.0 if spread else 1.0 / across
    frames = frames_held * across
    padded = -(-places // 16) * 16

    def to_clips(array):
        array = jnp.swapaxes(array, 1, 2)
        if spread:
            array = lax.all_to_all(array, "context", split_axis=0, concat_axis=0, tiled=True)
            return array.reshape((across, clips) + array.shape[1:])
        return lax.all_gather(array, "context", axis=0)

    def fill(array):
        array = jnp.swapaxes(array, 1, 2).reshape(frames, places, width)
        array = jnp.pad(array, ((0, 0), (0, padded - places), (0, 0)))
        return array.reshape(frames * padded, width)

    def by_place(array):
        array = array.reshape(across, frames_held, padded, width)[:, :, :places]
        return jnp.swapaxes(array, 1, 2)

    def from_clips(array):
        array = by_place(array)
        if spread:
            array = lax.all_to_all(array, "context", split_axis=0, concat_axis=0, tiled=True)
        else:
            array = lax.dynamic_slice_in_dim(array, place, 1, 0)
        return jnp.swapaxes(array, 1, 2)

    def send_back(array):
        array = by_place(array)
        if spread:
            return split_off(array, "context")
        return [lax.dynamic_index_in_dim(array, place, 0, keepdims=False)]

    def sent_back(pieces):
        return jnp.swapaxes(jnp.stack(in_order(pieces, "context")), 1, 2)

    if spread:
        valid = lax.dynamic_slice_in_dim(valid_clips, place * clips, clips, 0)
    else:
        valid = valid_clips
    keep = valid.astype(F32)

    def flat3(weight):
        return weight.reshape(own_rows, 3 * width)

    def by_shard(d):
        return d.reshape((lax.axis_size("shard"), across) + d.shape[1:])

    t_own = jnp.concatenate((flat3(temporal_qkv), temporal_proj, temporal_fc), axis=1).astype(BF)
    s_own = jnp.concatenate((flat3(spatial_qkv), spatial_proj), axis=1).astype(BF)
    mlp_own = jnp.concatenate((mlp_in, mlp_out), axis=0).astype(BF)
    first = collect(jnp.concatenate((t_own, s_own), axis=1), "context")
    t_first, s_first = first[..., : t_own.shape[1]], first[..., t_own.shape[1] :]
    mlp_all = lax.all_gather(after(mlp_own, first), ALL, axis=0, tiled=True)
    mlp_all = mlp_all.reshape(-1, halves, 2 * in_rows, in_cols)

    rows_in = to_clips(after(clips_in, first))
    t_chips = collect(t_first, "shard", hold=(rows_in,))
    t_all = collect(t_chips, "tensor", 2).reshape(-1, t_own.shape[1])
    pulled = to_clips(after(cotangent, rows_in))
    ones, spread_ones = temporal_tables(width, head, frames)

    def one_clip(x, pull, keep_one):
        sizes = dict(frames=frames, scale=scale)
        gain = [norm_gains[i : i + 1] for i in range(3)]
        shift = [norm_shifts[i : i + 1] for i in range(3)]
        wide = [width_bias[i : i + 1] for i in range(3)]
        x = fill(x)
        a_t, qkv_t, probs, o_t, y, x1 = temporal_forward(
            x, gain[0], shift[0], t_all, head_bias[0], wide[0], fc_bias[None], ones, spread_ones,
            **sizes,
        )
        s_all = collect(after(s_first, rows_in), "shard", hold=(x1,))
        s_all = collect(s_all, "tensor", 2).reshape(-1, s_own.shape[1])
        sizes_s = dict(sizes, real=places, head=head)
        a_s, qkv_s, o_s, x2 = spatial_forward(
            x1, gain[1], shift[1], s_all, head_bias[1], wide[1], **sizes_s
        )
        out, g2, db, d_m, d_hidden, sums_m = mlp(
            x2, fill(after(pull, x1)), keep_one.reshape(1, 1), gain[2], shift[2], mlp_all, hidden_bias[None], wide[2]
        )
        back_s = partial(spatial_backward, gain=gain[1], w=s_all, **sizes_s)
        grads_of = partial(weight_grads, halves=halves, rows=own_rows)
        d_m = split_off(share * d_m if share != 1.0 else d_m, "tensor")
        back = send_back(out)
        half = back_s(g2, db, qkv_s, x1, part=0)
        d_m = added(d_m, half[0]).astype(BF)
        tied = after(db, d_m, half[0], *back[1:2])
        d_m = split_off(by_shard(d_m), "shard")
        d_qkv_s, g1, dz, sums_s = back_s(g2, tied, qkv_s, x1, part=1, held=half)
        sums_s = sums_s + half[3]
        tied = after(d_qkv_s, *d_m[1:3], *back[2:3])
        d_s = share * grads_of([(a_s, tied), (db, o_s)], us=12)
        tied = after(dz, d_s, *d_m[3:])
        d_s = split_off(d_s, "tensor")
        dy, do, sums_y = temporal_pull(tied, t_all)
        d_s = added(d_s, dy).astype(BF)
        tied = after(dy, d_s, *back[3:])
        d_s = split_off(by_shard(d_s), "shard")
        d_r = share * grads_of([(tied, o_t), (y, dz)], us=6)
        output = sent_back([after(piece, d_r) for piece in back])
        d_s = added(d_s, d_r).astype(BF)
        d_m = added(d_m, d_r).astype(BF)
        tied = after(do, d_m, d_s, output)
        d_m = shed_at_once(d_m, "context")
        d_s = split_off(d_s, "context")
        d_r = split_off(d_r, "tensor")
        d_qkv_t, sums_q = temporal_backward(tied, qkv_t, probs, ones, spread_ones, **sizes)
        d_s = added(d_s, d_qkv_t)
        d_r = added(d_r, d_qkv_t).astype(BF)
        tied = after(d_qkv_t, d_r, d_s, d_m)
        d_r = split_off(by_shard(d_r), "shard")
        d_q = share * grads_of([(a_t, tied)], us=9)
        d_r = added(d_r, d_q)
        tied, d_q = lax.optimization_barrier((d_qkv_t, d_q, d_r))[:2]
        d_q = split_off(d_q, "tensor")
        into, sums_x = temporal_end(tied, x, g1, gain[0], t_all)
        d_q = added(d_q, into).astype(BF)
        into = from_clips(after(into, d_q))
        small = share * jnp.concatenate(
            (sums_m, sums_s, sums_y + sums_q + sums_x, d_hidden.reshape(-1, width)), axis=0
        )
        d_q = added(split_off(by_shard(d_q), "shard"))
        small = plus_others(plus_others(small, "tensor"), "shard")
        d_r = jnp.concatenate((d_r.astype(BF), d_q.astype(BF)), axis=-1)
        d_r = shed(d_r, "context")
        small = plus_others(after(small, d_q), "context")
        return output, into, (d_r, d_s, d_m, small)

    parts = [one_clip(rows_in[:, i], pulled[:, i], keep[i]) for i in range(clips)]
    output, input_grad = [
        jnp.stack([part[n] for part in parts], axis=1).reshape(clips_in.shape) for n in (0, 1)
    ]
    grads = parts[0][2]
    for part in parts[1:]:
        grads = jax.tree.map(jnp.add, grads, part[2])
    d_t, d_s, d_mlp, small = grads
    d_t_rest, d_t_qkv = d_t[:, : 2 * width], d_t[:, 2 * width :]
    m, s, t = small[0:8], small[8:16], small[16:24]
    return (
        output,
        input_grad,
        jnp.stack((t[0], s[0], m[0])),
        jnp.stack((t[1], s[1], m[1])),
        d_t_qkv.reshape(own_rows, 3, width),
        d_t_rest[:, :width],
        d_t_rest[:, width:],
        d_s[:, : 3 * width].reshape(own_rows, 3, width),
        d_s[:, 3 * width :],
        d_mlp[:in_rows],
        d_mlp[in_rows:],
        jnp.stack((t[2:4], s[2:4])),
        jnp.stack((t[4], m[3], m[2])),
        s[4],
        small[24:].reshape(-1),
    )


def solution(mesh):
    clip = P(("shard", "tensor"), "context", None, None)
    row, block = P(ALL, None), P(("shard", "context"), "tensor")
    deep, whole = P(ALL, None, None), P()
    weights = (deep, row, row, deep, row, block, block)
    in_specs = (clip, P(("shard", "tensor")), whole, whole) + weights + (whole,) * 4 + (clip,)
    out_specs = (clip, clip, whole, whole) + weights + (whole,) * 4
    return jax.shard_map(local, mesh=mesh, in_specs=in_specs, out_specs=out_specs, check_vma=False)
```

profile of v0, /device:TPU:0, one launch (start us, length us, event | category | flops | bytes accessed | tf_op | source)
XLA Modules:
  0.0 690.6 jit_solution(14100495136960633258)
XLA Ops:
  11.8 3.0 collective-permute-start.2
  14.8 2.6 collective-permute-start.1
  17.4 11.5 %collective-permute-done.2 = bf16[24,6912]{1,0:T(8,128)(2,1)S(1)} collective-permute-done((bf16[24,6912]{1,0:T(8,128)(2,1)S(1)}, bf16[24,6912]{1,0:T(8,128)(2,1)S(1)}, u32[]{:S(2)}, u32[]{:S(2)}) %collective-permute-start.2) | collective-permute-done | bytes 331808 | tf_op jit(solution)/shard_map/ppermute | solution.py:450
  29.0 11.7 %collective-permute-done.1 = bf16[24,6912]{1,0:T(8,128)(2,1)S(1)} collective-permute-done((bf16[24,6912]{1,0:T(8,128)(2,1)S(1)}, bf16[24,6912]{1,0:T(8,128)(2,1)S(1)}, u32[]{:S(2)}, u32[]{:S(2)}) %collective-permute-start.1) | collective-permute-done | bytes 331808 | tf_op jit(solution)/shard_map/ppermute | solution.py:450
  42.0 8.7 %all-to-all-start = ((bf16[4,196,2,768]{3,2,1,0:T(2,128)(2,1)}), bf16[4,196,2,768]{3,2,1,0:T(2,128)(2,1)S(1)}, u32[]{:S(2)}, u32[]{:S(2)}) async-start(bf16[4,196,2,768]{3,2,1,0:T(2,128)(2,1)} %bitcast.219), calls=%async_computation | async-start | bytes 4816896 | tf_op jit(solution)/shard_map/all_to_all | solution.py:568
  59.9 13.1 %collective-permute-done.5 = bf16[4,24,3840]{2,1,0:T(8,128)(2,1)S(1)} collective-permute-done((bf16[4,24,3840]{2,1,0:T(8,128)(2,1)}, bf16[4,24,3840]{2,1,0:T(8,128)(2,1)S(1)}, u32[]{:S(2)}, u32[]{:S(2)}) %collective-permute-start.5) | collective-permute-done | bytes 737312 | tf_op jit(solution)/shard_map/ppermute | solution.py:450
  73.0 42.9 %all-to-all-done = bf16[4,196,2,768]{3,2,1,0:T(2,128)(2,1)S(1)} async-done(((bf16[4,196,2,768]{3,2,1,0:T(2,128)(2,1)}), bf16[4,196,2,768]{3,2,1,0:T(2,128)(2,1)S(1)}, u32[]{:S(2)}, u32[]{:S(2)}) %all-to-all-start) | async-done | bytes 2408480 | tf_op jit(solution)/shard_map/all_to_all | solution.py:568
  122.5 5.1 and_convert_fusion.1.e_ref
  133.0 4.7 all-to-all-start.1
  140.5 2.1 select_bitcast_fusion.1
  143.2 2.9 copy.41
  146.1 43.1 %shard_map.271 = (bf16[1664,768]{1,0:T(8,128)(2,1)}, bf16[1664,2304]{1,0:T(8,128)(2,1)}, f32[1664,128]{1,0:T(8,128)}, bf16[1664,768]{1,0:T(8,128)(2,1)}, bf16[1664,768]{1,0:T(8,128)(2,1)}, /*index=5*/f32[1664,768]{1,0:T(8,128)}) custom-call(bf16[1664,768]{1,0:T(8,128)(2,1)} %bitcast.216, f32[1,768]{1,0:T(1,128)} %get-tuple-element.239.gain_ref, ...), custom_call_target="tpu_custom_call" | custom-call | flops 44000002048 | tf_op jit(solution)/shard_map/pallas_call | solution.py:317
  194.0 14.8 %all-to-all-done.1 = bf16[4,196,2,768]{3,2,1,0:T(2,128)(2,1)} async-done(((bf16[4,196,2,768]{3,2,1,0:T(2,128)(2,1)}), bf16[4,196,2,768]{3,2,1,0:T(2,128)(2,1)}, u32[]{:S(2)}, u32[]{:S(2)}) %all-to-all-start.1) | async-done | bytes 2408480 | tf_op jit(solution)/shard_map/all_to_all | solution.py:568
  214.9 2.6 copy.42
  217.4 25.4 %shard_map.272 = (bf16[1664,768]{1,0:T(8,128)(2,1)}, bf16[1664,2304]{1,0:T(8,128)(2,1)}, bf16[1664,768]{1,0:T(8,128)(2,1)}, f32[1664,768]{1,0:T(8,128)}) custom-call(f32[1664,768]{1,0:T(8,128)} %get-tuple-element.91.x_ref, f32[1,768]{1,0:T(1,128)} %get-tuple-element.240.gain_ref, f32[1,768]{1,0:T(1,128)} %get-tuple-element.247.shift_ref, ...), custom_call_target="tpu_custom_call" | custom-call | flops 30000001024 | tf_op jit(solution)/shard_map/pallas_call | solution.py:183
  242.8 74.4 %shard_map.273 = (bf16[1664,768]{1,0:T(8,128)(2,1)}, f32[1664,768]{1,0:T(8,128)}, bf16[1664,768]{1,0:T(8,128)(2,1)}, bf16[2,16,96,1536]{3,2,1,0:T(8,128)(2,1)}, f32[1,3072]{1,0:T(1,128)}, /*index=5*/f32[8,768]{1,0:T(8,128)}) custom-call(f32[1664,768]{1,0:T(8,128)} %get-tuple-element.96.x_ref, bf16[1664,768]{1,0:T(8,128)(2,1)} %bitcast.218, ...), custom_call_target="tpu_custom_call" | custom-call | flops 74999996416 | tf_op jit(solution)/shard_map/pallas_call | solution.py:113
  317.2 5.0 dynamic-slice_bitcast_fusion
  325.4 23.7 %shard_map.274 = (bf16[1664,2304]{1,0:T(8,128)(2,1)}, f32[1664,768]{1,0:T(8,128)}, bf16[1664,768]{1,0:T(8,128)(2,1)}, f32[8,768]{1,0:T(8,128)}) custom-call(f32[1664,768]{1,0:T(8,128)} %get-tuple-element.101.g2_ref, bf16[1664,768]{1,0:T(8,128)(2,1)} %get-tuple-element.107.db_ref.refs_1_, bf16[1664,2304]{1,0:T(8,128)(2,1)} %get-tuple-element.104.qkv_ref, ...), custom_call_target="tpu_custom_call" | custom-call | flops 24000000000 | tf_op jit(solution)/shard_map/pallas_call | solution.py:246
  349.1 5.3 fusion
  361.0 23.5 %shard_map.275 = (bf16[1664,2304]{1,0:T(8,128)(2,1)}, f32[1664,768]{1,0:T(8,128)}, bf16[1664,768]{1,0:T(8,128)(2,1)}, f32[8,768]{1,0:T(8,128)}) custom-call(f32[1664,768]{1,0:T(8,128)} %get-tuple-element.101.g2_ref, bf16[1664,768]{1,0:T(8,128)(2,1)} %get-tuple-element.107.db_ref.refs_1_, ...), custom_call_target="tpu_custom_call", output_to_operand_aliasing={{0}: (7, {}), {1}: (8, {}), {2}: (9, {})} | custom-call | flops 24000000000 | tf_op jit(solution)/shard_map/pallas_call | solution.py:246
  387.4 16.3 %shard_map.276 = bf16[2,384,3072]{2,1,0:T(8,128)(2,1)} custom-call(bf16[1664,768]{1,0:T(8,128)(2,1)} %get-tuple-element.111.refs_0_, bf16[1664,768]{1,0:T(8,128)(2,1)} %get-tuple-element.107.db_ref.refs_1_, bf16[1664,2304]{1,0:T(8,128)(2,1)} %get-tuple-element.113.refs_2_, bf16[1664,768]{1,0:T(8,128)(2,1)} %get-tuple-element.114.refs_3_), custom_call_target="tpu_custom_call" | custom-call | flops 12000000000 | tf_op jit(solution)/shard_map/pallas_call | solution.py:438
  403.7 3.2 dynamic-slice_bitcast_fusion.1
  412.9 2.4 collective-permute-start.11
  416.0 20.6 %collective-permute-done.17 = bf16[4,96,1536]{2,1,0:T(8,128)(2,1)} collective-permute-done((bf16[4,96,1536]{2,1,0:T(8,128)(2,1)}, bf16[4,96,1536]{2,1,0:T(8,128)(2,1)}, u32[]{:S(2)}, u32[]{:S(2)}) %collective-permute-start.17) | collective-permute-done | bytes 1179680 | tf_op jit(solution)/shard_map/ppermute | solution.py:450
  436.6 8.0 %shard_map.277 = (bf16[1664,768]{1,0:T(8,128)(2,1)}, bf16[1664,768]{1,0:T(8,128)(2,1)}, f32[8,768]{1,0:T(8,128)}) custom-call(bf16[1664,768]{1,0:T(8,128)(2,1)} %get-tuple-element.115.dz_ref.refs_3_, bf16[768,3840]{1,0:T(8,128)(2,1)} %bitcast.201, bf16[768,3840]{1,0:T(8,128)(2,1)} %bitcast.202), custom_call_target="tpu_custom_call" | custom-call | flops 8000000000 | tf_op jit(solution)/shard_map/pallas_call | solution.py:340
  444.6 3.3 fusion.1
  447.8 11.1 %shard_map.278 = bf16[2,384,1536]{2,1,0:T(8,128)(2,1)} custom-call(bf16[1664,768]{1,0:T(8,128)(2,1)} %get-tuple-element.118.refs_0_, bf16[1664,768]{1,0:T(8,128)(2,1)} %get-tuple-element.119.refs_1_, bf16[1664,768]{1,0:T(8,128)(2,1)} %get-tuple-element.120.refs_2_, bf16[1664,768]{1,0:T(8,128)(2,1)} %get-tuple-element.115.dz_ref.refs_3_), custom_call_target="tpu_custom_call" | custom-call | flops 6000000000 | tf_op jit(solution)/shard_map/pallas_call | solution.py:438
  458.9 2.4 dynamic-slice_bitcast_fusion.3
  461.3 3.6 fusion.6
  464.9 3.9 all-to-all-start.2
  472.5 3.5 fusion.12
  476.0 6.1 maximum_bitcast_fusion
  482.1 3.0 collective-permute-done.19
  485.2 12.3 %collective-permute-done.21 = bf16[4,24,3072]{2,1,0:T(8,128)(2,1)S(1)} collective-permute-done((bf16[4,24,3072]{2,1,0:T(8,128)(2,1)S(1)}, bf16[4,24,3072]{2,1,0:T(8,128)(2,1)S(1)}, u32[]{:S(2)}, u32[]{:S(2)}) %collective-permute-start.21) | collective-permute-done | bytes 589856 | tf_op jit(solution)/shard_map/ppermute | solution.py:450
  500.1 2.1 collective-permute-start.23
  502.2 2.4 collective-permute-start.25
  504.5 40.5 %shard_map.279 = (bf16[1664,2304]{1,0:T(8,128)(2,1)}, f32[8,768]{1,0:T(8,128)}) custom-call(bf16[1664,768]{1,0:T(8,128)(2,1)} %get-tuple-element.132.do_ref, bf16[1664,2304]{1,0:T(8,128)(2,1)} %get-tuple-element.133.qkv_ref, f32[1664,128]{1,0:T(8,128)} %get-tuple-element.134.p_ref, bf16[6144,128]{1,0:T(8,128)(2,1)} %and_convert_fusion.1.e_ref, ...), custom_call_target="tpu_custom_call" | custom-call | flops 40000000000 | tf_op jit(solution)/shard_map/pallas_call | solution.py:390
  553.4 11.3 %shard_map.280 = bf16[2,384,2304]{2,1,0:T(8,128)(2,1)} custom-call(bf16[1664,768]{1,0:T(8,128)(2,1)} %get-tuple-element.136.refs_0_, bf16[1664,2304]{1,0:T(8,128)(2,1)} %get-tuple-element.145.refs_1_.dqkv_ref), custom_call_target="tpu_custom_call" | custom-call | flops 8999999488 | tf_op jit(solution)/shard_map/pallas_call | solution.py:438
  566.3 2.8 dynamic-slice_bitcast_fusion.2
  569.1 13.1 %shard_map.281 = (bf16[1664,768]{1,0:T(8,128)(2,1)}, f32[8,768]{1,0:T(8,128)}) custom-call(bf16[1664,2304]{1,0:T(8,128)(2,1)} %get-tuple-element.145.refs_1_.dqkv_ref, bf16[1664,768]{1,0:T(8,128)(2,1)} %bitcast.217, f32[1664,768]{1,0:T(8,128)} %get-tuple-element.146.g1_ref, f32[1,768]{1,0:T(1,128)} %get-tuple-element.239.gain_ref, bf16[768,3840]{1,0:T(8,128)(2,1)} %bitcast.203), custom_call_target="tpu_custom_call" | custom-call | flops 12000000000 | tf_op jit(solution)/shard_map/pallas_call | solution.py:404
  586.4 2.1 collective-permute-start.33
  597.6 3.3 copy.65
  600.9 3.9 all-to-all-start.3
  606.4 8.3 %collective-permute-done.36 = bf16[4,24,2304]{2,1,0:T(8,128)(2,1)} collective-permute-done((bf16[4,24,2304]{2,1,0:T(8,128)(2,1)}, bf16[4,24,2304]{2,1,0:T(8,128)(2,1)}, u32[]{:S(2)}, u32[]{:S(2)}) %collective-permute-start.36) | collective-permute-done | bytes 442400 | tf_op jit(solution)/shard_map/ppermute | solution.py:450
  617.8 3.0 collective-permute-start.39
  624.1 2.4 collective-permute-start.41
  626.5 24.8 %collective-permute-done.39 = f32[28,768]{1,0:T(8,128)S(1)} collective-permute-done((f32[28,768]{1,0:T(8,128)S(1)}, f32[28,768]{1,0:T(8,128)S(1)}, u32[]{:S(2)}, u32[]{:S(2)}) %collective-permute-start.39) | collective-permute-done | bytes 86048 | tf_op jit(solution)/shard_map/ppermute | solution.py:450
  651.3 24.3 %collective-permute-done.38 = f32[28,768]{1,0:T(8,128)S(1)} collective-permute-done((f32[28,768]{1,0:T(8,128)S(1)}, f32[28,768]{1,0:T(8,128)S(1)}, u32[]{:S(2)}, u32[]{:S(2)}) %collective-permute-start.38) | collective-permute-done | bytes 86048 | tf_op jit(solution)/shard_map/ppermute | solution.py:450
  (213 shorter events, 105.1 us)
Async XLA Ops:
  11.8 17.2 %collective-permute-start.2 = (bf16[24,6912]{1,0:T(8,128)(2,1)S(1)}, bf16[24,6912]{1,0:T(8,128)(2,1)S(1)}, u32[]{:S(2)}, u32[]{:S(2)}) collective-permute-start(bf16[24,6912]{1,0:T(8,128)(2,1)S(1)} %convert_dynamic-update-slice_fusion), channel_id=1, source_target_pairs={{0,2},{2,0},{4,6},{6,4},{1,3},{3,1},{5,7},{7,5},{8,10},{10,8},{12,... | collective-permute-start | bytes 995336 | tf_op jit(solution)/shard_map/ppermute | solution.py:450
  14.8 25.8 %collective-permute-start.1 = (bf16[24,6912]{1,0:T(8,128)(2,1)S(1)}, bf16[24,6912]{1,0:T(8,128)(2,1)S(1)}, u32[]{:S(2)}, u32[]{:S(2)}) collective-permute-start(bf16[24,6912]{1,0:T(8,128)(2,1)S(1)} %convert_dynamic-update-slice_fusion), channel_id=1, source_target_pairs={{0,4},{2,6},{4,0},{6,2},{1,5},{3,7},{5,1},{7,3},{8,12},{10,14},{12... | collective-permute-start | bytes 995336 | tf_op jit(solution)/shard_map/ppermute | solution.py:450
  17.4 23.3 %collective-permute-start = (bf16[24,6912]{1,0:T(8,128)(2,1)S(1)}, bf16[24,6912]{1,0:T(8,128)(2,1)S(1)}, u32[]{:S(2)}, u32[]{:S(2)}) collective-permute-start(bf16[24,6912]{1,0:T(8,128)(2,1)S(1)} %convert_dynamic-update-slice_fusion), channel_id=1, source_target_pairs={{0,6},{2,4},{4,2},{6,0},{1,7},{3,5},{5,3},{7,1},{8,14},{10,12},{12... | collective-permute-start | bytes 995336 | tf_op jit(solution)/shard_map/ppermute | solution.py:450
  42.0 73.8 %all-to-all-start = ((bf16[4,196,2,768]{3,2,1,0:T(2,128)(2,1)}), bf16[4,196,2,768]{3,2,1,0:T(2,128)(2,1)S(1)}, u32[]{:S(2)}, u32[]{:S(2)}) async-start(bf16[4,196,2,768]{3,2,1,0:T(2,128)(2,1)} %bitcast.219), calls=%async_computation | async-start | bytes 4816896 | tf_op jit(solution)/shard_map/all_to_all | solution.py:568
  50.7 192.1 %all-gather.2.cloned.1.call-start = ((), (), s32[]{:S(2)}) async-start(), calls=%async_computation.4 | async-start | bytes 9732096 | tf_op jit(solution)/shard_map/all_gather | solution.py:615
  52.8 20.1 %collective-permute-start.5 = (bf16[4,24,3840]{2,1,0:T(8,128)(2,1)}, bf16[4,24,3840]{2,1,0:T(8,128)(2,1)S(1)}, u32[]{:S(2)}, u32[]{:S(2)}) collective-permute-start(bf16[4,24,3840]{2,1,0:T(8,128)(2,1)} %slice.158), channel_id=1, source_target_pairs={{0,8},{8,0},{16,24},{24,16},{1,9},{9,1},{17,25},{25,17},{2,10},{10... | collective-permute-start | bytes 2211848 | tf_op jit(solution)/shard_map/ppermute | solution.py:450
  54.3 61.6 %collective-permute-start.4 = (bf16[4,24,3840]{2,1,0:T(8,128)(2,1)}, bf16[4,24,3840]{2,1,0:T(8,128)(2,1)}, u32[]{:S(2)}, u32[]{:S(2)}) collective-permute-start(bf16[4,24,3840]{2,1,0:T(8,128)(2,1)} %slice.158), channel_id=1, source_target_pairs={{0,16},{8,24},{16,0},{24,8},{1,17},{9,25},{17,1},{25,9},{2,18},{10... | collective-permute-start | bytes 2211848 | tf_op jit(solution)/shard_map/ppermute | solution.py:450
  55.8 60.0 %collective-permute-start.3 = (bf16[4,24,3840]{2,1,0:T(8,128)(2,1)}, bf16[4,24,3840]{2,1,0:T(8,128)(2,1)}, u32[]{:S(2)}, u32[]{:S(2)}) collective-permute-start(bf16[4,24,3840]{2,1,0:T(8,128)(2,1)} %slice.158), channel_id=1, source_target_pairs={{0,24},{8,16},{16,8},{24,0},{1,25},{9,17},{17,9},{25,1},{2,26},{10... | collective-permute-start | bytes 2211848 | tf_op jit(solution)/shard_map/ppermute | solution.py:450
  120.2 19.5 %collective-permute-start.6 = (bf16[4,4,24,3840]{3,2,1,0:T(8,128)(2,1)}, bf16[4,4,24,3840]{3,2,1,0:T(8,128)(2,1)}, u32[]{:S(2)}, u32[]{:S(2)}) collective-permute-start(bf16[4,4,24,3840]{3,2,1,0:T(8,128)(2,1)} %pad_maximum_fusion.2), channel_id=1, source_target_pairs={{0,1},{1,0},{2,3},{3,2},{4,5},{5,4},{6,7},{7,6},{8,9},{9,8},{10,11... | collective-permute-start | bytes 8847368 | tf_op jit(solution)/shard_map/ppermute | solution.py:450
  129.5 59.7 %collective-permute-start.9 = (bf16[4,24,3072]{2,1,0:T(8,128)(2,1)}, bf16[4,24,3072]{2,1,0:T(8,128)(2,1)}, u32[]{:S(2)}, u32[]{:S(2)}) collective-permute-start(bf16[4,24,3072]{2,1,0:T(8,128)(2,1)} %slice.159), channel_id=1, source_target_pairs={{0,8},{8,0},{16,24},{24,16},{1,9},{9,1},{17,25},{25,17},{2,10},{10... | collective-permute-start | bytes 1769480 | tf_op jit(solution)/shard_map/ppermute | solution.py:450
  131.1 58.1 %collective-permute-start.8 = (bf16[4,24,3072]{2,1,0:T(8,128)(2,1)}, bf16[4,24,3072]{2,1,0:T(8,128)(2,1)}, u32[]{:S(2)}, u32[]{:S(2)}) collective-permute-start(bf16[4,24,3072]{2,1,0:T(8,128)(2,1)} %slice.159), channel_id=1, source_target_pairs={{0,16},{8,24},{16,0},{24,8},{1,17},{9,25},{17,1},{25,9},{2,18},{10... | collective-permute-start | bytes 1769480 | tf_op jit(solution)/shard_map/ppermute | solution.py:450
  132.8 56.4 %collective-permute-start.7 = (bf16[4,24,3072]{2,1,0:T(8,128)(2,1)}, bf16[4,24,3072]{2,1,0:T(8,128)(2,1)}, u32[]{:S(2)}, u32[]{:S(2)}) collective-permute-start(bf16[4,24,3072]{2,1,0:T(8,128)(2,1)} %slice.159), channel_id=1, source_target_pairs={{0,24},{8,16},{16,8},{24,0},{1,25},{9,17},{17,9},{25,1},{2,26},{10... | collective-permute-start | bytes 1769480 | tf_op jit(solution)/shard_map/ppermute | solution.py:450
  133.0 75.8 %all-to-all-start.1 = ((bf16[4,196,2,768]{3,2,1,0:T(2,128)(2,1)}), bf16[4,196,2,768]{3,2,1,0:T(2,128)(2,1)}, u32[]{:S(2)}, u32[]{:S(2)}) async-start(bf16[4,196,2,768]{3,2,1,0:T(2,128)(2,1)} %bitcast.220), calls=%async_computation.1 | async-start | bytes 4816896 | tf_op jit(solution)/shard_map/all_to_all | solution.py:568
  192.8 19.8 %collective-permute-start.10 = (bf16[4,4,24,3072]{3,2,1,0:T(8,128)(2,1)}, bf16[4,4,24,3072]{3,2,1,0:T(8,128)(2,1)}, u32[]{:S(2)}, u32[]{:S(2)}) collective-permute-start(bf16[4,4,24,3072]{3,2,1,0:T(8,128)(2,1)} %pad_maximum_fusion.3), channel_id=1, source_target_pairs={{0,1},{1,0},{2,3},{3,2},{4,5},{5,4},{6,7},{7,6},{8,9},{9,8},{10,11... | collective-permute-start | bytes 7077896 | tf_op jit(solution)/shard_map/ppermute | solution.py:450
  322.3 26.9 %collective-permute-start.12 = (bf16[16,96,1536]{2,1,0:T(8,128)(2,1)}, bf16[16,96,1536]{2,1,0:T(8,128)(2,1)}, u32[]{:S(2)}, u32[]{:S(2)}) collective-permute-start(bf16[16,96,1536]{2,1,0:T(8,128)(2,1)} %dynamic-slice_bitcast_fusion), channel_id=1, source_target_pairs={{0,1},{1,0},{2,3},{3,2},{4,5},{5,4},{6,7},{7,6},{8,9},{9,8},{10,11... | collective-permute-start | bytes 14155784 | tf_op jit(solution)/shard_map/ppermute | solution.py:450
  323.6 30.9 %collective-permute-start.13 = (bf16[196,2,768]{2,1,0:T(2,128)(2,1)S(1)}, bf16[196,2,768]{2,1,0:T(2,128)(2,1)S(1)}, u32[]{:S(2)}, u32[]{:S(2)}) collective-permute-start(bf16[196,2,768]{2,1,0:T(2,128)(2,1)S(1)} %bitcast.229), channel_id=1, source_target_pairs={{0,2},{2,0},{4,6},{6,4},{1,3},{3,1},{5,7},{7,5},{8,10},{10,8},{12,... | collective-permute-start | bytes 1806344 | tf_op jit(solution)/shard_map/ppermute | solution.py:450
  323.7 60.9 %collective-permute-start.16 = (bf16[196,2,768]{2,1,0:T(2,128)(2,1)S(1)}, bf16[196,2,768]{2,1,0:T(2,128)(2,1)}, u32[]{:S(2)}, u32[]{:S(2)}) collective-permute-start(bf16[196,2,768]{2,1,0:T(2,128)(2,1)S(1)} %bitcast.228), channel_id=1, source_target_pairs={{0,4},{2,6},{4,0},{6,2},{1,5},{3,7},{5,1},{7,3},{8,12},{10,14},{12... | collective-permute-start | bytes 1806344 | tf_op jit(solution)/shard_map/ppermute | solution.py:450
  357.9 28.0 %collective-permute-start.15 = (bf16[4,96,1536]{2,1,0:T(8,128)(2,1)}, bf16[4,96,1536]{2,1,0:T(8,128)(2,1)S(1)}, u32[]{:S(2)}, u32[]{:S(2)}) collective-permute-start(bf16[4,96,1536]{2,1,0:T(8,128)(2,1)} %get-tuple-element.177), channel_id=1, source_target_pairs={{0,16},{8,24},{16,0},{24,8},{1,17},{9,25},{17,1},{25,9},{2,18},{10... | collective-permute-start | bytes 3538952 | tf_op jit(solution)/shard_map/ppermute | solution.py:450
  359.6 27.8 %collective-permute-start.14 = (bf16[4,96,1536]{2,1,0:T(8,128)(2,1)}, bf16[4,96,1536]{2,1,0:T(8,128)(2,1)}, u32[]{:S(2)}, u32[]{:S(2)}) collective-permute-start(bf16[4,96,1536]{2,1,0:T(8,128)(2,1)} %get-tuple-element.178), channel_id=1, source_target_pairs={{0,8},{8,0},{16,24},{24,16},{1,9},{9,1},{17,25},{25,17},{2,10},{10... | collective-permute-start | bytes 3538952 | tf_op jit(solution)/shard_map/ppermute | solution.py:450
  407.0 37.6 %collective-permute-start.18 = (bf16[16,24,3072]{2,1,0:T(8,128)(2,1)}, bf16[16,24,3072]{2,1,0:T(8,128)(2,1)}, u32[]{:S(2)}, u32[]{:S(2)}) collective-permute-start(bf16[16,24,3072]{2,1,0:T(8,128)(2,1)} %dynamic-slice_bitcast_fusion.1), channel_id=1, source_target_pairs={{0,1},{1,0},{2,3},{3,2},{4,5},{5,4},{6,7},{7,6},{8,9},{9,8},{10,11... | collective-permute-start | bytes 7077896 | tf_op jit(solution)/shard_map/ppermute | solution.py:450
  407.0 29.6 %collective-permute-start.17 = (bf16[4,96,1536]{2,1,0:T(8,128)(2,1)}, bf16[4,96,1536]{2,1,0:T(8,128)(2,1)}, u32[]{:S(2)}, u32[]{:S(2)}) collective-permute-start(bf16[4,96,1536]{2,1,0:T(8,128)(2,1)} %get-tuple-element.176), channel_id=1, source_target_pairs={{0,24},{8,16},{16,8},{24,0},{1,25},{9,17},{17,9},{25,1},{2,26},{10... | collective-permute-start | bytes 3538952 | tf_op jit(solution)/shard_map/ppermute | solution.py:450
  412.9 34.9 %collective-permute-start.11 = (bf16[196,2,768]{2,1,0:T(2,128)(2,1)}, bf16[196,2,768]{2,1,0:T(2,128)(2,1)}, u32[]{:S(2)}, u32[]{:S(2)}) collective-permute-start(bf16[196,2,768]{2,1,0:T(2,128)(2,1)} %bitcast.184), channel_id=1, source_target_pairs={{0,6},{2,4},{4,2},{6,0},{1,7},{3,5},{5,3},{7,1},{8,14},{10,12},{12... | collective-permute-start | bytes 1806344 | tf_op jit(solution)/shard_map/ppermute | solution.py:450
  464.9 87.4 %all-to-all-start.2 = ((bf16[4,96,1536]{2,1,0:T(8,128)(2,1)}), bf16[4,96,1536]{2,1,0:T(8,128)(2,1)S(1)}, u32[]{:S(2)}, u32[]{:S(2)}) async-start(bf16[4,96,1536]{2,1,0:T(8,128)(2,1)} %fusion.6), calls=%async_computation.2 | async-start | bytes 2359296 | tf_op jit(solution)/shard_map/all_to_all | solution.py:520
  468.8 78.0 %collective-permute-start.22 = (bf16[16,24,1536]{2,1,0:T(8,128)(2,1)}, bf16[16,24,1536]{2,1,0:T(8,128)(2,1)}, u32[]{:S(2)}, u32[]{:S(2)}) collective-permute-start(bf16[16,24,1536]{2,1,0:T(8,128)(2,1)} %dynamic-slice_bitcast_fusion.3), channel_id=1, source_target_pairs={{0,1},{1,0},{2,3},{3,2},{4,5},{5,4},{6,7},{7,6},{8,9},{9,8},{10,11... | collective-permute-start | bytes 3538952 | tf_op jit(solution)/shard_map/ppermute | solution.py:450
  469.0 16.2 %collective-permute-start.19 = (bf16[4,24,3072]{2,1,0:T(8,128)(2,1)S(1)}, bf16[4,24,3072]{2,1,0:T(8,128)(2,1)S(1)}, u32[]{:S(2)}, u32[]{:S(2)}) collective-permute-start(bf16[4,24,3072]{2,1,0:T(8,128)(2,1)S(1)} %get-tuple-element.193), channel_id=1, source_target_pairs={{0,8},{8,0},{16,24},{24,16},{1,9},{9,1},{17,25},{25,17},{2,10},{10... | collective-permute-start | bytes 1769480 | tf_op jit(solution)/shard_map/ppermute | solution.py:450
  470.5 27.0 %collective-permute-start.21 = (bf16[4,24,3072]{2,1,0:T(8,128)(2,1)S(1)}, bf16[4,24,3072]{2,1,0:T(8,128)(2,1)S(1)}, u32[]{:S(2)}, u32[]{:S(2)}) collective-permute-start(bf16[4,24,3072]{2,1,0:T(8,128)(2,1)S(1)} %get-tuple-element.194), channel_id=1, source_target_pairs={{0,24},{8,16},{16,8},{24,0},{1,25},{9,17},{17,9},{25,1},{2,26},{10... | collective-permute-start | bytes 1769480 | tf_op jit(solution)/shard_map/ppermute | solution.py:450
  471.1 27.8 %collective-permute-start.20 = (bf16[4,24,3072]{2,1,0:T(8,128)(2,1)S(1)}, bf16[4,24,3072]{2,1,0:T(8,128)(2,1)S(1)}, u32[]{:S(2)}, u32[]{:S(2)}) collective-permute-start(bf16[4,24,3072]{2,1,0:T(8,128)(2,1)S(1)} %get-tuple-element.195), channel_id=1, source_target_pairs={{0,16},{8,24},{16,0},{24,8},{1,17},{9,25},{17,1},{25,9},{2,18},{10... | collective-permute-start | bytes 1769480 | tf_op jit(solution)/shard_map/ppermute | solution.py:450
  500.1 45.0 %collective-permute-start.23 = (bf16[24,3072]{1,0:T(8,128)(2,1)S(1)}, bf16[24,3072]{1,0:T(8,128)(2,1)S(1)}, u32[]{:S(2)}, u32[]{:S(2)}) collective-permute-start(bf16[24,3072]{1,0:T(8,128)(2,1)S(1)} %get-tuple-element.215), channel_id=1, source_target_pairs={{0,2},{2,0},{4,6},{6,4},{1,3},{3,1},{5,7},{7,5},{8,10},{10,8},{12,... | collective-permute-start | bytes 442376 | tf_op jit(solution)/shard_map/ppermute | solution.py:450
  502.2 42.9 %collective-permute-start.25 = (bf16[24,3072]{1,0:T(8,128)(2,1)S(1)}, bf16[24,3072]{1,0:T(8,128)(2,1)S(1)}, u32[]{:S(2)}, u32[]{:S(2)}) collective-permute-start(bf16[24,3072]{1,0:T(8,128)(2,1)S(1)} %get-tuple-element.216), channel_id=1, source_target_pairs={{0,6},{2,4},{4,2},{6,0},{1,7},{3,5},{5,3},{7,1},{8,14},{10,12},{12... | collective-permute-start | bytes 442376 | tf_op jit(solution)/shard_map/ppermute | solution.py:450
  504.5 40.6 %collective-permute-start.24 = (bf16[24,3072]{1,0:T(8,128)(2,1)S(1)}, bf16[24,3072]{1,0:T(8,128)(2,1)S(1)}, u32[]{:S(2)}, u32[]{:S(2)}) collective-permute-start(bf16[24,3072]{1,0:T(8,128)(2,1)S(1)} %get-tuple-element.217), channel_id=1, source_target_pairs={{0,4},{2,6},{4,0},{6,2},{1,5},{3,7},{5,1},{7,3},{8,12},{10,14},{12... | collective-permute-start | bytes 442376 | tf_op jit(solution)/shard_map/ppermute | solution.py:450
  548.8 16.3 %collective-permute-start.26 = (bf16[4,24,1536]{2,1,0:T(8,128)(2,1)S(1)}, bf16[4,24,1536]{2,1,0:T(8,128)(2,1)S(1)}, u32[]{:S(2)}, u32[]{:S(2)}) collective-permute-start(bf16[4,24,1536]{2,1,0:T(8,128)(2,1)S(1)} %get-tuple-element.207), channel_id=1, source_target_pairs={{0,8},{8,0},{16,24},{24,16},{1,9},{9,1},{17,25},{25,17},{2,10},{10... | collective-permute-start | bytes 884744 | tf_op jit(solution)/shard_map/ppermute | solution.py:450
  550.3 14.3 %collective-permute-start.28 = (bf16[4,24,1536]{2,1,0:T(8,128)(2,1)S(1)}, bf16[4,24,1536]{2,1,0:T(8,128)(2,1)}, u32[]{:S(2)}, u32[]{:S(2)}) collective-permute-start(bf16[4,24,1536]{2,1,0:T(8,128)(2,1)S(1)} %get-tuple-element.208), channel_id=1, source_target_pairs={{0,24},{8,16},{16,8},{24,0},{1,25},{9,17},{17,9},{25,1},{2,26},{10... | collective-permute-start | bytes 884744 | tf_op jit(solution)/shard_map/ppermute | solution.py:450
  551.8 13.3 %collective-permute-start.27 = (bf16[4,24,1536]{2,1,0:T(8,128)(2,1)S(1)}, bf16[4,24,1536]{2,1,0:T(8,128)(2,1)}, u32[]{:S(2)}, u32[]{:S(2)}) collective-permute-start(bf16[4,24,1536]{2,1,0:T(8,128)(2,1)S(1)} %get-tuple-element.209), channel_id=1, source_target_pairs={{0,16},{8,24},{16,0},{24,8},{1,17},{9,25},{17,1},{25,9},{2,18},{10... | collective-permute-start | bytes 884744 | tf_op jit(solution)/shard_map/ppermute | solution.py:450
  569.1 20.9 %collective-permute-start.29 = (bf16[16,24,2304]{2,1,0:T(8,128)(2,1)}, bf16[16,24,2304]{2,1,0:T(8,128)(2,1)}, u32[]{:S(2)}, u32[]{:S(2)}) collective-permute-start(bf16[16,24,2304]{2,1,0:T(8,128)(2,1)} %dynamic-slice_bitcast_fusion.2), channel_id=1, source_target_pairs={{0,1},{1,0},{2,3},{3,2},{4,5},{5,4},{6,7},{7,6},{8,9},{9,8},{10,11... | collective-permute-start | bytes 5308424 | tf_op jit(solution)/shard_map/ppermute | solution.py:450
  583.7 1.9 collective-permute-start.30
  586.4 9.2 %collective-permute-start.33 = (f32[28,768]{1,0:T(8,128)S(1)}, f32[28,768]{1,0:T(8,128)S(1)}, u32[]{:S(2)}, u32[]{:S(2)}) collective-permute-start(f32[28,768]{1,0:T(8,128)S(1)} %fusion.42), channel_id=1, source_target_pairs={{0,24},{8,16},{16,8},{24,0},{1,25},{9,17},{17,9},{25,1},{2,26},{10... | collective-permute-start | bytes 258056 | tf_op jit(solution)/shard_map/ppermute | solution.py:450
  588.5 16.3 %collective-permute-start.32 = (f32[28,768]{1,0:T(8,128)S(1)}, f32[28,768]{1,0:T(8,128)S(1)}, u32[]{:S(2)}, u32[]{:S(2)}) collective-permute-start(f32[28,768]{1,0:T(8,128)S(1)} %fusion.42), channel_id=1, source_target_pairs={{0,16},{8,24},{16,0},{24,8},{1,17},{9,25},{17,1},{25,9},{2,18},{10... | collective-permute-start | bytes 258056 | tf_op jit(solution)/shard_map/ppermute | solution.py:450
  589.4 15.3 %collective-permute-start.31 = (f32[28,768]{1,0:T(8,128)S(1)}, f32[28,768]{1,0:T(8,128)}, u32[]{:S(2)}, u32[]{:S(2)}) collective-permute-start(f32[28,768]{1,0:T(8,128)S(1)} %fusion.42), channel_id=1, source_target_pairs={{0,8},{8,0},{16,24},{24,16},{1,9},{9,1},{17,25},{25,17},{2,10},{10... | collective-permute-start | bytes 258056 | tf_op jit(solution)/shard_map/ppermute | solution.py:450
  593.1 13.3 %collective-permute-start.34 = (bf16[4,24,2304]{2,1,0:T(8,128)(2,1)}, bf16[4,24,2304]{2,1,0:T(8,128)(2,1)S(1)}, u32[]{:S(2)}, u32[]{:S(2)}) collective-permute-start(bf16[4,24,2304]{2,1,0:T(8,128)(2,1)} %get-tuple-element.200), channel_id=1, source_target_pairs={{0,8},{8,0},{16,24},{24,16},{1,9},{9,1},{17,25},{25,17},{2,10},{10... | collective-permute-start | bytes 1327112 | tf_op jit(solution)/shard_map/ppermute | solution.py:450
  594.6 20.2 %collective-permute-start.36 = (bf16[4,24,2304]{2,1,0:T(8,128)(2,1)}, bf16[4,24,2304]{2,1,0:T(8,128)(2,1)}, u32[]{:S(2)}, u32[]{:S(2)}) collective-permute-start(bf16[4,24,2304]{2,1,0:T(8,128)(2,1)} %get-tuple-element.201), channel_id=1, source_target_pairs={{0,24},{8,16},{16,8},{24,0},{1,25},{9,17},{17,9},{25,1},{2,26},{10... | collective-permute-start | bytes 1327112 | tf_op jit(solution)/shard_map/ppermute | solution.py:450
  595.6 20.5 %collective-permute-start.35 = (bf16[4,24,2304]{2,1,0:T(8,128)(2,1)}, bf16[4,24,2304]{2,1,0:T(8,128)(2,1)}, u32[]{:S(2)}, u32[]{:S(2)}) collective-permute-start(bf16[4,24,2304]{2,1,0:T(8,128)(2,1)} %get-tuple-element.202), channel_id=1, source_target_pairs={{0,16},{8,24},{16,0},{24,8},{1,17},{9,25},{17,1},{25,9},{2,18},{10... | collective-permute-start | bytes 1327112 | tf_op jit(solution)/shard_map/ppermute | solution.py:450
  600.9 81.2 %all-to-all-start.3 = ((bf16[4,196,2,768]{3,2,1,0:T(2,128)(2,1)}), bf16[4,196,2,768]{3,2,1,0:T(2,128)(2,1)S(1)}, u32[]{:S(2)}, u32[]{:S(2)}) async-start(bf16[4,196,2,768]{3,2,1,0:T(2,128)(2,1)} %bitcast.193), calls=%async_computation.3 | async-start | bytes 4816896 | tf_op jit(solution)/shard_map/all_to_all | solution.py:584
  617.8 33.5 %collective-permute-start.39 = (f32[28,768]{1,0:T(8,128)S(1)}, f32[28,768]{1,0:T(8,128)S(1)}, u32[]{:S(2)}, u32[]{:S(2)}) collective-permute-start(f32[28,768]{1,0:T(8,128)S(1)} %add_add_fusion.1), channel_id=1, source_target_pairs={{0,6},{2,4},{4,2},{6,0},{1,7},{3,5},{5,3},{7,1},{8,14},{10,12},{12... | collective-permute-start | bytes 258056 | tf_op jit(solution)/shard_map/ppermute | solution.py:450
  620.7 54.8 %collective-permute-start.38 = (f32[28,768]{1,0:T(8,128)S(1)}, f32[28,768]{1,0:T(8,128)S(1)}, u32[]{:S(2)}, u32[]{:S(2)}) collective-permute-start(f32[28,768]{1,0:T(8,128)S(1)} %add_add_fusion.1), channel_id=1, source_target_pairs={{0,4},{2,6},{4,0},{6,2},{1,5},{3,7},{5,1},{7,3},{8,12},{10,14},{12... | collective-permute-start | bytes 258056 | tf_op jit(solution)/shard_map/ppermute | solution.py:450
  621.3 54.2 %collective-permute-start.37 = (f32[28,768]{1,0:T(8,128)S(1)}, f32[28,768]{1,0:T(8,128)S(1)}, u32[]{:S(2)}, u32[]{:S(2)}) collective-permute-start(f32[28,768]{1,0:T(8,128)S(1)} %add_add_fusion.1), channel_id=1, source_target_pairs={{0,2},{2,0},{4,6},{6,4},{1,3},{3,1},{5,7},{7,5},{8,10},{10,8},{12,... | collective-permute-start | bytes 258056 | tf_op jit(solution)/shard_map/ppermute | solution.py:450
  623.0 56.3 %collective-permute-start.40 = (bf16[24,3840]{1,0:T(8,128)(2,1)}, bf16[24,3840]{1,0:T(8,128)(2,1)S(1)}, u32[]{:S(2)}, u32[]{:S(2)}) collective-permute-start(bf16[24,3840]{1,0:T(8,128)(2,1)} %get-tuple-element.210), channel_id=1, source_target_pairs={{0,2},{2,0},{4,6},{6,4},{1,3},{3,1},{5,7},{7,5},{8,10},{10,8},{12,... | collective-permute-start | bytes 552968 | tf_op jit(solution)/shard_map/ppermute | solution.py:450
  624.1 55.5 %collective-permute-start.41 = (bf16[24,3840]{1,0:T(8,128)(2,1)}, bf16[24,3840]{1,0:T(8,128)(2,1)}, u32[]{:S(2)}, u32[]{:S(2)}) collective-permute-start(bf16[24,3840]{1,0:T(8,128)(2,1)} %get-tuple-element.211), channel_id=1, source_target_pairs={{0,4},{2,6},{4,0},{6,2},{1,5},{3,7},{5,1},{7,3},{8,12},{10,14},{12... | collective-permute-start | bytes 552968 | tf_op jit(solution)/shard_map/ppermute | solution.py:450
  651.3 28.3 %collective-permute-start.42 = (bf16[24,3840]{1,0:T(8,128)(2,1)}, bf16[24,3840]{1,0:T(8,128)(2,1)}, u32[]{:S(2)}, u32[]{:S(2)}) collective-permute-start(bf16[24,3840]{1,0:T(8,128)(2,1)} %get-tuple-element.212), channel_id=1, source_target_pairs={{0,6},{2,4},{4,2},{6,0},{1,7},{3,5},{5,3},{7,1},{8,14},{10,12},{12... | collective-permute-start | bytes 552968 | tf_op jit(solution)/shard_map/ppermute | solution.py:450
  (29 other events, 216.9 us)
Sparse Core Ops, SparseCore 0:
  59.4 142.7 all-gather.1
where the time goes:
time: 696 us; the launch traced here: 691 us
  Pallas kernels  290 us (42%)
  waiting for transfers between devices  195 us (28%)
  starting transfers between devices  69.8 us (10%)
  other arithmetic  67.3 us (10%)
  local copies, waits for them, and re-layouts  53.1 us (8%)
  between operations  15.5 us (2%)
    ppermute x43, waiting for transfers between devices, exchange(): lax.ppermute(pieces[d], axis, [(i, i ^ d) for i in range(size)])  137 us
    pallas_call x1, Pallas kernels, mlp(): pl.pallas_call(partial(mlp_kernel, rb=rb, chunks=chunks), grid=(chunks,),...  74.4 us
    all_to_all x2, waiting for transfers between devices, to_clips(): lax.all_to_all(array, 'context', split_axis=0, concat_axis=0, tiled=True)  57.8 us
    ppermute x43, starting transfers between devices, exchange(): lax.ppermute(pieces[d], axis, [(i, i ^ d) for i in range(size)])  48.6 us
    pallas_call x2, Pallas kernels, spatial_backward(): pl.pallas_call(partial(sb_kernel, fb=fb, real=real, head=head, scale=scal...  47.2 us
    pallas_call x1, Pallas kernels, temporal_forward(): call(partial(tf_kernel, fb=fb, nb=nb, frames=frames, slot=LANES // frames...  43.1 us
    pallas_call x1, Pallas kernels, temporal_backward(): call(partial(tb_kernel, fb=fb, nb=nb, frames=frames, slot=LANES // frames...  40.5 us
    pallas_call x3, Pallas kernels, weight_grads(): call(partial(wg_kernel, starts=starts, halves=halves, rows=rows if fits e...  38.7 us
  transfers between devices with their start and end apart: 48, of which 18 were waited for; matrix products, arithmetic and copies ran while one was open for 13% of the time, Pallas kernels for 27%

commit v1 on v0

--- a/solution.py
+++ b/solution.py
@@ -261,11 +261,14 @@
         shift *= 2
     return rows
 
-def tf_kernel(x_ref, gain_ref, shift_ref, wqkv_ref, wproj_ref, wfc_ref, hb_ref, wb_ref, fcb_ref, e_ref, b_ref,
-              a_ref, qkv_ref, p_ref, o_ref, y_ref, x1_ref, all_ref, prod_ref, xs_ref, *, fb, nb, frames, slot, scale):
+def tf_kernel(x_ref, gain_ref, shift_ref, wqkv_ref, wproj_ref, wfc_ref, hb_ref, wb_ref, fcb_ref,
+              a_ref, qkv_ref, p_ref, o_ref, y_ref, x1_ref, all_ref, prod_ref, xs_ref, e_ref, b_ref, *, fb, nb, frames, slot, head, scale):
     M, D = x_ref.shape
     P = M // fb
     step = pl.program_id(0)
+    @pl.when(step == 0)
+    def _():
+        fill_tables(e_ref, b_ref, slot, head)
     @pl.when(step < nb)
     def _():
         x = x_ref[...].astype(F32)
@@ -301,25 +304,32 @@
         z = (mm(y, wfc_ref[...], 1, 0) + fcb_ref[...]).astype(BF)
         x1_ref[...] = xs_ref[pl.ds(base, M), :].astype(F32) + z.astype(F32)
 
-def temporal_tables(D, head, frames):
-    slot = LANES // frames
-    lane = jnp.arange(LANES)
-    feat = jnp.arange(frames * D)
-    e = ((feat[:, None] // D == lane[None, :] // slot) & ((feat[:, None] % D) // head == lane[None, :] % slot)).astype(BF)
-    return e, e.T
-
-def temporal_forward(x, gain, shift, w, hb, wb, fcb, e, b, *, frames, scale, fb=2):
+def fill_tables(e_ref, b_ref, slot, head):
+    D = e_ref.shape[0] * slot // LANES
+    for g in range(LANES // slot):
+        for ref, at, wide in ((e_ref, 1, 0), (b_ref, 0, 1)):
+            shape = (D, LANES) if wide == 0 else (LANES, D)
+            lane = lax.broadcasted_iota(jnp.int32, shape, at)
+            feature = lax.broadcasted_iota(jnp.int32, shape, wide)
+            hit = ((lane // slot == g) & (lane % slot == feature // head)).astype(F32).astype(BF)
+            if wide == 0:
+                ref[g * D:(g + 1) * D, :] = hit
+            else:
+                ref[:, g * D:(g + 1) * D] = hit
+
+def temporal_forward(x, gain, shift, w, hb, wb, fcb, *, frames, head, scale, fb=2):
     T, D = x.shape
     M = T // frames * fb
     nb = frames // fb
     first = lambda w: pl.BlockSpec((M, w), lambda j: (jnp.minimum(j, nb - 1), 0))
     last = lambda w: pl.BlockSpec((M, w), lambda j: (jnp.maximum(j - nb, 0), 0))
-    return call(partial(tf_kernel, fb=fb, nb=nb, frames=frames, slot=LANES // frames, scale=scale), 44, 2 * nb,
-        [first(D), once(1, D), once(1, D), column(D, 3 * D, 0), column(D, D, 3), column(D, D, 4), once(2, D), once(1, D), once(1, D), once(*e.shape), once(*b.shape)],
+    return call(partial(tf_kernel, fb=fb, nb=nb, frames=frames, slot=LANES // frames, head=head, scale=scale), 44, 2 * nb,
+        [first(D), once(1, D), once(1, D), column(D, 3 * D, 0), column(D, D, 3), column(D, D, 4), once(2, D), once(1, D), once(1, D)],
         [first(D), first(3 * D), last(LANES), last(D), last(D), last(D)],
         (sds(T, D), sds(T, 3 * D), sds(T, LANES, t=F32), sds(T, D), sds(T, D), sds(T, D, t=F32)),
-        [pltpu.VMEM((T, 3 * D), BF), pltpu.VMEM((M, frames * D), BF), pltpu.VMEM((T, D), BF)])(
-        x, gain, shift, w, w, w, hb, wb, fcb, e, b)
+        [pltpu.VMEM((T, 3 * D), BF), pltpu.VMEM((M, frames * D), BF), pltpu.VMEM((T, D), BF),
+         pltpu.VMEM((frames * D, LANES), BF), pltpu.VMEM((LANES, frames * D), BF)])(
+        x, gain, shift, w, w, w, hb, wb, fcb)
 
 def zero_first(*refs):
     @pl.when(pl.program_id(0) == 0)
@@ -340,12 +350,15 @@
     return call(pull_kernel, 8, blocks, [blk, column(D, D, 3), column(D, D, 4)], [blk, blk, once(8, D)],
                 (sds(T, D), sds(T, D), sds(8, D, t=F32)))(dz, w, w)
 
-def tb_kernel(do_ref, qkv_ref, p_ref, e_ref, b_ref, dqkv_ref, sums_ref, dk_ref, dv_ref, prod_ref, *, fb, nb, frames, slot, scale):
+def tb_kernel(do_ref, qkv_ref, p_ref, dqkv_ref, sums_ref, dk_ref, dv_ref, prod_ref, e_ref, b_ref, *, fb, nb, frames, slot, head, scale):
     M = p_ref.shape[0]
     T, D = do_ref.shape
     P = M // fb
     step = pl.program_id(0)
     zero_first(sums_ref, dk_ref, dv_ref)
+    @pl.when(step == 0)
+    def _():
+        fill_tables(e_ref, b_ref, slot, head)
     base = pl.multiple_of(step * M, M)
     for f in range(fb):
         do = do_ref[pl.ds(base + f * P, P), :]
@@ -383,14 +396,15 @@
             add_sum(sums_ref, 3, low)
             dqkv_ref[gr, 2 * D:] = low
 
-def temporal_backward(do, qkv, p, e, b, *, frames, scale, fb=2):
+def temporal_backward(do, qkv, p, *, frames, head, scale, fb=2):
     T, D = do.shape
     M = T // frames * fb
     nb = frames // fb
-    return call(partial(tb_kernel, fb=fb, nb=nb, frames=frames, slot=LANES // frames, scale=scale), 40, nb,
-        [once(T, D), once(T, 3 * D), pl.BlockSpec((M, LANES), lambda j: (j, 0)), once(*e.shape), once(*b.shape)],
+    return call(partial(tb_kernel, fb=fb, nb=nb, frames=frames, slot=LANES // frames, head=head, scale=scale), 40, nb,
+        [once(T, D), once(T, 3 * D), pl.BlockSpec((M, LANES), lambda j: (j, 0))],
         [once(T, 3 * D), once(8, D)], (sds(T, 3 * D), sds(8, D, t=F32)),
-        [pltpu.VMEM((T, D), F32), pltpu.VMEM((T, D), F32), pltpu.VMEM((M, frames * D), BF)])(do, qkv, p, e, b)
+        [pltpu.VMEM((T, D), F32), pltpu.VMEM((T, D), F32), pltpu.VMEM((M, frames * D), BF),
+         pltpu.VMEM((frames * D, LANES), BF), pltpu.VMEM((LANES, frames * D), BF)])(do, qkv, p)
 
 def end_kernel(dqkv_ref, x_ref, g1_ref, gain_ref, wqkv_ref, out_ref, sums_ref):
     zero_first(sums_ref)
@@ -516,8 +530,9 @@
     return added(split_off(array, axis), *hold)
 
 
-def shed_at_once(array, axis):
+def shed_at_once(array, axis, *hold):
     came = lax.all_to_all(array.astype(BF), axis, split_axis=0, concat_axis=0, tiled=True)
+    came = after(came, *hold)
     return jnp.sum(came.astype(F32), axis=0)
 
 
@@ -579,7 +594,6 @@
         return jnp.swapaxes(array, 1, 2)
 
     def from_clips(array):
-        array = by_place(array)
         if spread:
             array = lax.all_to_all(array, "context", split_axis=0, concat_axis=0, tiled=True)
         else:
@@ -619,21 +633,19 @@
     t_chips = collect(t_first, "shard", hold=(rows_in,))
     t_all = collect(t_chips, "tensor", 2).reshape(-1, t_own.shape[1])
     pulled = to_clips(after(cotangent, rows_in))
-    ones, spread_ones = temporal_tables(width, head, frames)
 
     def one_clip(x, pull, keep_one):
-        sizes = dict(frames=frames, scale=scale)
+        sizes = dict(frames=frames, head=head, scale=scale)
         gain = [norm_gains[i : i + 1] for i in range(3)]
         shift = [norm_shifts[i : i + 1] for i in range(3)]
         wide = [width_bias[i : i + 1] for i in range(3)]
         x = fill(x)
         a_t, qkv_t, probs, o_t, y, x1 = temporal_forward(
-            x, gain[0], shift[0], t_all, head_bias[0], wide[0], fc_bias[None], ones, spread_ones,
-            **sizes,
+            x, gain[0], shift[0], t_all, head_bias[0], wide[0], fc_bias[None], **sizes,
         )
         s_all = collect(after(s_first, rows_in), "shard", hold=(x1,))
         s_all = collect(s_all, "tensor", 2).reshape(-1, s_own.shape[1])
-        sizes_s = dict(sizes, real=places, head=head)
+        sizes_s = dict(sizes, real=places)
         a_s, qkv_s, o_s, x2 = spatial_forward(
             x1, gain[1], shift[1], s_all, head_bias[1], wide[1], **sizes_s
         )
@@ -652,41 +664,44 @@
         sums_s = sums_s + half[3]
         tied = after(d_qkv_s, *d_m[1:3], *back[2:3])
         d_s = share * grads_of([(a_s, tied), (db, o_s)], us=12)
-        tied = after(dz, d_s, *d_m[3:])
+        tied = after(dz, d_s)
         d_s = split_off(d_s, "tensor")
         dy, do, sums_y = temporal_pull(tied, t_all)
         d_s = added(d_s, dy).astype(BF)
-        tied = after(dy, d_s, *back[3:])
+        tied = after(dy, d_s, *back[3:], *d_m[3:])
         d_s = split_off(by_shard(d_s), "shard")
         d_r = share * grads_of([(tied, o_t), (y, dz)], us=6)
-        output = sent_back([after(piece, d_r) for piece in back])
-        d_s = added(d_s, d_r).astype(BF)
         d_m = added(d_m, d_r).astype(BF)
-        tied = after(do, d_m, d_s, output)
-        d_m = shed_at_once(d_m, "context")
-        d_s = split_off(d_s, "context")
+        tied = after(do, d_m, d_r)
+        d_m = lax.all_to_all(d_m, "context", split_axis=0, concat_axis=0, tiled=True)
         d_r = split_off(d_r, "tensor")
-        d_qkv_t, sums_q = temporal_backward(tied, qkv_t, probs, ones, spread_ones, **sizes)
-        d_s = added(d_s, d_qkv_t)
+        d_qkv_t, sums_q = temporal_backward(tied, qkv_t, probs, **sizes)
+        d_m = jnp.sum(after(d_m, d_qkv_t).astype(F32), axis=0)
+        d_s = added(d_s, d_qkv_t).astype(BF)
         d_r = added(d_r, d_qkv_t).astype(BF)
         tied = after(d_qkv_t, d_r, d_s, d_m)
         d_r = split_off(by_shard(d_r), "shard")
         d_q = share * grads_of([(a_t, tied)], us=9)
-        d_r = added(d_r, d_q)
-        tied, d_q = lax.optimization_barrier((d_qkv_t, d_q, d_r))[:2]
+        d_r = added(d_r, d_q).astype(BF)
+        d_s = shed_at_once(d_s, "context", d_q)
+        tied, d_q, d_r, d_s = lax.optimization_barrier((d_qkv_t, d_q, d_r, d_s))
         d_q = split_off(d_q, "tensor")
+        d_r = split_off(d_r, "context")
         into, sums_x = temporal_end(tied, x, g1, gain[0], t_all)
-        d_q = added(d_q, into).astype(BF)
-        into = from_clips(after(into, d_q))
+        d_r = added(d_r, into)
+        swapped = after(by_place(into), d_r)
+        into = from_clips(swapped)
+        output = sent_back([after(piece, swapped) for piece in back])
         small = share * jnp.concatenate(
             (sums_m, sums_s, sums_y + sums_q + sums_x, d_hidden.reshape(-1, width)), axis=0
         )
-        d_q = added(split_off(by_shard(d_q), "shard"))
-        small = plus_others(plus_others(small, "tensor"), "shard")
-        d_r = jnp.concatenate((d_r.astype(BF), d_q.astype(BF)), axis=-1)
-        d_r = shed(d_r, "context")
-        small = plus_others(after(small, d_q), "context")
-        return output, into, (d_r, d_s, d_m, small)
+        d_q = added(d_q, swapped).astype(BF)
+        small = plus_others(small, "tensor")
+        d_q = added(split_off(by_shard(after(d_q, small)), "shard")).astype(BF)
+        small = plus_others(after(small, d_q), "shard")
+        d_q = shed(after(d_q, small), "context")
+        small = plus_others(small, "context")
+        return output, into, (d_q, d_r, d_s, d_m, small)
 
     parts = [one_clip(rows_in[:, i], pulled[:, i], keep[i]) for i in range(clips)]
     output, input_grad = [
@@ -695,8 +710,7 @@
     grads = parts[0][2]
     for part in parts[1:]:
         grads = jax.tree.map(jnp.add, grads, part[2])
-    d_t, d_s, d_mlp, small = grads
-    d_t_rest, d_t_qkv = d_t[:, : 2 * width], d_t[:, 2 * width :]
+    d_t_qkv, d_t_rest, d_s, d_mlp, small = grads
     m, s, t = small[0:8], small[8:16], small[16:24]
     return (
         output,

time: 696 us -> 655 us (0.941)
  waiting for transfers between devices: 195 us -> 146 us
  starting transfers between devices: 69.8 us -> 92.8 us
  other arithmetic: 67.3 us -> 55.7 us
    ppermute x43, waiting for transfers between devices: 137 us -> 80.4 us  [exchange(): lax.ppermute(pieces[d], axis, [(i, i ^ d) for i in range(size)])]
    ppermute x43, starting transfers between devices: 48.6 us -> 66.8 us  [exchange(): lax.ppermute(pieces[d], axis, [(i, i ^ d) for i in range(size)])]
    squeeze x9 -> x10, local copies, waits for them, and re-layouts: 16.8 us -> 16.4 us  [split_off(): lax.dynamic_index_in_dim(array, place ^ d, 0, keepdims=False)]
  transfers between devices with their start and end apart: 48 -> 49, of which waited for: 18 -> 19; matrix products, arithmetic and copies ran while one was open for 13% -> 13% of each run, Pallas kernels for 27% -> 29%
where the time goes in v1:
time: 655 us; the launch traced here: 651 us
  Pallas kernels  289 us (44%)
  waiting for transfers between devices  146 us (22%)
  starting transfers between devices  92.8 us (14%)
  other arithmetic  55.7 us (9%)
  local copies, waits for them, and re-layouts  53 us (8%)
  between operations  15.6 us (2%)
    ppermute x43, waiting for transfers between devices, exchange(): lax.ppermute(pieces[d], axis, [(i, i ^ d) for i in range(size)])  80.4 us
    pallas_call x1, Pallas kernels, mlp(): pl.pallas_call(partial(mlp_kernel, rb=rb, chunks=chunks), grid=(chunks,),...  74.4 us
    ppermute x43, starting transfers between devices, exchange(): lax.ppermute(pieces[d], axis, [(i, i ^ d) for i in range(size)])  66.8 us
    all_to_all x2, waiting for transfers between devices, to_clips(): lax.all_to_all(array, 'context', split_axis=0, concat_axis=0, tiled=True)  62.6 us
    pallas_call x2, Pallas kernels, spatial_backward(): pl.pallas_call(partial(sb_kernel, fb=fb, real=real, head=head, scale=scal...  47.2 us
    pallas_call x1, Pallas kernels, temporal_forward(): call(partial(tf_kernel, fb=fb, nb=nb, frames=frames, slot=LANES // frames...  42.4 us
    pallas_call x1, Pallas kernels, temporal_backward(): call(partial(tb_kernel, fb=fb, nb=nb, frames=frames, slot=LANES // frames...  39.8 us
    pallas_call x3, Pallas kernels, weight_grads(): call(partial(wg_kernel, starts=starts, halves=halves, rows=rows if fits e...  38.7 us
  transfers between devices with their start and end apart: 49, of which 19 were waited for; matrix products, arithmetic and copies ran while one was open for 13% of the time, Pallas kernels for 29%

profile of v1, /device:TPU:0, one launch (start us, length us, event | category | flops | bytes accessed | tf_op | source)
XLA Modules:
  0.0 651.4 jit_solution(1607508363961428949)
XLA Ops:
  11.8 3.0 collective-permute-start.2
  14.8 2.6 collective-permute-start.1
  17.4 11.5 %collective-permute-done.2 = bf16[24,6912]{1,0:T(8,128)(2,1)S(1)} collective-permute-done((bf16[24,6912]{1,0:T(8,128)(2,1)S(1)}, bf16[24,6912]{1,0:T(8,128)(2,1)S(1)}, u32[]{:S(2)}, u32[]{:S(2)}) %collective-permute-start.2) | collective-permute-done | bytes 331808 | tf_op jit(solution)/shard_map/ppermute | solution.py:464
  29.0 11.7 %collective-permute-done.1 = bf16[24,6912]{1,0:T(8,128)(2,1)S(1)} collective-permute-done((bf16[24,6912]{1,0:T(8,128)(2,1)S(1)}, bf16[24,6912]{1,0:T(8,128)(2,1)S(1)}, u32[]{:S(2)}, u32[]{:S(2)}) %collective-permute-start.1) | collective-permute-done | bytes 331808 | tf_op jit(solution)/shard_map/ppermute | solution.py:464
  42.0 8.7 %all-to-all-start = ((bf16[4,196,2,768]{3,2,1,0:T(2,128)(2,1)}), bf16[4,196,2,768]{3,2,1,0:T(2,128)(2,1)S(1)}, u32[]{:S(2)}, u32[]{:S(2)}) async-start(bf16[4,196,2,768]{3,2,1,0:T(2,128)(2,1)} %bitcast.216), calls=%async_computation | async-start | bytes 4816896 | tf_op jit(solution)/shard_map/all_to_all | solution.py:583
  58.0 15.8 %collective-permute-done.5 = bf16[4,24,3840]{2,1,0:T(8,128)(2,1)S(1)} collective-permute-done((bf16[4,24,3840]{2,1,0:T(8,128)(2,1)}, bf16[4,24,3840]{2,1,0:T(8,128)(2,1)S(1)}, u32[]{:S(2)}, u32[]{:S(2)}) %collective-permute-start.5) | collective-permute-done | bytes 737312 | tf_op jit(solution)/shard_map/ppermute | solution.py:464
  73.8 42.1 %all-to-all-done = bf16[4,196,2,768]{3,2,1,0:T(2,128)(2,1)S(1)} async-done(((bf16[4,196,2,768]{3,2,1,0:T(2,128)(2,1)}), bf16[4,196,2,768]{3,2,1,0:T(2,128)(2,1)S(1)}, u32[]{:S(2)}, u32[]{:S(2)}) %all-to-all-start) | async-done | bytes 2408480 | tf_op jit(solution)/shard_map/all_to_all | solution.py:583
  115.9 2.0 select_bitcast_fusion.7
  128.1 4.7 all-to-all-start.1
  135.6 2.1 select_bitcast_fusion.1
  138.3 2.9 copy.41
  141.2 42.4 %shard_map.271 = (bf16[1664,768]{1,0:T(8,128)(2,1)}, bf16[1664,2304]{1,0:T(8,128)(2,1)}, f32[1664,128]{1,0:T(8,128)}, bf16[1664,768]{1,0:T(8,128)(2,1)}, bf16[1664,768]{1,0:T(8,128)(2,1)}, /*index=5*/f32[1664,768]{1,0:T(8,128)}) custom-call(bf16[1664,768]{1,0:T(8,128)(2,1)} %bitcast.213, f32[1,768]{1,0:T(1,128)} %get-tuple-element.251.gain_ref, ...), custom_call_target="tpu_custom_call" | custom-call | flops 44000002048 | tf_op jit(solution)/shard_map/pallas_call | solution.py:326
  188.4 20.4 %all-to-all-done.1 = bf16[4,196,2,768]{3,2,1,0:T(2,128)(2,1)} async-done(((bf16[4,196,2,768]{3,2,1,0:T(2,128)(2,1)}), bf16[4,196,2,768]{3,2,1,0:T(2,128)(2,1)}, u32[]{:S(2)}, u32[]{:S(2)}) %all-to-all-start.1) | async-done | bytes 2408480 | tf_op jit(solution)/shard_map/all_to_all | solution.py:583
  214.9 2.6 copy.42
  217.5 25.4 %shard_map.272 = (bf16[1664,768]{1,0:T(8,128)(2,1)}, bf16[1664,2304]{1,0:T(8,128)(2,1)}, bf16[1664,768]{1,0:T(8,128)(2,1)}, f32[1664,768]{1,0:T(8,128)}) custom-call(f32[1664,768]{1,0:T(8,128)} %get-tuple-element.97.x_ref, f32[1,768]{1,0:T(1,128)} %get-tuple-element.252.gain_ref, f32[1,768]{1,0:T(1,128)} %get-tuple-element.255.shift_ref, ...), custom_call_target="tpu_custom_call" | custom-call | flops 30000001024 | tf_op jit(solution)/shard_map/pallas_call | solution.py:183
  242.8 74.4 %shard_map.273 = (bf16[1664,768]{1,0:T(8,128)(2,1)}, f32[1664,768]{1,0:T(8,128)}, bf16[1664,768]{1,0:T(8,128)(2,1)}, bf16[2,16,96,1536]{3,2,1,0:T(8,128)(2,1)}, f32[1,3072]{1,0:T(1,128)}, /*index=5*/f32[8,768]{1,0:T(8,128)}) custom-call(f32[1664,768]{1,0:T(8,128)} %get-tuple-element.102.x_ref, bf16[1664,768]{1,0:T(8,128)(2,1)} %bitcast.215, ...), custom_call_target="tpu_custom_call" | custom-call | flops 74999996416 | tf_op jit(solution)/shard_map/pallas_call | solution.py:113
  317.2 5.0 dynamic-slice_bitcast_fusion
  325.3 23.7 %shard_map.274 = (bf16[1664,2304]{1,0:T(8,128)(2,1)}, f32[1664,768]{1,0:T(8,128)}, bf16[1664,768]{1,0:T(8,128)(2,1)}, f32[8,768]{1,0:T(8,128)}) custom-call(f32[1664,768]{1,0:T(8,128)} %get-tuple-element.107.g2_ref, bf16[1664,768]{1,0:T(8,128)(2,1)} %get-tuple-element.113.db_ref.refs_1_, bf16[1664,2304]{1,0:T(8,128)(2,1)} %get-tuple-element.110.qkv_ref, ...), custom_call_target="tpu_custom_call" | custom-call | flops 24000000000 | tf_op jit(solution)/shard_map/pallas_call | solution.py:246
  349.1 5.3 fusion
  361.0 23.5 %shard_map.275 = (bf16[1664,2304]{1,0:T(8,128)(2,1)}, f32[1664,768]{1,0:T(8,128)}, bf16[1664,768]{1,0:T(8,128)(2,1)}, f32[8,768]{1,0:T(8,128)}) custom-call(f32[1664,768]{1,0:T(8,128)} %get-tuple-element.107.g2_ref, bf16[1664,768]{1,0:T(8,128)(2,1)} %get-tuple-element.113.db_ref.refs_1_, ...), custom_call_target="tpu_custom_call", output_to_operand_aliasing={{0}: (7, {}), {1}: (8, {}), {2}: (9, {})} | custom-call | flops 24000000000 | tf_op jit(solution)/shard_map/pallas_call | solution.py:246
  387.4 16.3 %shard_map.276 = bf16[2,384,3072]{2,1,0:T(8,128)(2,1)} custom-call(bf16[1664,768]{1,0:T(8,128)(2,1)} %get-tuple-element.117.refs_0_, bf16[1664,768]{1,0:T(8,128)(2,1)} %get-tuple-element.113.db_ref.refs_1_, bf16[1664,2304]{1,0:T(8,128)(2,1)} %get-tuple-element.119.refs_2_, bf16[1664,768]{1,0:T(8,128)(2,1)} %get-tuple-element.120.refs_3_), custom_call_target="tpu_custom_call" | custom-call | flops 12000000000 | tf_op jit(solution)/shard_map/pallas_call | solution.py:452
  403.7 3.2 dynamic-slice_bitcast_fusion.1
  410.7 2.4 collective-permute-start.11
  415.2 8.0 %shard_map.277 = (bf16[1664,768]{1,0:T(8,128)(2,1)}, bf16[1664,768]{1,0:T(8,128)(2,1)}, f32[8,768]{1,0:T(8,128)}) custom-call(bf16[1664,768]{1,0:T(8,128)(2,1)} %get-tuple-element.121.dz_ref.refs_3_, bf16[768,3840]{1,0:T(8,128)(2,1)} %bitcast.198, bf16[768,3840]{1,0:T(8,128)(2,1)} %bitcast.199), custom_call_target="tpu_custom_call" | custom-call | flops 8000000000 | tf_op jit(solution)/shard_map/pallas_call | solution.py:350
  423.2 3.3 fusion.1
  426.5 2.5 collective-permute-done.11
  429.0 13.5 %collective-permute-done.18 = bf16[4,96,1536]{2,1,0:T(8,128)(2,1)} collective-permute-done((bf16[4,96,1536]{2,1,0:T(8,128)(2,1)}, bf16[4,96,1536]{2,1,0:T(8,128)(2,1)}, u32[]{:S(2)}, u32[]{:S(2)}) %collective-permute-start.18) | collective-permute-done | bytes 1179680 | tf_op jit(solution)/shard_map/ppermute | solution.py:464
  442.5 11.1 %shard_map.278 = bf16[2,384,1536]{2,1,0:T(8,128)(2,1)} custom-call(bf16[1664,768]{1,0:T(8,128)(2,1)} %get-tuple-element.125.refs_0_, bf16[1664,768]{1,0:T(8,128)(2,1)} %get-tuple-element.126.refs_1_, bf16[1664,768]{1,0:T(8,128)(2,1)} %get-tuple-element.127.refs_2_, bf16[1664,768]{1,0:T(8,128)(2,1)} %get-tuple-element.121.dz_ref.refs_3_), custom_call_target="tpu_custom_call" | custom-call | flops 6000000000 | tf_op jit(solution)/shard_map/pallas_call | solution.py:452
  453.5 2.4 dynamic-slice_bitcast_fusion.3
  455.9 3.6 fusion.6
  459.5 3.7 all-to-all-start.2
  468.1 39.8 %shard_map.279 = (bf16[1664,2304]{1,0:T(8,128)(2,1)}, f32[8,768]{1,0:T(8,128)}) custom-call(bf16[1664,768]{1,0:T(8,128)(2,1)} %get-tuple-element.131.do_ref, bf16[1664,2304]{1,0:T(8,128)(2,1)} %get-tuple-element.132.qkv_ref, f32[1664,128]{1,0:T(8,128)} %get-tuple-element.133.p_ref), custom_call_target="tpu_custom_call" | custom-call | flops 40000000000 | tf_op jit(solution)/shard_map/pallas_call | solution.py:403
  507.9 2.8 fusion.9
  516.7 5.2 all-to-all-start.3
  522.1 11.3 %shard_map.280 = bf16[2,384,2304]{2,1,0:T(8,128)(2,1)} custom-call(bf16[1664,768]{1,0:T(8,128)(2,1)} %get-tuple-element.135.refs_0_, bf16[1664,2304]{1,0:T(8,128)(2,1)} %get-tuple-element.146.refs_1_.dqkv_ref), custom_call_target="tpu_custom_call" | custom-call | flops 8999999488 | tf_op jit(solution)/shard_map/pallas_call | solution.py:452
  534.2 2.5 all-to-all-done.3
  544.6 13.0 %shard_map.281 = (bf16[1664,768]{1,0:T(8,128)(2,1)}, f32[8,768]{1,0:T(8,128)}) custom-call(bf16[1664,2304]{1,0:T(8,128)(2,1)} %get-tuple-element.146.refs_1_.dqkv_ref, bf16[1664,768]{1,0:T(8,128)(2,1)} %bitcast.214, f32[1664,768]{1,0:T(8,128)} %get-tuple-element.147.g1_ref, f32[1,768]{1,0:T(1,128)} %get-tuple-element.251.gain_ref, bf16[768,3840]{1,0:T(8,128)(2,1)} %bitcast.200), custom_call_target="tpu_custom_call" | custom-call | flops 12000000000 | tf_op jit(solution)/shard_map/pallas_call | solution.py:418
  560.8 3.3 copy.65
  564.1 3.8 all-to-all-start.4
  568.0 3.8 fusion.13
  577.4 6.1 maximum_bitcast_fusion
  583.5 3.5 collective-permute-done.31
  586.9 8.6 %collective-permute-done.33 = bf16[4,24,2304]{2,1,0:T(8,128)(2,1)S(1)} collective-permute-done((bf16[4,24,2304]{2,1,0:T(8,128)(2,1)S(1)}, bf16[4,24,2304]{2,1,0:T(8,128)(2,1)S(1)}, u32[]{:S(2)}, u32[]{:S(2)}) %collective-permute-start.33) | collective-permute-done | bytes 442400 | tf_op jit(solution)/shard_map/ppermute | solution.py:464
  597.1 2.4 collective-permute-start.36
  604.8 3.6 collective-permute-start.39
  610.5 2.4 collective-permute-start.42
  614.4 19.0 %collective-permute-start.41 = (bf16[24,2304]{1,0:T(8,128)(2,1)S(1)}, bf16[24,2304]{1,0:T(8,128)(2,1)}, u32[]{:S(2)}, u32[]{:S(2)}) collective-permute-start(bf16[24,2304]{1,0:T(8,128)(2,1)S(1)} %get-tuple-element.226), channel_id=1, source_target_pairs={{0,4},{2,6},{4,0},{6,2},{1,5},{3,7},{5,1},{7,3},{8,12},{10,14},{12... | collective-permute-start | bytes 331784 | tf_op jit(solution)/shard_map/ppermute | solution.py:464
  633.4 2.7 collective-permute-done.38
  (209 shorter events, 102.3 us)
Async XLA Ops:
  11.8 17.2 %collective-permute-start.2 = (bf16[24,6912]{1,0:T(8,128)(2,1)S(1)}, bf16[24,6912]{1,0:T(8,128)(2,1)S(1)}, u32[]{:S(2)}, u32[]{:S(2)}) collective-permute-start(bf16[24,6912]{1,0:T(8,128)(2,1)S(1)} %convert_dynamic-update-slice_fusion), channel_id=1, source_target_pairs={{0,2},{2,0},{4,6},{6,4},{1,3},{3,1},{5,7},{7,5},{8,10},{10,8},{12,... | collective-permute-start | bytes 995336 | tf_op jit(solution)/shard_map/ppermute | solution.py:464
  14.8 25.8 %collective-permute-start.1 = (bf16[24,6912]{1,0:T(8,128)(2,1)S(1)}, bf16[24,6912]{1,0:T(8,128)(2,1)S(1)}, u32[]{:S(2)}, u32[]{:S(2)}) collective-permute-start(bf16[24,6912]{1,0:T(8,128)(2,1)S(1)} %convert_dynamic-update-slice_fusion), channel_id=1, source_target_pairs={{0,4},{2,6},{4,0},{6,2},{1,5},{3,7},{5,1},{7,3},{8,12},{10,14},{12... | collective-permute-start | bytes 995336 | tf_op jit(solution)/shard_map/ppermute | solution.py:464
  17.4 23.3 %collective-permute-start = (bf16[24,6912]{1,0:T(8,128)(2,1)S(1)}, bf16[24,6912]{1,0:T(8,128)(2,1)S(1)}, u32[]{:S(2)}, u32[]{:S(2)}) collective-permute-start(bf16[24,6912]{1,0:T(8,128)(2,1)S(1)} %convert_dynamic-update-slice_fusion), channel_id=1, source_target_pairs={{0,6},{2,4},{4,2},{6,0},{1,7},{3,5},{5,3},{7,1},{8,14},{10,12},{12... | collective-permute-start | bytes 995336 | tf_op jit(solution)/shard_map/ppermute | solution.py:464
  42.0 73.9 %all-to-all-start = ((bf16[4,196,2,768]{3,2,1,0:T(2,128)(2,1)}), bf16[4,196,2,768]{3,2,1,0:T(2,128)(2,1)S(1)}, u32[]{:S(2)}, u32[]{:S(2)}) async-start(bf16[4,196,2,768]{3,2,1,0:T(2,128)(2,1)} %bitcast.216), calls=%async_computation | async-start | bytes 4816896 | tf_op jit(solution)/shard_map/all_to_all | solution.py:583
  50.7 192.1 %all-gather.2.cloned.1.call-start = ((), (), s32[]{:S(2)}) async-start(), calls=%async_computation.5 | async-start | bytes 9732096 | tf_op jit(solution)/shard_map/all_gather | solution.py:629
  52.7 21.1 %collective-permute-start.5 = (bf16[4,24,3840]{2,1,0:T(8,128)(2,1)}, bf16[4,24,3840]{2,1,0:T(8,128)(2,1)S(1)}, u32[]{:S(2)}, u32[]{:S(2)}) collective-permute-start(bf16[4,24,3840]{2,1,0:T(8,128)(2,1)} %slice.151), channel_id=1, source_target_pairs={{0,8},{8,0},{16,24},{24,16},{1,9},{9,1},{17,25},{25,17},{2,10},{10... | collective-permute-start | bytes 2211848 | tf_op jit(solution)/shard_map/ppermute | solution.py:464
  54.2 61.7 %collective-permute-start.4 = (bf16[4,24,3840]{2,1,0:T(8,128)(2,1)}, bf16[4,24,3840]{2,1,0:T(8,128)(2,1)}, u32[]{:S(2)}, u32[]{:S(2)}) collective-permute-start(bf16[4,24,3840]{2,1,0:T(8,128)(2,1)} %slice.151), channel_id=1, source_target_pairs={{0,16},{8,24},{16,0},{24,8},{1,17},{9,25},{17,1},{25,9},{2,18},{10... | collective-permute-start | bytes 2211848 | tf_op jit(solution)/shard_map/ppermute | solution.py:464
  55.7 60.2 %collective-permute-start.3 = (bf16[4,24,3840]{2,1,0:T(8,128)(2,1)}, bf16[4,24,3840]{2,1,0:T(8,128)(2,1)}, u32[]{:S(2)}, u32[]{:S(2)}) collective-permute-start(bf16[4,24,3840]{2,1,0:T(8,128)(2,1)} %slice.151), channel_id=1, source_target_pairs={{0,24},{8,16},{16,8},{24,0},{1,25},{9,17},{17,9},{25,1},{2,26},{10... | collective-permute-start | bytes 2211848 | tf_op jit(solution)/shard_map/ppermute | solution.py:464
  120.3 14.5 %collective-permute-start.6 = (bf16[4,4,24,3840]{3,2,1,0:T(8,128)(2,1)}, bf16[4,4,24,3840]{3,2,1,0:T(8,128)(2,1)}, u32[]{:S(2)}, u32[]{:S(2)}) collective-permute-start(bf16[4,4,24,3840]{3,2,1,0:T(8,128)(2,1)} %pad_maximum_fusion.2), channel_id=1, source_target_pairs={{0,1},{1,0},{2,3},{3,2},{4,5},{5,4},{6,7},{7,6},{8,9},{9,8},{10,11... | collective-permute-start | bytes 8847368 | tf_op jit(solution)/shard_map/ppermute | solution.py:464
  124.6 59.0 %collective-permute-start.9 = (bf16[4,24,3072]{2,1,0:T(8,128)(2,1)}, bf16[4,24,3072]{2,1,0:T(8,128)(2,1)}, u32[]{:S(2)}, u32[]{:S(2)}) collective-permute-start(bf16[4,24,3072]{2,1,0:T(8,128)(2,1)} %slice.152), channel_id=1, source_target_pairs={{0,8},{8,0},{16,24},{24,16},{1,9},{9,1},{17,25},{25,17},{2,10},{10... | collective-permute-start | bytes 1769480 | tf_op jit(solution)/shard_map/ppermute | solution.py:464
  126.1 57.5 %collective-permute-start.8 = (bf16[4,24,3072]{2,1,0:T(8,128)(2,1)}, bf16[4,24,3072]{2,1,0:T(8,128)(2,1)}, u32[]{:S(2)}, u32[]{:S(2)}) collective-permute-start(bf16[4,24,3072]{2,1,0:T(8,128)(2,1)} %slice.152), channel_id=1, source_target_pairs={{0,16},{8,24},{16,0},{24,8},{1,17},{9,25},{17,1},{25,9},{2,18},{10... | collective-permute-start | bytes 1769480 | tf_op jit(solution)/shard_map/ppermute | solution.py:464
  127.8 55.8 %collective-permute-start.7 = (bf16[4,24,3072]{2,1,0:T(8,128)(2,1)}, bf16[4,24,3072]{2,1,0:T(8,128)(2,1)}, u32[]{:S(2)}, u32[]{:S(2)}) collective-permute-start(bf16[4,24,3072]{2,1,0:T(8,128)(2,1)} %slice.152), channel_id=1, source_target_pairs={{0,24},{8,16},{16,8},{24,0},{1,25},{9,17},{17,9},{25,1},{2,26},{10... | collective-permute-start | bytes 1769480 | tf_op jit(solution)/shard_map/ppermute | solution.py:464
  128.1 80.8 %all-to-all-start.1 = ((bf16[4,196,2,768]{3,2,1,0:T(2,128)(2,1)}), bf16[4,196,2,768]{3,2,1,0:T(2,128)(2,1)}, u32[]{:S(2)}, u32[]{:S(2)}) async-start(bf16[4,196,2,768]{3,2,1,0:T(2,128)(2,1)} %bitcast.217), calls=%async_computation.1 | async-start | bytes 4816896 | tf_op jit(solution)/shard_map/all_to_all | solution.py:583
  187.2 25.4 %collective-permute-start.10 = (bf16[4,4,24,3072]{3,2,1,0:T(8,128)(2,1)}, bf16[4,4,24,3072]{3,2,1,0:T(8,128)(2,1)}, u32[]{:S(2)}, u32[]{:S(2)}) collective-permute-start(bf16[4,4,24,3072]{3,2,1,0:T(8,128)(2,1)} %pad_maximum_fusion.3), channel_id=1, source_target_pairs={{0,1},{1,0},{2,3},{3,2},{4,5},{5,4},{6,7},{7,6},{8,9},{9,8},{10,11... | collective-permute-start | bytes 7077896 | tf_op jit(solution)/shard_map/ppermute | solution.py:464
  322.3 26.8 %collective-permute-start.12 = (bf16[16,96,1536]{2,1,0:T(8,128)(2,1)}, bf16[16,96,1536]{2,1,0:T(8,128)(2,1)}, u32[]{:S(2)}, u32[]{:S(2)}) collective-permute-start(bf16[16,96,1536]{2,1,0:T(8,128)(2,1)} %dynamic-slice_bitcast_fusion), channel_id=1, source_target_pairs={{0,1},{1,0},{2,3},{3,2},{4,5},{5,4},{6,7},{7,6},{8,9},{9,8},{10,11... | collective-permute-start | bytes 14155784 | tf_op jit(solution)/shard_map/ppermute | solution.py:464
  323.6 30.8 %collective-permute-start.13 = (bf16[196,2,768]{2,1,0:T(2,128)(2,1)S(1)}, bf16[196,2,768]{2,1,0:T(2,128)(2,1)S(1)}, u32[]{:S(2)}, u32[]{:S(2)}) collective-permute-start(bf16[196,2,768]{2,1,0:T(2,128)(2,1)S(1)} %bitcast.226), channel_id=1, source_target_pairs={{0,2},{2,0},{4,6},{6,4},{1,3},{3,1},{5,7},{7,5},{8,10},{10,8},{12,... | collective-permute-start | bytes 1806344 | tf_op jit(solution)/shard_map/ppermute | solution.py:464
  323.6 60.9 %collective-permute-start.16 = (bf16[196,2,768]{2,1,0:T(2,128)(2,1)S(1)}, bf16[196,2,768]{2,1,0:T(2,128)(2,1)}, u32[]{:S(2)}, u32[]{:S(2)}) collective-permute-start(bf16[196,2,768]{2,1,0:T(2,128)(2,1)S(1)} %bitcast.225), channel_id=1, source_target_pairs={{0,4},{2,6},{4,0},{6,2},{1,5},{3,7},{5,1},{7,3},{8,12},{10,14},{12... | collective-permute-start | bytes 1806344 | tf_op jit(solution)/shard_map/ppermute | solution.py:464
  357.8 28.1 %collective-permute-start.15 = (bf16[4,96,1536]{2,1,0:T(8,128)(2,1)}, bf16[4,96,1536]{2,1,0:T(8,128)(2,1)S(1)}, u32[]{:S(2)}, u32[]{:S(2)}) collective-permute-start(bf16[4,96,1536]{2,1,0:T(8,128)(2,1)} %get-tuple-element.189), channel_id=1, source_target_pairs={{0,16},{8,24},{16,0},{24,8},{1,17},{9,25},{17,1},{25,9},{2,18},{10... | collective-permute-start | bytes 3538952 | tf_op jit(solution)/shard_map/ppermute | solution.py:464
  359.5 27.9 %collective-permute-start.14 = (bf16[4,96,1536]{2,1,0:T(8,128)(2,1)}, bf16[4,96,1536]{2,1,0:T(8,128)(2,1)}, u32[]{:S(2)}, u32[]{:S(2)}) collective-permute-start(bf16[4,96,1536]{2,1,0:T(8,128)(2,1)} %get-tuple-element.190), channel_id=1, source_target_pairs={{0,8},{8,0},{16,24},{24,16},{1,9},{9,1},{17,25},{25,17},{2,10},{10... | collective-permute-start | bytes 3538952 | tf_op jit(solution)/shard_map/ppermute | solution.py:464
  406.9 16.3 %collective-permute-start.17 = (bf16[16,24,3072]{2,1,0:T(8,128)(2,1)}, bf16[16,24,3072]{2,1,0:T(8,128)(2,1)}, u32[]{:S(2)}, u32[]{:S(2)}) collective-permute-start(bf16[16,24,3072]{2,1,0:T(8,128)(2,1)} %dynamic-slice_bitcast_fusion.1), channel_id=1, source_target_pairs={{0,1},{1,0},{2,3},{3,2},{4,5},{5,4},{6,7},{7,6},{8,9},{9,8},{10,11... | collective-permute-start | bytes 7077896 | tf_op jit(solution)/shard_map/ppermute | solution.py:464
  410.7 18.2 %collective-permute-start.11 = (bf16[196,2,768]{2,1,0:T(2,128)(2,1)}, bf16[196,2,768]{2,1,0:T(2,128)(2,1)}, u32[]{:S(2)}, u32[]{:S(2)}) collective-permute-start(bf16[196,2,768]{2,1,0:T(2,128)(2,1)} %bitcast.182), channel_id=1, source_target_pairs={{0,6},{2,4},{4,2},{6,0},{1,7},{3,5},{5,3},{7,1},{8,14},{10,12},{12... | collective-permute-start | bytes 1806344 | tf_op jit(solution)/shard_map/ppermute | solution.py:464
  413.2 29.3 %collective-permute-start.18 = (bf16[4,96,1536]{2,1,0:T(8,128)(2,1)}, bf16[4,96,1536]{2,1,0:T(8,128)(2,1)}, u32[]{:S(2)}, u32[]{:S(2)}) collective-permute-start(bf16[4,96,1536]{2,1,0:T(8,128)(2,1)} %get-tuple-element.188), channel_id=1, source_target_pairs={{0,24},{8,16},{16,8},{24,0},{1,25},{9,17},{17,9},{25,1},{2,26},{10... | collective-permute-start | bytes 3538952 | tf_op jit(solution)/shard_map/ppermute | solution.py:464
  459.5 57.2 %all-to-all-start.2 = ((bf16[4,96,1536]{2,1,0:T(8,128)(2,1)}), bf16[4,96,1536]{2,1,0:T(8,128)(2,1)S(1)}, u32[]{:S(2)}, u32[]{:S(2)}) async-start(bf16[4,96,1536]{2,1,0:T(8,128)(2,1)} %fusion.6), calls=%async_computation.2 | async-start | bytes 2359296 | tf_op jit(solution)/shard_map/all_to_all | solution.py:676
  463.2 47.5 %collective-permute-start.19 = (bf16[16,24,1536]{2,1,0:T(8,128)(2,1)}, bf16[16,24,1536]{2,1,0:T(8,128)(2,1)}, u32[]{:S(2)}, u32[]{:S(2)}) collective-permute-start(bf16[16,24,1536]{2,1,0:T(8,128)(2,1)} %dynamic-slice_bitcast_fusion.3), channel_id=1, source_target_pairs={{0,1},{1,0},{2,3},{3,2},{4,5},{5,4},{6,7},{7,6},{8,9},{9,8},{10,11... | collective-permute-start | bytes 3538952 | tf_op jit(solution)/shard_map/ppermute | solution.py:464
  464.6 43.3 %collective-permute-start.20 = (bf16[4,24,3072]{2,1,0:T(8,128)(2,1)}, bf16[4,24,3072]{2,1,0:T(8,128)(2,1)}, u32[]{:S(2)}, u32[]{:S(2)}) collective-permute-start(bf16[4,24,3072]{2,1,0:T(8,128)(2,1)} %get-tuple-element.205), channel_id=1, source_target_pairs={{0,8},{8,0},{16,24},{24,16},{1,9},{9,1},{17,25},{25,17},{2,10},{10... | collective-permute-start | bytes 1769480 | tf_op jit(solution)/shard_map/ppermute | solution.py:464
  466.1 41.9 %collective-permute-start.22 = (bf16[4,24,3072]{2,1,0:T(8,128)(2,1)}, bf16[4,24,3072]{2,1,0:T(8,128)(2,1)}, u32[]{:S(2)}, u32[]{:S(2)}) collective-permute-start(bf16[4,24,3072]{2,1,0:T(8,128)(2,1)} %get-tuple-element.206), channel_id=1, source_target_pairs={{0,24},{8,16},{16,8},{24,0},{1,25},{9,17},{17,9},{25,1},{2,26},{10... | collective-permute-start | bytes 1769480 | tf_op jit(solution)/shard_map/ppermute | solution.py:464
  466.6 41.3 %collective-permute-start.21 = (bf16[4,24,3072]{2,1,0:T(8,128)(2,1)}, bf16[4,24,3072]{2,1,0:T(8,128)(2,1)}, u32[]{:S(2)}, u32[]{:S(2)}) collective-permute-start(bf16[4,24,3072]{2,1,0:T(8,128)(2,1)} %get-tuple-element.207), channel_id=1, source_target_pairs={{0,16},{8,24},{16,0},{24,8},{1,17},{9,25},{17,1},{25,9},{2,18},{10... | collective-permute-start | bytes 1769480 | tf_op jit(solution)/shard_map/ppermute | solution.py:464
  513.2 23.7 %collective-permute-start.23 = (bf16[4,24,1536]{2,1,0:T(8,128)(2,1)}, bf16[4,24,1536]{2,1,0:T(8,128)(2,1)}, u32[]{:S(2)}, u32[]{:S(2)}) collective-permute-start(bf16[4,24,1536]{2,1,0:T(8,128)(2,1)} %get-tuple-element.219), channel_id=1, source_target_pairs={{0,8},{8,0},{16,24},{24,16},{1,9},{9,1},{17,25},{25,17},{2,10},{10... | collective-permute-start | bytes 884744 | tf_op jit(solution)/shard_map/ppermute | solution.py:464
  514.7 22.1 %collective-permute-start.25 = (bf16[4,24,1536]{2,1,0:T(8,128)(2,1)}, bf16[4,24,1536]{2,1,0:T(8,128)(2,1)}, u32[]{:S(2)}, u32[]{:S(2)}) collective-permute-start(bf16[4,24,1536]{2,1,0:T(8,128)(2,1)} %get-tuple-element.220), channel_id=1, source_target_pairs={{0,24},{8,16},{16,8},{24,0},{1,25},{9,17},{17,9},{25,1},{2,26},{10... | collective-permute-start | bytes 884744 | tf_op jit(solution)/shard_map/ppermute | solution.py:464
  515.2 21.6 %collective-permute-start.24 = (bf16[4,24,1536]{2,1,0:T(8,128)(2,1)}, bf16[4,24,1536]{2,1,0:T(8,128)(2,1)}, u32[]{:S(2)}, u32[]{:S(2)}) collective-permute-start(bf16[4,24,1536]{2,1,0:T(8,128)(2,1)} %get-tuple-element.221), channel_id=1, source_target_pairs={{0,16},{8,24},{16,0},{24,8},{1,17},{9,25},{17,1},{25,9},{2,18},{10... | collective-permute-start | bytes 884744 | tf_op jit(solution)/shard_map/ppermute | solution.py:464
  516.7 20.1 %all-to-all-start.3 = ((bf16[4,24,3072]{2,1,0:T(8,128)(2,1)}), bf16[4,24,3072]{2,1,0:T(8,128)(2,1)S(1)}, u32[]{:S(2)}, u32[]{:S(2)}) async-start(bf16[4,24,3072]{2,1,0:T(8,128)(2,1)} %fusion.9), calls=%async_computation.3 | async-start | bytes 1179648 | tf_op jit(solution)/shard_map/all_to_all | solution.py:534
  539.7 24.4 %collective-permute-start.26 = (bf16[24,1536]{1,0:T(8,128)(2,1)S(1)}, bf16[24,1536]{1,0:T(8,128)(2,1)S(1)}, u32[]{:S(2)}, u32[]{:S(2)}) collective-permute-start(bf16[24,1536]{1,0:T(8,128)(2,1)S(1)} %get-tuple-element.227), channel_id=1, source_target_pairs={{0,2},{2,0},{4,6},{6,4},{1,3},{3,1},{5,7},{7,5},{8,10},{10,8},{12,... | collective-permute-start | bytes 221192 | tf_op jit(solution)/shard_map/ppermute | solution.py:464
  539.8 24.3 %collective-permute-start.28 = (bf16[24,1536]{1,0:T(8,128)(2,1)S(1)}, bf16[24,1536]{1,0:T(8,128)(2,1)S(1)}, u32[]{:S(2)}, u32[]{:S(2)}) collective-permute-start(bf16[24,1536]{1,0:T(8,128)(2,1)S(1)} %get-tuple-element.228), channel_id=1, source_target_pairs={{0,6},{2,4},{4,2},{6,0},{1,7},{3,5},{5,3},{7,1},{8,14},{10,12},{12... | collective-permute-start | bytes 221192 | tf_op jit(solution)/shard_map/ppermute | solution.py:464
  541.6 22.5 %collective-permute-start.27 = (bf16[24,1536]{1,0:T(8,128)(2,1)S(1)}, bf16[24,1536]{1,0:T(8,128)(2,1)S(1)}, u32[]{:S(2)}, u32[]{:S(2)}) collective-permute-start(bf16[24,1536]{1,0:T(8,128)(2,1)S(1)} %get-tuple-element.229), channel_id=1, source_target_pairs={{0,4},{2,6},{4,0},{6,2},{1,5},{3,7},{5,1},{7,3},{8,12},{10,14},{12... | collective-permute-start | bytes 221192 | tf_op jit(solution)/shard_map/ppermute | solution.py:464
  544.6 27.2 %collective-permute-start.30 = (bf16[16,24,2304]{2,1,0:T(8,128)(2,1)}, bf16[16,24,2304]{2,1,0:T(8,128)(2,1)}, u32[]{:S(2)}, u32[]{:S(2)}) collective-permute-start(bf16[16,24,2304]{2,1,0:T(8,128)(2,1)} %dynamic-slice_bitcast_fusion.2), channel_id=1, source_target_pairs={{0,1},{1,0},{2,3},{3,2},{4,5},{5,4},{6,7},{7,6},{8,9},{9,8},{10,11... | collective-permute-start | bytes 5308424 | tf_op jit(solution)/shard_map/ppermute | solution.py:464
  558.4 13.3 %collective-permute-start.29 = (f32[28,768]{1,0:T(8,128)S(1)}, f32[28,768]{1,0:T(8,128)S(1)}, u32[]{:S(2)}, u32[]{:S(2)}) collective-permute-start(f32[28,768]{1,0:T(8,128)S(1)} %pad_maximum_fusion.6), channel_id=1, source_target_pairs={{0,1},{1,0},{2,3},{3,2},{4,5},{5,4},{6,7},{7,6},{8,9},{9,8},{10,11... | collective-permute-start | bytes 258056 | tf_op jit(solution)/shard_map/ppermute | solution.py:464
  564.1 78.8 %all-to-all-start.4 = ((bf16[4,196,2,768]{3,2,1,0:T(2,128)(2,1)}), bf16[4,196,2,768]{3,2,1,0:T(2,128)(2,1)S(1)}, u32[]{:S(2)}, u32[]{:S(2)}) async-start(bf16[4,196,2,768]{3,2,1,0:T(2,128)(2,1)} %bitcast.178), calls=%async_computation.4 | async-start | bytes 4816896 | tf_op jit(solution)/shard_map/all_to_all | solution.py:598
  573.8 13.1 %collective-permute-start.31 = (bf16[4,24,2304]{2,1,0:T(8,128)(2,1)S(1)}, bf16[4,24,2304]{2,1,0:T(8,128)(2,1)S(1)}, u32[]{:S(2)}, u32[]{:S(2)}) collective-permute-start(bf16[4,24,2304]{2,1,0:T(8,128)(2,1)S(1)} %get-tuple-element.212), channel_id=1, source_target_pairs={{0,8},{8,0},{16,24},{24,16},{1,9},{9,1},{17,25},{25,17},{2,10},{10... | collective-permute-start | bytes 1327112 | tf_op jit(solution)/shard_map/ppermute | solution.py:464
  575.4 20.2 %collective-permute-start.33 = (bf16[4,24,2304]{2,1,0:T(8,128)(2,1)S(1)}, bf16[4,24,2304]{2,1,0:T(8,128)(2,1)S(1)}, u32[]{:S(2)}, u32[]{:S(2)}) collective-permute-start(bf16[4,24,2304]{2,1,0:T(8,128)(2,1)S(1)} %get-tuple-element.213), channel_id=1, source_target_pairs={{0,24},{8,16},{16,8},{24,0},{1,25},{9,17},{17,9},{25,1},{2,26},{10... | collective-permute-start | bytes 1327112 | tf_op jit(solution)/shard_map/ppermute | solution.py:464
  575.9 21.0 %collective-permute-start.32 = (bf16[4,24,2304]{2,1,0:T(8,128)(2,1)S(1)}, bf16[4,24,2304]{2,1,0:T(8,128)(2,1)S(1)}, u32[]{:S(2)}, u32[]{:S(2)}) collective-permute-start(bf16[4,24,2304]{2,1,0:T(8,128)(2,1)S(1)} %get-tuple-element.214), channel_id=1, source_target_pairs={{0,16},{8,24},{16,0},{24,8},{1,17},{9,25},{17,1},{25,9},{2,18},{10... | collective-permute-start | bytes 1327112 | tf_op jit(solution)/shard_map/ppermute | solution.py:464
  597.1 5.8 collective-permute-start.36
  599.6 4.6 collective-permute-start.35
  604.8 9.6 %collective-permute-start.39 = (f32[28,768]{1,0:T(8,128)S(1)}, f32[28,768]{1,0:T(8,128)S(1)}, u32[]{:S(2)}, u32[]{:S(2)}) collective-permute-start(f32[28,768]{1,0:T(8,128)S(1)} %add_add_fusion.1), channel_id=1, source_target_pairs={{0,6},{2,4},{4,2},{6,0},{1,7},{3,5},{5,3},{7,1},{8,14},{10,12},{12... | collective-permute-start | bytes 258056 | tf_op jit(solution)/shard_map/ppermute | solution.py:464
  608.3 27.8 %collective-permute-start.38 = (f32[28,768]{1,0:T(8,128)S(1)}, f32[28,768]{1,0:T(8,128)S(1)}, u32[]{:S(2)}, u32[]{:S(2)}) collective-permute-start(f32[28,768]{1,0:T(8,128)S(1)} %add_add_fusion.1), channel_id=1, source_target_pairs={{0,4},{2,6},{4,0},{6,2},{1,5},{3,7},{5,1},{7,3},{8,12},{10,14},{12... | collective-permute-start | bytes 258056 | tf_op jit(solution)/shard_map/ppermute | solution.py:464
  608.3 27.8 %collective-permute-start.37 = (f32[28,768]{1,0:T(8,128)S(1)}, f32[28,768]{1,0:T(8,128)S(1)}, u32[]{:S(2)}, u32[]{:S(2)}) collective-permute-start(f32[28,768]{1,0:T(8,128)S(1)} %add_add_fusion.1), channel_id=1, source_target_pairs={{0,2},{2,0},{4,6},{6,4},{1,3},{3,1},{5,7},{7,5},{8,10},{10,8},{12,... | collective-permute-start | bytes 258056 | tf_op jit(solution)/shard_map/ppermute | solution.py:464
  609.3 30.6 %collective-permute-start.40 = (bf16[24,2304]{1,0:T(8,128)(2,1)S(1)}, bf16[24,2304]{1,0:T(8,128)(2,1)S(1)}, u32[]{:S(2)}, u32[]{:S(2)}) collective-permute-start(bf16[24,2304]{1,0:T(8,128)(2,1)S(1)} %get-tuple-element.224), channel_id=1, source_target_pairs={{0,2},{2,0},{4,6},{6,4},{1,3},{3,1},{5,7},{7,5},{8,10},{10,8},{12,... | collective-permute-start | bytes 331784 | tf_op jit(solution)/shard_map/ppermute | solution.py:464
  610.5 29.4 %collective-permute-start.42 = (bf16[24,2304]{1,0:T(8,128)(2,1)S(1)}, bf16[24,2304]{1,0:T(8,128)(2,1)S(1)}, u32[]{:S(2)}, u32[]{:S(2)}) collective-permute-start(bf16[24,2304]{1,0:T(8,128)(2,1)S(1)} %get-tuple-element.225), channel_id=1, source_target_pairs={{0,6},{2,4},{4,2},{6,0},{1,7},{3,5},{5,3},{7,1},{8,14},{10,12},{12... | collective-permute-start | bytes 331784 | tf_op jit(solution)/shard_map/ppermute | solution.py:464
  614.4 26.8 %collective-permute-start.41 = (bf16[24,2304]{1,0:T(8,128)(2,1)S(1)}, bf16[24,2304]{1,0:T(8,128)(2,1)}, u32[]{:S(2)}, u32[]{:S(2)}) collective-permute-start(bf16[24,2304]{1,0:T(8,128)(2,1)S(1)} %get-tuple-element.226), channel_id=1, source_target_pairs={{0,4},{2,6},{4,0},{6,2},{1,5},{3,7},{5,1},{7,3},{8,12},{10,14},{12... | collective-permute-start | bytes 331784 | tf_op jit(solution)/shard_map/ppermute | solution.py:464
  (29 other events, 194.3 us)
Sparse Core Ops, SparseCore 0:
  58.1 141.1 all-gather.1

commit v2 on v1

--- a/solution.py
+++ b/solution.py
@@ -22,17 +22,19 @@
     inv = lax.rsqrt(jnp.mean(centered * centered, axis=-1, keepdims=True) + EPS)
     return centered * inv, inv
 
-def mlp_kernel(x_ref, cot_ref, keep_ref, gain_ref, shift_ref, w_ref, hb_ref, wb_ref,
+def mlp_kernel(x_ref, cota_ref, cotb_ref, keep_ref, gain_ref, shift_ref, w_ref, hb_ref, wb_ref,
                out_ref, g2_ref, db_ref, dw_ref, dhb_ref, sums_ref,
-               a_ref, at_ref, dm_ref, dmt_ref, m_ref, da_ref, h_ref, du_ref, *, rb, chunks):
+               a_ref, at_ref, dm_ref, dmt_ref, m_ref, da_ref, h_ref, du_ref, *, rb, chunks, frames):
     step = pl.program_id(0)
     T, D = x_ref.shape
+    cot_ref = out_ref
     nb = T // rb
     blocks, _, both, hc = w_ref.shape
     half = both // 2
 
     @pl.when(step == 0)
     def _():
+        merge(cot_ref, (cota_ref, cotb_ref), frames)
         def body(i, c):
             r = pl.ds(pl.multiple_of(i * rb, 16), rb)
             unit, _ = norm_stats(x_ref[r, :])
@@ -71,8 +73,8 @@
             m_ref[r, :] += m
             da_ref[r, :] += da
     dhb_ref[...] = tot
-    dw_ref[0, :, :half, :] = mm(at_ref[...], du_ref[...], 1, 0).astype(BF).reshape(blocks, half, hc)
-    dw_ref[0, :, half:, :] = mm(dmt_ref[...], h_ref[...], 1, 0).astype(BF).reshape(blocks, half, hc)
+    dw_ref[:, 0, :half, :] = mm(at_ref[...], du_ref[...], 1, 0).astype(BF).reshape(blocks, half, hc)
+    dw_ref[:, 0, half:, :] = mm(dmt_ref[...], h_ref[...], 1, 0).astype(BF).reshape(blocks, half, hc)
 
     @pl.when(step == chunks - 1)
     def _():
@@ -80,8 +82,8 @@
         def body(i, c):
             r = pl.ds(pl.multiple_of(i * rb, 16), rb)
             x = x_ref[r, :]
+            g3 = k * cot_ref[r, :].astype(F32)
             out_ref[r, :] = (k * (x + (m_ref[r, :] + wb_ref[...]))).astype(BF)
-            g3 = k * cot_ref[r, :].astype(F32)
             da = da_ref[r, :]
             unit, inv = norm_stats(x)
             sc = da * gain_ref[...]
@@ -99,7 +101,7 @@
         for j in range(4):
             sums_ref[j:j+1, :] = c[j]
 
-def mlp(x2, cot, keep, gain, shift, w4, hb, wb):
+def mlp(x2, cot_a, cot_b, keep, gain, shift, w4, hb, wb, *, frames):
     T, D = x2.shape
     B, H2, R, C = w4.shape
     rb = T // 4 if T % 64 == 0 else T
@@ -108,19 +110,18 @@
     chunks = H2 * per
     full = lambda *s: pl.BlockSpec(s, lambda j: (0,) * len(s), pipeline_mode=pl.Buffered(1))
     wspec = pl.BlockSpec((B, 1, R, hc), lambda j: (0, j // per, 0, j % per))
-    dspec = pl.BlockSpec((1, B, R, hc), lambda j: (j // per, 0, 0, j % per))
     hspec = pl.BlockSpec((1, hc), lambda j: (0, j))
     return pl.pallas_call(
-        partial(mlp_kernel, rb=rb, chunks=chunks),
+        partial(mlp_kernel, rb=rb, chunks=chunks, frames=frames),
         grid=(chunks,),
-        in_specs=[full(T, D), full(T, D), pl.BlockSpec(memory_space=pltpu.SMEM), full(1, D), full(1, D), wspec, hspec, full(1, D)],
-        out_specs=[full(T, D), full(T, D), full(T, D), dspec, hspec, full(8, D)],
-        out_shape=(sds(T, D), sds(T, D, t=F32), sds(T, D), sds(H2, B, R, C), sds(1, H2 * C, t=F32), sds(8, D, t=F32)),
+        in_specs=[full(T, D), full(*cot_a.shape), full(*cot_b.shape), pl.BlockSpec(memory_space=pltpu.SMEM), full(1, D), full(1, D), wspec, hspec, full(1, D)],
+        out_specs=[full(T, D), full(T, D), full(T, D), wspec, hspec, full(8, D)],
+        out_shape=(sds(T, D), sds(T, D, t=F32), sds(T, D), sds(*w4.shape), sds(1, H2 * C, t=F32), sds(8, D, t=F32)),
         scratch_shapes=[pltpu.VMEM((T, D), BF), pltpu.VMEM((D, T), BF), pltpu.VMEM((T, D), BF), pltpu.VMEM((D, T), BF),
                         pltpu.VMEM((T, D), F32), pltpu.VMEM((T, D), F32), pltpu.VMEM((T, hc), BF), pltpu.VMEM((T, hc), BF)],
         compiler_params=pltpu.CompilerParams(vmem_limit_bytes=VMEM),
         cost_estimate=cost(75),
-    )(x2, cot, keep, gain, shift, w4, hb, wb)
+    )(x2, cot_a, cot_b, keep, gain, shift, w4, hb, wb)
 LANES = 128
 LOW = -1e30
 
@@ -150,9 +151,28 @@
     lane = lax.broadcasted_iota(jnp.int32, (1, LANES), 1)
     return [jnp.where(lane // head == i, value, 0.0).astype(BF) for i in range(LANES // head)]
 
-def sf_kernel(x_ref, gain_ref, shift_ref, wqkv_ref, wproj_ref, hb_ref, wb_ref, a_ref, qkv_ref, o_ref, x2_ref, *, fb, real, head, scale):
+def merge(dst_ref, parts, fb):
+    P = dst_ref.shape[0] // fb
+    for f in range(fb):
+        at = f * P
+        for part in parts:
+            n = part.shape[0] // fb
+            dst_ref[at:at + n, :] = part[f * n:(f + 1) * n, :]
+            at += n
+
+def split(value, dst_refs, fb):
+    P = value.shape[0] // fb
+    for f in range(fb):
+        at = f * P
+        for dst in dst_refs:
+            n = dst.shape[0] // fb
+            dst[f * n:(f + 1) * n, :] = value[at:at + n, :]
+            at += n
+
+def sf_kernel(xa_ref, xb_ref, gain_ref, shift_ref, wqkv_ref, wproj_ref, hb_ref, wb_ref, a_ref, qkv_ref, o_ref, x2_ref, x_ref, *, fb, real, head, scale):
     M, D = x_ref.shape
     P = M // fb
+    merge(x_ref, (xa_ref, xb_ref), fb)
     unit, _ = norm_stats(x_ref[...])
     a = (unit * gain_ref[...] + shift_ref[...]).astype(BF)
     a_ref[...] = a
@@ -176,14 +196,18 @@
             o_ref[r, j * LANES:(j + 1) * LANES] = o.astype(BF)
     x2_ref[...] = x_ref[...] + (mm(o_ref[...], wproj_ref[...], 1, 1) + wb_ref[...])
 
-def spatial_forward(x1, gain, shift, w, hb, wb, *, frames, real, head, scale, fb=2):
-    T, D = x1.shape
-    M = T // frames * fb
-    blk = lambda w: pl.BlockSpec((M, w), lambda j: (j, 0))
-    return call(partial(sf_kernel, fb=fb, real=real, head=head, scale=scale), 30, frames // fb,
-        [blk(D), once(1, D), once(1, D), column(D, 3 * D, 0), column(D, D, 3), once(2, D), once(1, D)],
-        [blk(D), blk(3 * D), blk(D), blk(D)], (sds(T, D), sds(T, 3 * D), sds(T, D), sds(T, D, t=F32)))(
-        x1, gain, shift, w, w, hb, wb)
+def frame_blocks(rows, width, at=0):
+    return pl.BlockSpec((rows, width), lambda j: (j + at, 0))
+
+def spatial_forward(xa, xb, gain, shift, w, hb, wb, *, frames, real, head, scale, fb=2):
+    D = xa.shape[1]
+    steps = frames // fb
+    T = xa.shape[0] + xb.shape[0]
+    blk = lambda width, rows=T: frame_blocks(rows // steps, width)
+    return call(partial(sf_kernel, fb=fb, real=real, head=head, scale=scale), 30, steps,
+        [blk(D, xa.shape[0]), blk(D, xb.shape[0]), once(1, D), once(1, D), column(D, 3 * D, 0), column(D, D, 3), once(2, D), once(1, D)],
+        [blk(D), blk(3 * D), blk(D), blk(D), blk(D)], (sds(T, D), sds(T, 3 * D), sds(T, D), sds(T, D, t=F32), sds(T, D, t=F32)))(
+        xa, xb, gain, shift, w, w, hb, wb)
 
 def norm_back_store(x, gain, da, base, sums_ref, at):
     unit, inv = norm_stats(x)
@@ -197,7 +221,7 @@
     sums_ref[at:at + 1, :] += jnp.sum(rows.astype(F32), axis=0, keepdims=True)
 
 def sb_kernel(g2_ref, db_ref, qkv_ref, x_ref, gain_ref, wqkv_ref, wproj_ref, *rest, fb, real, head, scale):
-    dqkv_ref, g1_ref, dz_ref, sums_ref, do_ref = rest[-5:]
+    dqkv_ref, g1a_ref, g1b_ref, dza_ref, dzb_ref, sums_ref, do_ref = rest[-7:]
     M, D = x_ref.shape
     P = M // fb
     @pl.when(pl.program_id(0) == 0)
@@ -232,23 +256,25 @@
     add_sum(sums_ref, 3, dqkv_ref[:, 2 * D:])
     da = mm(dqkv_ref[...], wqkv_ref[...], 1, 1)
     g1 = norm_back_store(x_ref[...], gain_ref[...], da, g2_ref[...], sums_ref, 0)
-    g1_ref[...] = g1
+    split(g1, (g1a_ref, g1b_ref), fb)
     low = g1.astype(BF)
-    dz_ref[...] = low
+    split(low, (dza_ref, dzb_ref), fb)
     add_sum(sums_ref, 4, low)
 
-def spatial_backward(g2, db, qkv, x1, *, gain, w, frames, real, head, scale, part, held=None, fb=2):
+def spatial_backward(g2, db, qkv, x1, *, gain, w, first, frames, real, head, scale, part, held=None, fb=2):
     T, D = x1.shape
     M = T // frames * fb
     nb = frames // fb // 2
-    blk = lambda w: pl.BlockSpec((M, w), lambda j: (j + part * nb, 0))
-    kept = [] if held is None else list(held[:3])
+    blk = lambda width, rows=M: frame_blocks(rows, width, part * nb)
+    kept = [] if held is None else list(held[:5])
+    low, high = frames * first, T - frames * first
+    ends = [blk(D, first * fb), blk(D, M - first * fb)]
     return pl.pallas_call(
         partial(sb_kernel, fb=fb, real=real, head=head, scale=scale), grid=(nb,),
         in_specs=[blk(D), blk(D), blk(3 * D), blk(D), once(1, D), column(D, 3 * D, 0), column(D, D, 3)]
         + [pl.BlockSpec(memory_space=pl.ANY)] * len(kept),
-        out_specs=[blk(3 * D), blk(D), blk(D), once(8, D)],
-        out_shape=(sds(T, 3 * D), sds(T, D, t=F32), sds(T, D), sds(8, D, t=F32)),
+        out_specs=[blk(3 * D)] + ends + ends + [once(8, D)],
+        out_shape=(sds(T, 3 * D), sds(low, D, t=F32), sds(high, D, t=F32), sds(low, D), sds(high, D), sds(8, D, t=F32)),
         scratch_shapes=[pltpu.VMEM((M, D), BF)],
         input_output_aliases={7 + i: i for i in range(len(kept))},
         compiler_params=pltpu.CompilerParams(vmem_limit_bytes=VMEM), cost_estimate=cost(24),
@@ -317,13 +343,13 @@
             else:
                 ref[:, g * D:(g + 1) * D] = hit
 
-def temporal_forward(x, gain, shift, w, hb, wb, fcb, *, frames, head, scale, fb=2):
+def temporal_forward(x, gain, shift, w, hb, wb, fcb, *, frames, head, scale, fb=4):
     T, D = x.shape
     M = T // frames * fb
     nb = frames // fb
     first = lambda w: pl.BlockSpec((M, w), lambda j: (jnp.minimum(j, nb - 1), 0))
     last = lambda w: pl.BlockSpec((M, w), lambda j: (jnp.maximum(j - nb, 0), 0))
-    return call(partial(tf_kernel, fb=fb, nb=nb, frames=frames, slot=LANES // frames, head=head, scale=scale), 44, 2 * nb,
+    return call(partial(tf_kernel, fb=fb, nb=nb, frames=frames, slot=LANES // frames, head=head, scale=scale), 22, 2 * nb,
         [first(D), once(1, D), once(1, D), column(D, 3 * D, 0), column(D, D, 3), column(D, D, 4), once(2, D), once(1, D), once(1, D)],
         [first(D), first(3 * D), last(LANES), last(D), last(D), last(D)],
         (sds(T, D), sds(T, 3 * D), sds(T, LANES, t=F32), sds(T, D), sds(T, D), sds(T, D, t=F32)),
@@ -344,10 +370,10 @@
     add_sum(sums_ref, 4, dy)
     do_ref[...] = mm(dy, wproj_ref[...], 1, 0).astype(BF)
 
-def temporal_pull(dz, w, *, blocks=4):
+def temporal_pull(dz, w, *, blocks=2):
     T, D = dz.shape
     blk = pl.BlockSpec((T // blocks, D), lambda j: (j, 0))
-    return call(pull_kernel, 8, blocks, [blk, column(D, D, 3), column(D, D, 4)], [blk, blk, once(8, D)],
+    return call(pull_kernel, 4, blocks, [blk, column(D, D, 3), column(D, D, 4)], [blk, blk, once(8, D)],
                 (sds(T, D), sds(T, D), sds(8, D, t=F32)))(dz, w, w)
 
 def tb_kernel(do_ref, qkv_ref, p_ref, dqkv_ref, sums_ref, dk_ref, dv_ref, prod_ref, e_ref, b_ref, *, fb, nb, frames, slot, head, scale):
@@ -396,11 +422,11 @@
             add_sum(sums_ref, 3, low)
             dqkv_ref[gr, 2 * D:] = low
 
-def temporal_backward(do, qkv, p, *, frames, head, scale, fb=2):
+def temporal_backward(do, qkv, p, *, frames, head, scale, fb=4):
     T, D = do.shape
     M = T // frames * fb
     nb = frames // fb
-    return call(partial(tb_kernel, fb=fb, nb=nb, frames=frames, slot=LANES // frames, head=head, scale=scale), 40, nb,
+    return call(partial(tb_kernel, fb=fb, nb=nb, frames=frames, slot=LANES // frames, head=head, scale=scale), 20, nb,
         [once(T, D), once(T, 3 * D), pl.BlockSpec((M, LANES), lambda j: (j, 0))],
         [once(T, 3 * D), once(8, D)], (sds(T, 3 * D), sds(8, D, t=F32)),
         [pltpu.VMEM((T, D), F32), pltpu.VMEM((T, D), F32), pltpu.VMEM((M, frames * D), BF),
@@ -412,24 +438,28 @@
     out = norm_back_store(x_ref[...].astype(F32), gain_ref[...], da, g1_ref[...], sums_ref, 0)
     out_ref[...] = out.astype(BF)
 
-def temporal_end(dqkv, x, g1, gain, w, *, blocks=4):
+def temporal_end(dqkv, x, g1, gain, w, *, blocks=2):
     T, D = x.shape
     blk = lambda w: pl.BlockSpec((T // blocks, w), lambda j: (j, 0))
-    return call(end_kernel, 12, blocks, [blk(3 * D), blk(D), blk(D), once(1, D), column(D, 3 * D, 0)], [blk(D), once(8, D)],
+    return call(end_kernel, 7, blocks, [blk(3 * D), blk(D), blk(D), once(1, D), column(D, 3 * D, 0)], [blk(D), once(8, D)],
                 (sds(T, D), sds(8, D, t=F32)))(dqkv, x, g1, gain, w)
 
-def wg_kernel(*refs, starts, halves, rows):
-    n = len(starts)
-    a_refs, b_refs, out_ref, t_ref = refs[:n], refs[n:2 * n], refs[2 * n], refs[2 * n + 1]
+def wg_kernel(*refs, starts, counts, halves, rows):
+    n = sum(counts)
+    a_refs, b_refs, out_ref, t_refs = refs[:n], refs[n:2 * n], refs[2 * n], refs[2 * n + 1:]
     step = pl.program_id(0)
-    for i in range(n):
+    at = 0
+    for i, many in enumerate(counts):
+        mine = range(at, at + many)
+        at += many
         @pl.when(step == starts[i])
         def _():
-            t_ref[...] = a_refs[i][...].T
-        stop = starts[i + 1] if i + 1 < n else step + 1
+            for t_ref, n_at in zip(t_refs, mine):
+                t_ref[...] = a_refs[n_at][...].T
+        stop = starts[i + 1] if i + 1 < len(counts) else step + 1
         @pl.when((step >= starts[i]) & (step < stop))
         def _():
-            res = mm(t_ref[...], b_refs[i][...], 1, 0)
+            res = sum(mm(t_ref[...], b_refs[n_at][...], 1, 0) for t_ref, n_at in zip(t_refs, mine))
             if rows:
                 parts = res.reshape(-1, halves, rows, res.shape[-1])
                 for h in range(halves):
@@ -438,24 +468,30 @@
                 out_ref[0] = res.astype(BF)
 
 def weight_grads(pairs, halves, rows, us):
-    T, D = pairs[0][0].shape
-    starts, steps = [], 0
-    for a, b in pairs:
+    D = pairs[0][0][0].shape[1]
+    starts, steps, specs, b_specs = [], 0, [], []
+    for many_a, many_b in pairs:
         starts.append(steps)
-        steps += b.shape[1] // D
+        chunks = many_b[0].shape[1] // D
+        for a in many_a:
+            specs.append(once(*a.shape))
+            b_specs.append(chunk_spec(a.shape[0], D, steps, chunks))
+        steps += chunks
     cols = steps * D
     fits = rows % 8 == 0
-    def chunk(i):
-        many = pairs[i][1].shape[1] // D
-        return pl.BlockSpec((T, D), lambda j: (0, jnp.clip(j - starts[i], 0, many - 1)))
     groups = halves if fits else 1
-    out = call(partial(wg_kernel, starts=starts, halves=halves, rows=rows if fits else 0), us, steps,
-        [once(T, D)] * len(pairs) + [chunk(i) for i in range(len(pairs))],
-        [pl.BlockSpec((groups, D // groups, D), lambda j: (0, 0, j))], (sds(groups, D // groups, cols),),
-        [pltpu.VMEM((D, T), BF)])(*[a for a, _ in pairs], *[b for _, b in pairs])[0]
+    counts = [len(many_a) for many_a, _ in pairs]
+    lefts = [a for many_a, _ in pairs for a in many_a]
+    rights = [b for _, many_b in pairs for b in many_b]
+    out = call(partial(wg_kernel, starts=starts, counts=counts, halves=halves, rows=rows if fits else 0), us, steps,
+        specs + b_specs, [pl.BlockSpec((groups, D // groups, D), lambda j: (0, 0, j))], (sds(groups, D // groups, cols),),
+        [pltpu.VMEM((D, a.shape[0]), BF) for a in pairs[0][0]])(*lefts, *rights)[0]
     if fits:
         return out.reshape(halves, -1, rows, cols)
     return jnp.swapaxes(out.reshape(-1, halves, rows, cols), 0, 1)
+
+def chunk_spec(rows, cols, start, many):
+    return pl.BlockSpec((rows, cols), lambda j: (0, jnp.clip(j - start, 0, many - 1)))
 
 
 def exchange(pieces, axis):
@@ -575,7 +611,8 @@
     clips = held // across if spread else held
     share = 1.0 if spread else 1.0 / across
     frames = frames_held * across
-    padded = -(-places // 16) * 16
+    first_places = places // 32 * 16
+    cuts = (slice(0, first_places), slice(first_places, places))
 
     def to_clips(array):
         array = jnp.swapaxes(array, 1, 2)
@@ -585,12 +622,12 @@
         return lax.all_gather(array, "context", axis=0)
 
     def fill(array):
-        array = jnp.swapaxes(array, 1, 2).reshape(frames, places, width)
-        array = jnp.pad(array, ((0, 0), (0, padded - places), (0, 0)))
-        return array.reshape(frames * padded, width)
-
-    def by_place(array):
-        array = array.reshape(across, frames_held, padded, width)[:, :, :places]
+        array = jnp.swapaxes(array, 1, 2).reshape(frames, array.shape[1], width)
+        array = jnp.pad(array, ((0, 0), (0, -array.shape[1] % 16), (0, 0)))
+        return array.reshape(-1, width)
+
+    def by_place(array, real):
+        array = array.reshape(across, frames_held, -1, width)[:, :, :real]
         return jnp.swapaxes(array, 1, 2)
 
     def from_clips(array):
@@ -598,10 +635,10 @@
             array = lax.all_to_all(array, "context", split_axis=0, concat_axis=0, tiled=True)
         else:
             array = lax.dynamic_slice_in_dim(array, place, 1, 0)
-        return jnp.swapaxes(array, 1, 2)
+        return array
 
     def send_back(array):
-        array = by_place(array)
+        array = by_place(array, places)
         if spread:
             return split_off(array, "context")
         return [lax.dynamic_index_in_dim(array, place, 0, keepdims=False)]
@@ -624,99 +661,115 @@
     t_own = jnp.concatenate((flat3(temporal_qkv), temporal_proj, temporal_fc), axis=1).astype(BF)
     s_own = jnp.concatenate((flat3(spatial_qkv), spatial_proj), axis=1).astype(BF)
     mlp_own = jnp.concatenate((mlp_in, mlp_out), axis=0).astype(BF)
-    first = collect(jnp.concatenate((t_own, s_own), axis=1), "context")
+    clip_parts = [clips_in[:, :, cut] for cut in cuts]
+    pull_parts = [cotangent[:, :, cut] for cut in cuts]
+    gain = [norm_gains[i : i + 1] for i in range(3)]
+    shift = [norm_shifts[i : i + 1] for i in range(3)]
+    wide = [width_bias[i : i + 1] for i in range(3)]
+    head_pairs, fc_row, hidden_row = [head_bias[0], head_bias[1]], fc_bias[None], hidden_bias[None]
+    early = clip_parts + pull_parts + gain + shift + wide + head_pairs + [fc_row, hidden_row]
+    first = collect(jnp.concatenate((t_own, s_own), axis=1), "context", hold=early)
     t_first, s_first = first[..., : t_own.shape[1]], first[..., t_own.shape[1] :]
+    rows_a = to_clips(after(clip_parts[0], first))
     mlp_all = lax.all_gather(after(mlp_own, first), ALL, axis=0, tiled=True)
     mlp_all = mlp_all.reshape(-1, halves, 2 * in_rows, in_cols)
-
-    rows_in = to_clips(after(clips_in, first))
-    t_chips = collect(t_first, "shard", hold=(rows_in,))
+    t_chips = collect(t_first, "shard", hold=(rows_a,))
     t_all = collect(t_chips, "tensor", 2).reshape(-1, t_own.shape[1])
-    pulled = to_clips(after(cotangent, rows_in))
-
-    def one_clip(x, pull, keep_one):
+    rows_b = to_clips(after(clip_parts[1], rows_a))
+    pull_a = to_clips(after(pull_parts[0], rows_b))
+    pull_b = to_clips(after(pull_parts[1], pull_a))
+
+    def one_clip(x_a, x_b, pull_a, pull_b, keep_one):
         sizes = dict(frames=frames, head=head, scale=scale)
-        gain = [norm_gains[i : i + 1] for i in range(3)]
-        shift = [norm_shifts[i : i + 1] for i in range(3)]
-        wide = [width_bias[i : i + 1] for i in range(3)]
-        x = fill(x)
-        a_t, qkv_t, probs, o_t, y, x1 = temporal_forward(
-            x, gain[0], shift[0], t_all, head_bias[0], wide[0], fc_bias[None], **sizes,
+        forward_t = partial(
+            temporal_forward, gain=gain[0], shift=shift[0], w=t_all, hb=head_pairs[0], wb=wide[0],
+            fcb=fc_row, **sizes,
         )
-        s_all = collect(after(s_first, rows_in), "shard", hold=(x1,))
-        s_all = collect(s_all, "tensor", 2).reshape(-1, s_own.shape[1])
+        x_a = fill(x_a)
+        at_a, qkv_a, probs_a, o_a, y_a, x1_a = forward_t(x_a)
+        s_all = collect(after(s_first, rows_a), "shard", hold=(x1_a,))
+        x_b = fill(after(x_b, x1_a, s_all))
+        at_b, qkv_b, probs_b, o_b, y_b, x1_b = forward_t(x_b)
+        s_all = collect(s_all, "tensor", 2, hold=(x1_b,)).reshape(-1, s_own.shape[1])
+        pull_a = after(pull_a, x1_b)
         sizes_s = dict(sizes, real=places)
-        a_s, qkv_s, o_s, x2 = spatial_forward(
-            x1, gain[1], shift[1], s_all, head_bias[1], wide[1], **sizes_s
+        a_s, qkv_s, o_s, x2, x1 = spatial_forward(
+            x1_a, after(x1_b, pull_a), gain[1], shift[1], s_all, head_pairs[1], wide[1], **sizes_s
         )
         out, g2, db, d_m, d_hidden, sums_m = mlp(
-            x2, fill(after(pull, x1)), keep_one.reshape(1, 1), gain[2], shift[2], mlp_all, hidden_bias[None], wide[2]
+            x2, fill(pull_a), fill(after(pull_b, x2)), keep_one.reshape(1, 1), gain[2], shift[2], mlp_all, hidden_row, wide[2],
+            frames=frames,
         )
-        back_s = partial(spatial_backward, gain=gain[1], w=s_all, **sizes_s)
+        back_s = partial(spatial_backward, gain=gain[1], w=s_all, first=first_places, **sizes_s)
         grads_of = partial(weight_grads, halves=halves, rows=own_rows)
-        d_m = split_off(share * d_m if share != 1.0 else d_m, "tensor")
+        d_m = (share * d_m if share != 1.0 else d_m).astype(BF).reshape(-1, in_cols)
+        d_m = lax.psum_scatter(d_m, ALL, scatter_dimension=0, tiled=True)
         back = send_back(out)
         half = back_s(g2, db, qkv_s, x1, part=0)
-        d_m = added(d_m, half[0]).astype(BF)
-        tied = after(db, d_m, half[0], *back[1:2])
-        d_m = split_off(by_shard(d_m), "shard")
-        d_qkv_s, g1, dz, sums_s = back_s(g2, tied, qkv_s, x1, part=1, held=half)
-        sums_s = sums_s + half[3]
-        tied = after(d_qkv_s, *d_m[1:3], *back[2:3])
-        d_s = share * grads_of([(a_s, tied), (db, o_s)], us=12)
-        tied = after(dz, d_s)
+        tied = after(db, half[0], *back[1:2])
+        d_qkv_s, g1_a, g1_b, dz_a, dz_b, sums_s = back_s(g2, tied, qkv_s, x1, part=1, held=half)
+        sums_s = sums_s + half[5]
+        tied = after(d_qkv_s, *back[2:3])
+        d_s = share * grads_of([([a_s], [tied]), ([db], [o_s])], us=12)
+        tied = after(dz_a, d_s)
         d_s = split_off(d_s, "tensor")
-        dy, do, sums_y = temporal_pull(tied, t_all)
-        d_s = added(d_s, dy).astype(BF)
-        tied = after(dy, d_s, *back[3:], *d_m[3:])
+        dy_a, do_a, sums_y = temporal_pull(tied, t_all)
+        dy_b, do_b, sums_yb = temporal_pull(after(dz_b, dy_a), t_all)
+        d_s = added(d_s, dy_b).astype(BF)
+        tied = after(dy_b, d_s, *back[3:])
         d_s = split_off(by_shard(d_s), "shard")
-        d_r = share * grads_of([(tied, o_t), (y, dz)], us=6)
-        d_m = added(d_m, d_r).astype(BF)
-        tied = after(do, d_m, d_r)
-        d_m = lax.all_to_all(d_m, "context", split_axis=0, concat_axis=0, tiled=True)
+        d_r = share * grads_of([([dy_a, tied], [o_a, o_b]), ([y_a, y_b], [dz_a, dz_b])], us=6)
+        tied = after(do_a, d_r)
         d_r = split_off(d_r, "tensor")
-        d_qkv_t, sums_q = temporal_backward(tied, qkv_t, probs, **sizes)
-        d_m = jnp.sum(after(d_m, d_qkv_t).astype(F32), axis=0)
-        d_s = added(d_s, d_qkv_t).astype(BF)
-        d_r = added(d_r, d_qkv_t).astype(BF)
-        tied = after(d_qkv_t, d_r, d_s, d_m)
+        d_qkv_a, sums_q = temporal_backward(tied, qkv_a, probs_a, **sizes)
+        d_s = added(d_s, d_qkv_a).astype(BF)
+        d_r = added(d_r, d_qkv_a).astype(BF)
+        tied = after(d_qkv_a, d_r, d_s)
+        d_s = split_off(d_s, "context")
+        into_a, sums_x = temporal_end(tied, x_a, g1_a, gain[0], t_all)
+        swap_a = by_place(into_a, first_places)
+        into_a = from_clips(swap_a)
+        tied = after(do_b, swap_a, d_r, d_m)
+        d_m = d_m.astype(F32)
         d_r = split_off(by_shard(d_r), "shard")
-        d_q = share * grads_of([(a_t, tied)], us=9)
-        d_r = added(d_r, d_q).astype(BF)
-        d_s = shed_at_once(d_s, "context", d_q)
-        tied, d_q, d_r, d_s = lax.optimization_barrier((d_qkv_t, d_q, d_r, d_s))
+        d_qkv_b, sums_qb = temporal_backward(tied, qkv_b, probs_b, **sizes)
+        d_s = added(d_s, d_qkv_b)
+        d_r = added(d_r, d_qkv_b).astype(BF)
+        tied = after(d_qkv_b, d_r, d_s)
+        d_q = share * grads_of([([at_a, at_b], [d_qkv_a, tied])], us=9)
+        tied, d_q = lax.optimization_barrier((d_qkv_b, d_q, into_a))[:2]
         d_q = split_off(d_q, "tensor")
-        d_r = split_off(d_r, "context")
-        into, sums_x = temporal_end(tied, x, g1, gain[0], t_all)
-        d_r = added(d_r, into)
-        swapped = after(by_place(into), d_r)
-        into = from_clips(swapped)
-        output = sent_back([after(piece, swapped) for piece in back])
-        small = share * jnp.concatenate(
-            (sums_m, sums_s, sums_y + sums_q + sums_x, d_hidden.reshape(-1, width)), axis=0
-        )
-        d_q = added(d_q, swapped).astype(BF)
-        small = plus_others(small, "tensor")
-        d_q = added(split_off(by_shard(after(d_q, small)), "shard")).astype(BF)
-        small = plus_others(after(small, d_q), "shard")
-        d_q = shed(after(d_q, small), "context")
-        small = plus_others(small, "context")
-        return output, into, (d_q, d_r, d_s, d_m, small)
-
-    parts = [one_clip(rows_in[:, i], pulled[:, i], keep[i]) for i in range(clips)]
+        into_b, sums_xb = temporal_end(tied, x_b, g1_b, gain[0], t_all)
+        swap_b = by_place(into_b, places - first_places)
+        into_b = from_clips(after(swap_b, into_a))
+        t, m = sums_y + sums_yb + sums_q + sums_qb + sums_x + sums_xb, sums_m
+        rows = [v[n : n + 1] for n in (0, 1) for v in (t, sums_s, m)] + [t[2:4], sums_s[2:4]]
+        rows = rows + [t[4:5], m[3:4], m[2:3], sums_s[4:5], d_hidden.reshape(-1, width)]
+        small = plus_others(share * jnp.concatenate(rows, axis=0), "tensor")
+        d_q = added(d_q, swap_b).astype(BF)
+        small = plus_others(small, "shard")
+        d_q = added(split_off(by_shard(d_q), "shard"), small).astype(BF)
+        output = sent_back([after(piece, d_q) for piece in back])
+        small = plus_others(after(small, d_q), "context")
+        d_q = shed(jnp.concatenate((d_r, d_q), axis=-1), "context")
+        into = jnp.swapaxes(jnp.concatenate((into_a, after(into_b, output)), axis=1), 1, 2)
+        return output, into, (d_q, d_s, d_m, small)
+
+    given = (rows_a, rows_b, pull_a, pull_b)
+    parts = [one_clip(*[v[:, i] for v in given], keep[i]) for i in range(clips)]
     output, input_grad = [
         jnp.stack([part[n] for part in parts], axis=1).reshape(clips_in.shape) for n in (0, 1)
     ]
     grads = parts[0][2]
     for part in parts[1:]:
         grads = jax.tree.map(jnp.add, grads, part[2])
-    d_t_qkv, d_t_rest, d_s, d_mlp, small = grads
-    m, s, t = small[0:8], small[8:16], small[16:24]
+    d_t, d_s, d_mlp, small = grads
+    d_t_rest, d_t_qkv = d_t[:, : 2 * width], d_t[:, 2 * width :]
     return (
         output,
         input_grad,
-        jnp.stack((t[0], s[0], m[0])),
-        jnp.stack((t[1], s[1], m[1])),
+        small[0:3],
+        small[3:6],
         d_t_qkv.reshape(own_rows, 3, width),
         d_t_rest[:, :width],
         d_t_rest[:, width:],
@@ -724,10 +777,10 @@
         d_s[:, 3 * width :],
         d_mlp[:in_rows],
         d_mlp[in_rows:],
-        jnp.stack((t[2:4], s[2:4])),
-        jnp.stack((t[4], m[3], m[2])),
-        s[4],
-        small[24:].reshape(-1),
+        small[6:10].reshape(2, 2, width),
+        small[10:13],
+        small[13],
+        small[14:].reshape(-1),
     )
 
 

time: 655 us -> 627 us (0.957)
  waiting for transfers between devices: 146 us -> 107 us
  Pallas kernels: 289 us -> 305 us
  starting transfers between devices: 92.8 us -> 82.3 us
  local copies, waits for them, and re-layouts: 53 us -> 62.7 us
  other arithmetic: 55.7 us -> 47.7 us
    all_to_all x2 -> x4, waiting for transfers between devices: 62.6 us -> 26.6 us  [to_clips(): lax.all_to_all(array, 'context', split_axis=0, concat_axis=0, tiled=True)]
    ppermute x43 -> x39, starting transfers between devices: 66.8 us -> 51.8 us  [exchange(): lax.ppermute(pieces[d], axis, [(i, i ^ d) for i in range(size)])]
    slice x6 -> x17, local copies, waits for them, and re-layouts: 3.83 us -> 16.4 us  [the longest x2 5.22 us: local(): clip_parts = [clips_in[:, :, cut] for cut in cuts]]
    convert_element_type x8 -> x6, other arithmetic: 20.1 us -> 10.4 us  [the longest x1 3.26 us: one_clip(): d_s = added(d_s, dy_b).astype(BF)]
    all_to_all x2 -> x4, starting transfers between devices: 13.4 us -> 22.8 us  [to_clips(): lax.all_to_all(array, 'context', split_axis=0, concat_axis=0, tiled=True)]
    all_to_all x2 -> x0, starting transfers between devices: 8.88 us -> none  [the longest x1 5.18 us: shed_at_once(): lax.all_to_all(array.astype(BF), axis, split_axis=0, concat_axis=0, tiled...]
    pallas_call x7 -> x9, Pallas kernels: 159 us -> 167 us  [the longest x1 75.2 us: mlp(): pl.pallas_call(partial(mlp_kernel, rb=rb, chunks=chunks, frames=frames),...]
    squeeze x10 -> x7, local copies, waits for them, and re-layouts: 16.4 us -> 9.8 us  [split_off(): lax.dynamic_index_in_dim(array, place ^ d, 0, keepdims=False)]
  transfers between devices with their start and end apart: 49 -> 47, of which waited for: 19 -> 15; matrix products, arithmetic and copies ran while one was open for 13% -> 15% of each run, Pallas kernels for 29% -> 37%
where the time goes in v2:
time: 627 us; the launch traced here: 621 us
  Pallas kernels  305 us (49%)
  waiting for transfers between devices  107 us (17%)
  starting transfers between devices  82.3 us (13%)
  local copies, waits for them, and re-layouts  62.7 us (10%)
  other arithmetic  47.7 us (8%)
  between operations  15.6 us (2%)
    ppermute x39, waiting for transfers between devices, exchange(): lax.ppermute(pieces[d], axis, [(i, i ^ d) for i in range(size)])  80.5 us
    pallas_call x1, Pallas kernels, mlp(): pl.pallas_call(partial(mlp_kernel, rb=rb, chunks=chunks, frames=frames),...  75.2 us
    ppermute x39, starting transfers between devices, exchange(): lax.ppermute(pieces[d], axis, [(i, i ^ d) for i in range(size)])  51.8 us
    pallas_call x2, Pallas kernels, spatial_backward(): pl.pallas_call(partial(sb_kernel, fb=fb, real=real, head=head, scale=scal...  49.3 us
    pallas_call x2, Pallas kernels, temporal_forward(): call(partial(tf_kernel, fb=fb, nb=nb, frames=frames, slot=LANES // frames...  48 us
    pallas_call x2, Pallas kernels, temporal_backward(): call(partial(tb_kernel, fb=fb, nb=nb, frames=frames, slot=LANES // frames...  40.6 us
    pallas_call x3, Pallas kernels, weight_grads(): call(partial(wg_kernel, starts=starts, counts=counts, halves=halves, rows...  38.8 us
    all_to_all x4, waiting for transfers between devices, to_clips(): lax.all_to_all(array, 'context', split_axis=0, concat_axis=0, tiled=True)  26.6 us
  transfers between devices with their start and end apart: 47, of which 15 were waited for; matrix products, arithmetic and copies ran while one was open for 15% of the time, Pallas kernels for 37%

profile of v2, /device:TPU:0, one launch (start us, length us, event | category | flops | bytes accessed | tf_op | source)
XLA Modules:
  0.0 620.9 jit_solution(3691719954848493311)
XLA Ops:
  12.0 3.0 collective-permute-start.2
  15.1 2.6 collective-permute-start.1
  21.8 3.2 slice.135
  32.2 8.7 %collective-permute-done.1 = bf16[24,6912]{1,0:T(8,128)(2,1)S(1)} collective-permute-done((bf16[24,6912]{1,0:T(8,128)(2,1)S(1)}, bf16[24,6912]{1,0:T(8,128)(2,1)S(1)}, u32[]{:S(2)}, u32[]{:S(2)}) %collective-permute-start.1) | collective-permute-done | bytes 331808 | tf_op jit(solution)/shard_map/ppermute | solution.py:500
  42.2 8.6 %all-to-all-start = ((bf16[4,96,2,768]{3,2,1,0:T(2,128)(2,1)}), bf16[4,96,2,768]{3,2,1,0:T(2,128)(2,1)S(1)}, u32[]{:S(2)}, u32[]{:S(2)}) async-start(bf16[4,96,2,768]{3,2,1,0:T(2,128)(2,1)} %bitcast.210), calls=%async_computation | async-start | bytes 2359296 | tf_op jit(solution)/shard_map/all_to_all | solution.py:620
  55.2 18.3 %collective-permute-done.5 = bf16[4,24,3840]{2,1,0:T(8,128)(2,1)S(1)} collective-permute-done((bf16[4,24,3840]{2,1,0:T(8,128)(2,1)}, bf16[4,24,3840]{2,1,0:T(8,128)(2,1)S(1)}, u32[]{:S(2)}, u32[]{:S(2)}) %collective-permute-start.5) | collective-permute-done | bytes 737312 | tf_op jit(solution)/shard_map/ppermute | solution.py:500
  73.5 11.1 %all-to-all-done = bf16[4,96,2,768]{3,2,1,0:T(2,128)(2,1)S(1)} async-done(((bf16[4,96,2,768]{3,2,1,0:T(2,128)(2,1)}), bf16[4,96,2,768]{3,2,1,0:T(2,128)(2,1)S(1)}, u32[]{:S(2)}, u32[]{:S(2)}) %all-to-all-start) | async-done | bytes 1179680 | tf_op jit(solution)/shard_map/all_to_all | solution.py:620
  84.6 4.7 collective-permute-done.4
  97.8 5.1 all-to-all-start.1
  108.1 2.9 copy.46
  111.1 22.6 %shard_map.271 = (bf16[768,768]{1,0:T(8,128)(2,1)}, bf16[768,2304]{1,0:T(8,128)(2,1)}, f32[768,128]{1,0:T(8,128)}, bf16[768,768]{1,0:T(8,128)(2,1)}, bf16[768,768]{1,0:T(8,128)(2,1)}, /*index=5*/f32[768,768]{1,0:T(8,128)}) custom-call(bf16[768,768]{1,0:T(8,128)(2,1)} %bitcast.224, f32[1,768]{1,0:T(1,128)} %get-tuple-element.297.gain_ref, ...), custom_call_target="tpu_custom_call" | custom-call | flops 22000001024 | tf_op jit(solution)/shard_map/pallas_call | solution.py:352
  134.5 3.2 collective-permute-done.7
  142.5 15.6 %all-to-all-done.1 = bf16[4,100,2,768]{3,2,1,0:T(2,128)(2,1)} async-done(((bf16[4,100,2,768]{3,2,1,0:T(2,128)(2,1)}), bf16[4,100,2,768]{3,2,1,0:T(2,128)(2,1)}, u32[]{:S(2)}, u32[]{:S(2)}) %all-to-all-start.1) | async-done | bytes 1228832 | tf_op jit(solution)/shard_map/all_to_all | solution.py:620
  158.1 4.0 all-to-all-start.2
  164.7 25.4 %shard_map.272 = (bf16[896,768]{1,0:T(8,128)(2,1)}, bf16[896,2304]{1,0:T(8,128)(2,1)}, f32[896,128]{1,0:T(8,128)}, bf16[896,768]{1,0:T(8,128)(2,1)}, bf16[896,768]{1,0:T(8,128)(2,1)}, /*index=5*/f32[896,768]{1,0:T(8,128)}) custom-call(bf16[896,768]{1,0:T(8,128)(2,1)} %bitcast.220, f32[1,768]{1,0:T(1,128)} %get-tuple-element.297.gain_ref, ...), custom_call_target="tpu_custom_call" | custom-call | flops 22000001024 | tf_op jit(solution)/shard_map/pallas_call | solution.py:352
  190.1 5.1 all-to-all-start.3
  198.6 2.6 copy.48
  201.2 25.5 %shard_map.273 = (bf16[1664,768]{1,0:T(8,128)(2,1)}, bf16[1664,2304]{1,0:T(8,128)(2,1)}, bf16[1664,768]{1,0:T(8,128)(2,1)}, f32[1664,768]{1,0:T(8,128)}, f32[1664,768]{1,0:T(8,128)}) custom-call(f32[768,768]{1,0:T(8,128)} %get-tuple-element.122.xa_ref, f32[896,768]{1,0:T(8,128)} %get-tuple-element.131.xb_ref, f32[1,768]{1,0:T(1,128)} %get-tuple-element.298.gain_ref, ...), custom_call_target="tpu_custom_call" | custom-call | flops 30000001024 | tf_op jit(solution)/shard_map/pallas_call | solution.py:207
  229.3 75.2 %shard_map.274 = (bf16[1664,768]{1,0:T(8,128)(2,1)}, f32[1664,768]{1,0:T(8,128)}, bf16[1664,768]{1,0:T(8,128)(2,1)}, bf16[16,2,96,1536]{3,2,1,0:T(8,128)(2,1)}, f32[1,3072]{1,0:T(1,128)}, /*index=5*/f32[8,768]{1,0:T(8,128)}) custom-call(f32[1664,768]{1,0:T(8,128)} %get-tuple-element.133.x_ref, bf16[768,768]{1,0:T(8,128)(2,1)} %bitcast.226, ...), custom_call_target="tpu_custom_call" | custom-call | flops 74999996416 | tf_op jit(solution)/shard_map/pallas_call | solution.py:114
  312.7 24.5 %shard_map.275 = (bf16[1664,2304]{1,0:T(8,128)(2,1)}, f32[768,768]{1,0:T(8,128)}, f32[896,768]{1,0:T(8,128)}, bf16[768,768]{1,0:T(8,128)(2,1)}, bf16[896,768]{1,0:T(8,128)(2,1)}, /*index=5*/f32[8,768]{1,0:T(8,128)}) custom-call(f32[1664,768]{1,0:T(8,128)} %get-tuple-element.137.g2_ref, bf16[1664,768]{1,0:T(8,128)(2,1)} %get-tuple-element.142.db_ref.refs_1_, ...), custom_call_target="tpu_custom_call" | custom-call | flops 24000000000 | tf_op jit(solution)/shard_map/pallas_call | solution.py:272
  337.3 24.7 %shard_map.276 = (bf16[1664,2304]{1,0:T(8,128)(2,1)}, f32[768,768]{1,0:T(8,128)}, f32[896,768]{1,0:T(8,128)}, bf16[768,768]{1,0:T(8,128)(2,1)}, bf16[896,768]{1,0:T(8,128)(2,1)}, /*index=5*/f32[8,768]{1,0:T(8,128)}) custom-call(f32[1664,768]{1,0:T(8,128)} %get-tuple-element.137.g2_ref,, ...), custom_call_target="tpu_custom_call", output_to_operand_aliasing={{0}: (7, {}), {1}: (8, {}), {2}: (9, {}), {3}: (10, {}), {4... | custom-call | flops 24000000000 | tf_op jit(solution)/shard_map/pallas_call | solution.py:272
  362.1 16.1 %shard_map.277 = bf16[2,384,3072]{2,1,0:T(8,128)(2,1)} custom-call(bf16[1664,768]{1,0:T(8,128)(2,1)} %get-tuple-element.149.refs_0_, bf16[1664,768]{1,0:T(8,128)(2,1)} %get-tuple-element.142.db_ref.refs_1_, bf16[1664,2304]{1,0:T(8,128)(2,1)} %get-tuple-element.151.refs_2_, bf16[1664,768]{1,0:T(8,128)(2,1)} %get-tuple-element.152.refs_3_), custom_call_target="tpu_custom_call" | custom-call | flops 12000000000 | tf_op jit(solution)/shard_map/pallas_call | solution.py:486
  378.2 3.3 dynamic-slice_bitcast_fusion
  383.3 5.2 shard_map.278
  388.5 5.7 shard_map.279
  395.6 3.3 fusion
  401.4 11.4 %shard_map.280 = bf16[2,384,1536]{2,1,0:T(8,128)(2,1)} custom-call(bf16[768,768]{1,0:T(8,128)(2,1)} %get-tuple-element.154.refs_0_, bf16[896,768]{1,0:T(8,128)(2,1)} %get-tuple-element.160.refs_1_, bf16[768,768]{1,0:T(8,128)(2,1)} %get-tuple-element.161.refs_2_, bf16[896,768]{1,0:T(8,128)(2,1)} %get-tuple-element.162.refs_3_, ...), custom_call_target="tpu_custom_call" | custom-call | flops 6000000000 | tf_op jit(solution)/shard_map/pallas_call | solution.py:486
  419.1 18.8 %shard_map.281 = (bf16[768,2304]{1,0:T(8,128)(2,1)}, f32[8,768]{1,0:T(8,128)}) custom-call(bf16[768,768]{1,0:T(8,128)(2,1)} %get-tuple-element.165.do_ref, bf16[768,2304]{1,0:T(8,128)(2,1)} %get-tuple-element.166.qkv_ref, f32[768,128]{1,0:T(8,128)} %get-tuple-element.167.p_ref), custom_call_target="tpu_custom_call" | custom-call | flops 20000000000 | tf_op jit(solution)/shard_map/pallas_call | solution.py:429
  437.8 11.7 %collective-permute-done.18 = bf16[4,24,3072]{2,1,0:T(8,128)(2,1)} collective-permute-done((bf16[4,24,3072]{2,1,0:T(8,128)(2,1)}, bf16[4,24,3072]{2,1,0:T(8,128)(2,1)}, u32[]{:S(2)}, u32[]{:S(2)}) %collective-permute-start.18) | collective-permute-done | bytes 589856 | tf_op jit(solution)/shard_map/ppermute | solution.py:500
  449.5 3.9 collective-permute-done.17
  455.9 5.7 collective-permute-start.22
  468.3 8.1 %shard_map.282 = (bf16[768,768]{1,0:T(8,128)(2,1)}, f32[8,768]{1,0:T(8,128)}) custom-call(bf16[768,2304]{1,0:T(8,128)(2,1)} %get-tuple-element.173.dqkv_ref.refs_2_, bf16[768,768]{1,0:T(8,128)(2,1)} %bitcast.225, f32[768,768]{1,0:T(8,128)} %get-tuple-element.174.g1_ref, f32[1,768]{1,0:T(1,128)} %get-tuple-element.297.gain_ref, bf16[768,3840]{1,0:T(8,128)(2,1)} %bitcast.195), custom_call_target="tpu_custom_call" | custom-call | flops 7000000000 | tf_op jit(solution)/shard_map/pallas_call | solution.py:444
  476.3 3.5 copy.75
  479.9 4.1 all-to-all-start.4
  484.0 21.8 %shard_map.283 = (bf16[896,2304]{1,0:T(8,128)(2,1)}, f32[8,768]{1,0:T(8,128)}) custom-call(bf16[896,768]{1,0:T(8,128)(2,1)} %get-tuple-element.177.do_ref, bf16[896,2304]{1,0:T(8,128)(2,1)} %get-tuple-element.178.qkv_ref, f32[896,128]{1,0:T(8,128)} %get-tuple-element.179.p_ref), custom_call_target="tpu_custom_call" | custom-call | flops 20000000000 | tf_op jit(solution)/shard_map/pallas_call | solution.py:429
  505.8 3.0 collective-permute-start.23
  510.1 6.6 %collective-permute-done.23 = bf16[24,3072]{1,0:T(8,128)(2,1)S(1)} collective-permute-done((bf16[24,3072]{1,0:T(8,128)(2,1)S(1)}, bf16[24,3072]{1,0:T(8,128)(2,1)S(1)}, u32[]{:S(2)}, u32[]{:S(2)}) %collective-permute-start.23) | collective-permute-done | bytes 147488 | tf_op jit(solution)/shard_map/ppermute | solution.py:500
  517.7 11.2 %shard_map.284 = bf16[2,384,2304]{2,1,0:T(8,128)(2,1)} custom-call(bf16[768,768]{1,0:T(8,128)(2,1)} %get-tuple-element.181.refs_0_, bf16[896,768]{1,0:T(8,128)(2,1)} %get-tuple-element.182.refs_1_, bf16[768,2304]{1,0:T(8,128)(2,1)} %get-tuple-element.173.dqkv_ref.refs_2_, bf16[896,2304]{1,0:T(8,128)(2,1)} %get-tuple-element.191.refs_3_.dqkv_ref), custom_call_target="tpu_custom_call" | custom-call | flops 8999999488 | tf_op jit(solution)/shard_map/pallas_call | solution.py:486
  529.0 2.8 dynamic-slice_bitcast_fusion.1
  533.2 9.1 %shard_map.285 = (bf16[896,768]{1,0:T(8,128)(2,1)}, f32[8,768]{1,0:T(8,128)}) custom-call(bf16[896,2304]{1,0:T(8,128)(2,1)} %get-tuple-element.191.refs_3_.dqkv_ref, bf16[896,768]{1,0:T(8,128)(2,1)} %bitcast.221, f32[896,768]{1,0:T(8,128)} %get-tuple-element.192.g1_ref, f32[1,768]{1,0:T(1,128)} %get-tuple-element.297.gain_ref, bf16[768,3840]{1,0:T(8,128)(2,1)} %bitcast.196), custom_call_target="tpu_custom_call" | custom-call | flops 7000000000 | tf_op jit(solution)/shard_map/pallas_call | solution.py:444
  549.2 3.5 all-to-all-start.5
  564.1 8.0 %collective-permute-done.26 = bf16[4,24,2304]{2,1,0:T(8,128)(2,1)S(1)} collective-permute-done((bf16[4,24,2304]{2,1,0:T(8,128)(2,1)S(1)}, bf16[4,24,2304]{2,1,0:T(8,128)(2,1)S(1)}, u32[]{:S(2)}, u32[]{:S(2)}) %collective-permute-start.26) | collective-permute-done | bytes 442400 | tf_op jit(solution)/shard_map/ppermute | solution.py:500
  572.1 7.6 %collective-permute-done.32 = bf16[4,24,2304]{2,1,0:T(8,128)(2,1)S(1)} collective-permute-done((bf16[4,24,2304]{2,1,0:T(8,128)(2,1)S(1)}, bf16[4,24,2304]{2,1,0:T(8,128)(2,1)S(1)}, u32[]{:S(2)}, u32[]{:S(2)}) %collective-permute-start.32) | collective-permute-done | bytes 442400 | tf_op jit(solution)/shard_map/ppermute | solution.py:500
  581.3 3.6 collective-permute-start.35
  589.1 6.1 maximum_bitcast_fusion
  596.3 2.9 collective-permute-start.37
  599.3 4.5 maximum_bitcast_fusion.1
  608.6 2.8 collective-permute-done.38
  (224 shorter events, 114.4 us)
Async XLA Ops:
  7.2 222.1 %all-gather.2.cloned.1.call-start = ((), (), s32[]{:S(2)}) async-start(), calls=%async_computation.7 | async-start | bytes 9732096 | tf_op jit(solution)/shard_map/all_gather | solution.py:674
  12.0 20.2 %collective-permute-start.2 = (bf16[24,6912]{1,0:T(8,128)(2,1)S(1)}, bf16[24,6912]{1,0:T(8,128)(2,1)S(1)}, u32[]{:S(2)}, u32[]{:S(2)}) collective-permute-start(bf16[24,6912]{1,0:T(8,128)(2,1)S(1)} %convert_dynamic-update-slice_fusion), channel_id=1, source_target_pairs={{0,2},{2,0},{4,6},{6,4},{1,3},{3,1},{5,7},{7,5},{8,10},{10,8},{12,... | collective-permute-start | bytes 995336 | tf_op jit(solution)/shard_map/ppermute | solution.py:500
  15.1 25.8 %collective-permute-start.1 = (bf16[24,6912]{1,0:T(8,128)(2,1)S(1)}, bf16[24,6912]{1,0:T(8,128)(2,1)S(1)}, u32[]{:S(2)}, u32[]{:S(2)}) collective-permute-start(bf16[24,6912]{1,0:T(8,128)(2,1)S(1)} %convert_dynamic-update-slice_fusion), channel_id=1, source_target_pairs={{0,4},{2,6},{4,0},{6,2},{1,5},{3,7},{5,1},{7,3},{8,12},{10,14},{12... | collective-permute-start | bytes 995336 | tf_op jit(solution)/shard_map/ppermute | solution.py:500
  17.6 23.3 %collective-permute-start = (bf16[24,6912]{1,0:T(8,128)(2,1)S(1)}, bf16[24,6912]{1,0:T(8,128)(2,1)}, u32[]{:S(2)}, u32[]{:S(2)}) collective-permute-start(bf16[24,6912]{1,0:T(8,128)(2,1)S(1)} %convert_dynamic-update-slice_fusion), channel_id=1, source_target_pairs={{0,6},{2,4},{4,2},{6,0},{1,7},{3,5},{5,3},{7,1},{8,14},{10,12},{12... | collective-permute-start | bytes 995336 | tf_op jit(solution)/shard_map/ppermute | solution.py:500
  42.2 42.4 %all-to-all-start = ((bf16[4,96,2,768]{3,2,1,0:T(2,128)(2,1)}), bf16[4,96,2,768]{3,2,1,0:T(2,128)(2,1)S(1)}, u32[]{:S(2)}, u32[]{:S(2)}) async-start(bf16[4,96,2,768]{3,2,1,0:T(2,128)(2,1)} %bitcast.210), calls=%async_computation | async-start | bytes 2359296 | tf_op jit(solution)/shard_map/all_to_all | solution.py:620
  51.8 21.7 %collective-permute-start.5 = (bf16[4,24,3840]{2,1,0:T(8,128)(2,1)}, bf16[4,24,3840]{2,1,0:T(8,128)(2,1)S(1)}, u32[]{:S(2)}, u32[]{:S(2)}) collective-permute-start(bf16[4,24,3840]{2,1,0:T(8,128)(2,1)} %slice.179), channel_id=1, source_target_pairs={{0,8},{8,0},{16,24},{24,16},{1,9},{9,1},{17,25},{25,17},{2,10},{10... | collective-permute-start | bytes 2211848 | tf_op jit(solution)/shard_map/ppermute | solution.py:500
  53.2 36.0 %collective-permute-start.4 = (bf16[4,24,3840]{2,1,0:T(8,128)(2,1)}, bf16[4,24,3840]{2,1,0:T(8,128)(2,1)}, u32[]{:S(2)}, u32[]{:S(2)}) collective-permute-start(bf16[4,24,3840]{2,1,0:T(8,128)(2,1)} %slice.179), channel_id=1, source_target_pairs={{0,16},{8,24},{16,0},{24,8},{1,17},{9,25},{17,1},{25,9},{2,18},{10... | collective-permute-start | bytes 2211848 | tf_op jit(solution)/shard_map/ppermute | solution.py:500
  54.8 34.5 %collective-permute-start.3 = (bf16[4,24,3840]{2,1,0:T(8,128)(2,1)}, bf16[4,24,3840]{2,1,0:T(8,128)(2,1)}, u32[]{:S(2)}, u32[]{:S(2)}) collective-permute-start(bf16[4,24,3840]{2,1,0:T(8,128)(2,1)} %slice.179), channel_id=1, source_target_pairs={{0,24},{8,16},{16,8},{24,0},{1,25},{9,17},{17,9},{25,1},{2,26},{10... | collective-permute-start | bytes 2211848 | tf_op jit(solution)/shard_map/ppermute | solution.py:500
  92.9 12.4 %collective-permute-start.6 = (bf16[4,4,24,3840]{3,2,1,0:T(8,128)(2,1)}, bf16[4,4,24,3840]{3,2,1,0:T(8,128)(2,1)}, u32[]{:S(2)}, u32[]{:S(2)}) collective-permute-start(bf16[4,4,24,3840]{3,2,1,0:T(8,128)(2,1)} %pad_maximum_fusion.2), channel_id=1, source_target_pairs={{0,1},{1,0},{2,3},{3,2},{4,5},{5,4},{6,7},{7,6},{8,9},{9,8},{10,11... | collective-permute-start | bytes 8847368 | tf_op jit(solution)/shard_map/ppermute | solution.py:500
  93.8 39.9 %collective-permute-start.9 = (bf16[4,24,3072]{2,1,0:T(8,128)(2,1)}, bf16[4,24,3072]{2,1,0:T(8,128)(2,1)S(1)}, u32[]{:S(2)}, u32[]{:S(2)}) collective-permute-start(bf16[4,24,3072]{2,1,0:T(8,128)(2,1)} %slice.180), channel_id=1, source_target_pairs={{0,8},{8,0},{16,24},{24,16},{1,9},{9,1},{17,25},{25,17},{2,10},{10... | collective-permute-start | bytes 1769480 | tf_op jit(solution)/shard_map/ppermute | solution.py:500
  93.8 39.9 %collective-permute-start.8 = (bf16[4,24,3072]{2,1,0:T(8,128)(2,1)}, bf16[4,24,3072]{2,1,0:T(8,128)(2,1)}, u32[]{:S(2)}, u32[]{:S(2)}) collective-permute-start(bf16[4,24,3072]{2,1,0:T(8,128)(2,1)} %slice.180), channel_id=1, source_target_pairs={{0,16},{8,24},{16,0},{24,8},{1,17},{9,25},{17,1},{25,9},{2,18},{10... | collective-permute-start | bytes 1769480 | tf_op jit(solution)/shard_map/ppermute | solution.py:500
  96.3 41.5 %collective-permute-start.7 = (bf16[4,24,3072]{2,1,0:T(8,128)(2,1)}, bf16[4,24,3072]{2,1,0:T(8,128)(2,1)}, u32[]{:S(2)}, u32[]{:S(2)}) collective-permute-start(bf16[4,24,3072]{2,1,0:T(8,128)(2,1)} %slice.180), channel_id=1, source_target_pairs={{0,24},{8,16},{16,8},{24,0},{1,25},{9,17},{17,9},{25,1},{2,26},{10... | collective-permute-start | bytes 1769480 | tf_op jit(solution)/shard_map/ppermute | solution.py:500
  97.8 60.3 %all-to-all-start.1 = ((bf16[4,100,2,768]{3,2,1,0:T(2,128)(2,1)}), bf16[4,100,2,768]{3,2,1,0:T(2,128)(2,1)}, u32[]{:S(2)}, u32[]{:S(2)}) async-start(bf16[4,100,2,768]{3,2,1,0:T(2,128)(2,1)} %bitcast.200), calls=%async_computation.1 | async-start | bytes 2457600 | tf_op jit(solution)/shard_map/all_to_all | solution.py:620
  141.3 55.0 %collective-permute-start.10 = (bf16[4,4,24,3072]{3,2,1,0:T(8,128)(2,1)}, bf16[4,4,24,3072]{3,2,1,0:T(8,128)(2,1)}, u32[]{:S(2)}, u32[]{:S(2)}) collective-permute-start(bf16[4,4,24,3072]{3,2,1,0:T(8,128)(2,1)} %pad_maximum_fusion.3), channel_id=1, source_target_pairs={{0,1},{1,0},{2,3},{3,2},{4,5},{5,4},{6,7},{7,6},{8,9},{9,8},{10,11... | collective-permute-start | bytes 7077896 | tf_op jit(solution)/shard_map/ppermute | solution.py:500
  158.1 32.0 %all-to-all-start.2 = ((bf16[4,96,2,768]{3,2,1,0:T(2,128)(2,1)}), bf16[4,96,2,768]{3,2,1,0:T(2,128)(2,1)S(1)}, u32[]{:S(2)}, u32[]{:S(2)}) async-start(bf16[4,96,2,768]{3,2,1,0:T(2,128)(2,1)} %bitcast.26), calls=%async_computation.2 | async-start | bytes 2359296 | tf_op jit(solution)/shard_map/all_to_all | solution.py:620
  190.1 36.6 %all-to-all-start.3 = ((bf16[4,100,2,768]{3,2,1,0:T(2,128)(2,1)}), bf16[4,100,2,768]{3,2,1,0:T(2,128)(2,1)}, u32[]{:S(2)}, u32[]{:S(2)}) async-start(bf16[4,100,2,768]{3,2,1,0:T(2,128)(2,1)} %bitcast.199), calls=%async_computation.3 | async-start | bytes 2457600 | tf_op jit(solution)/shard_map/all_to_all | solution.py:620
  195.2 288.8 %reduce-scatter.2.cloned.1.call-start = ((), (), s32[]{:S(2)}) async-start(), calls=%async_computation.8 | async-start | bytes 9732096 | tf_op jit(solution)/shard_map/reduce_scatter | solution.py:706
  308.3 29.0 %collective-permute-start.12 = (bf16[196,2,768]{2,1,0:T(2,128)(2,1)S(1)}, bf16[196,2,768]{2,1,0:T(2,128)(2,1)S(1)}, u32[]{:S(2)}, u32[]{:S(2)}) collective-permute-start(bf16[196,2,768]{2,1,0:T(2,128)(2,1)S(1)} %bitcast.231), channel_id=1, source_target_pairs={{0,2},{2,0},{4,6},{6,4},{1,3},{3,1},{5,7},{7,5},{8,10},{10,8},{12,... | collective-permute-start | bytes 1806344 | tf_op jit(solution)/shard_map/ppermute | solution.py:500
  310.4 51.7 %collective-permute-start.13 = (bf16[196,2,768]{2,1,0:T(2,128)(2,1)S(1)}, bf16[196,2,768]{2,1,0:T(2,128)(2,1)S(1)}, u32[]{:S(2)}, u32[]{:S(2)}) collective-permute-start(bf16[196,2,768]{2,1,0:T(2,128)(2,1)S(1)} %bitcast.230), channel_id=1, source_target_pairs={{0,4},{2,6},{4,0},{6,2},{1,5},{3,7},{5,1},{7,3},{8,12},{10,14},{12... | collective-permute-start | bytes 1806344 | tf_op jit(solution)/shard_map/ppermute | solution.py:500
  381.4 12.8 %collective-permute-start.14 = (bf16[16,24,3072]{2,1,0:T(8,128)(2,1)}, bf16[16,24,3072]{2,1,0:T(8,128)(2,1)S(1)}, u32[]{:S(2)}, u32[]{:S(2)}) collective-permute-start(bf16[16,24,3072]{2,1,0:T(8,128)(2,1)} %dynamic-slice_bitcast_fusion), channel_id=1, source_target_pairs={{0,1},{1,0},{2,3},{3,2},{4,5},{5,4},{6,7},{7,6},{8,9},{9,8},{10,11... | collective-permute-start | bytes 7077896 | tf_op jit(solution)/shard_map/ppermute | solution.py:500
  382.7 18.7 %collective-permute-start.11 = (bf16[196,2,768]{2,1,0:T(2,128)(2,1)}, bf16[196,2,768]{2,1,0:T(2,128)(2,1)S(1)}, u32[]{:S(2)}, u32[]{:S(2)}) collective-permute-start(bf16[196,2,768]{2,1,0:T(2,128)(2,1)} %bitcast.177), channel_id=1, source_target_pairs={{0,6},{2,4},{4,2},{6,0},{1,7},{3,5},{5,3},{7,1},{8,14},{10,12},{12... | collective-permute-start | bytes 1806344 | tf_op jit(solution)/shard_map/ppermute | solution.py:500
  414.2 48.8 %collective-permute-start.15 = (bf16[16,24,1536]{2,1,0:T(8,128)(2,1)S(1)}, bf16[16,24,1536]{2,1,0:T(8,128)(2,1)}, u32[]{:S(2)}, u32[]{:S(2)}) collective-permute-start(bf16[16,24,1536]{2,1,0:T(8,128)(2,1)S(1)} %dynamic-slice_bitcast_fusion.2), channel_id=1, source_target_pairs={{0,1},{1,0},{2,3},{3,2},{4,5},{5,4},{6,7},{7,6},{8,9},{9,8},{10,11... | collective-permute-start | bytes 3538952 | tf_op jit(solution)/shard_map/ppermute | solution.py:500
  415.6 22.3 %collective-permute-start.16 = (bf16[4,24,3072]{2,1,0:T(8,128)(2,1)}, bf16[4,24,3072]{2,1,0:T(8,128)(2,1)S(1)}, u32[]{:S(2)}, u32[]{:S(2)}) collective-permute-start(bf16[4,24,3072]{2,1,0:T(8,128)(2,1)} %get-tuple-element.246), channel_id=1, source_target_pairs={{0,8},{8,0},{16,24},{24,16},{1,9},{9,1},{17,25},{25,17},{2,10},{10... | collective-permute-start | bytes 1769480 | tf_op jit(solution)/shard_map/ppermute | solution.py:500
  417.2 32.4 %collective-permute-start.18 = (bf16[4,24,3072]{2,1,0:T(8,128)(2,1)}, bf16[4,24,3072]{2,1,0:T(8,128)(2,1)}, u32[]{:S(2)}, u32[]{:S(2)}) collective-permute-start(bf16[4,24,3072]{2,1,0:T(8,128)(2,1)} %get-tuple-element.247), channel_id=1, source_target_pairs={{0,24},{8,16},{16,8},{24,0},{1,25},{9,17},{17,9},{25,1},{2,26},{10... | collective-permute-start | bytes 1769480 | tf_op jit(solution)/shard_map/ppermute | solution.py:500
  418.5 34.8 %collective-permute-start.17 = (bf16[4,24,3072]{2,1,0:T(8,128)(2,1)}, bf16[4,24,3072]{2,1,0:T(8,128)(2,1)}, u32[]{:S(2)}, u32[]{:S(2)}) collective-permute-start(bf16[4,24,3072]{2,1,0:T(8,128)(2,1)} %get-tuple-element.248), channel_id=1, source_target_pairs={{0,16},{8,24},{16,0},{24,8},{1,17},{9,25},{17,1},{25,9},{2,18},{10... | collective-permute-start | bytes 1769480 | tf_op jit(solution)/shard_map/ppermute | solution.py:500
  437.8 25.2 %copy-start.8 = (bf16[2,384,1536]{2,1,0:T(8,128)(2,1)S(1)}, bf16[2,384,1536]{2,1,0:T(8,128)(2,1)}, u32[]{:S(2)}) copy-start(bf16[2,384,1536]{2,1,0:T(8,128)(2,1)} %shard_map.280) | copy-start | bytes 7077892
  455.9 54.2 %collective-permute-start.22 = (bf16[24,3072]{1,0:T(8,128)(2,1)}, bf16[24,3072]{1,0:T(8,128)(2,1)S(1)}, u32[]{:S(2)}, u32[]{:S(2)}) collective-permute-start(bf16[24,3072]{1,0:T(8,128)(2,1)} %get-tuple-element.266), channel_id=1, source_target_pairs={{0,2},{2,0},{4,6},{6,4},{1,3},{3,1},{5,7},{7,5},{8,10},{10,8},{12,... | collective-permute-start | bytes 442376 | tf_op jit(solution)/shard_map/ppermute | solution.py:500
  461.6 48.5 %collective-permute-start.24 = (bf16[24,3072]{1,0:T(8,128)(2,1)}, bf16[24,3072]{1,0:T(8,128)(2,1)}, u32[]{:S(2)}, u32[]{:S(2)}) collective-permute-start(bf16[24,3072]{1,0:T(8,128)(2,1)} %get-tuple-element.267), channel_id=1, source_target_pairs={{0,6},{2,4},{4,2},{6,0},{1,7},{3,5},{5,3},{7,1},{8,14},{10,12},{12... | collective-permute-start | bytes 442376 | tf_op jit(solution)/shard_map/ppermute | solution.py:500
  464.7 44.0 %collective-permute-start.19 = (bf16[4,24,1536]{2,1,0:T(8,128)(2,1)S(1)}, bf16[4,24,1536]{2,1,0:T(8,128)(2,1)}, u32[]{:S(2)}, u32[]{:S(2)}) collective-permute-start(bf16[4,24,1536]{2,1,0:T(8,128)(2,1)S(1)} %get-tuple-element.260), channel_id=1, source_target_pairs={{0,8},{8,0},{16,24},{24,16},{1,9},{9,1},{17,25},{25,17},{2,10},{10... | collective-permute-start | bytes 884744 | tf_op jit(solution)/shard_map/ppermute | solution.py:500
  466.4 39.4 %collective-permute-start.21 = (bf16[4,24,1536]{2,1,0:T(8,128)(2,1)S(1)}, bf16[4,24,1536]{2,1,0:T(8,128)(2,1)}, u32[]{:S(2)}, u32[]{:S(2)}) collective-permute-start(bf16[4,24,1536]{2,1,0:T(8,128)(2,1)S(1)} %get-tuple-element.261), channel_id=1, source_target_pairs={{0,24},{8,16},{16,8},{24,0},{1,25},{9,17},{17,9},{25,1},{2,26},{10... | collective-permute-start | bytes 884744 | tf_op jit(solution)/shard_map/ppermute | solution.py:500
  466.5 42.2 %collective-permute-start.20 = (bf16[4,24,1536]{2,1,0:T(8,128)(2,1)S(1)}, bf16[4,24,1536]{2,1,0:T(8,128)(2,1)}, u32[]{:S(2)}, u32[]{:S(2)}) collective-permute-start(bf16[4,24,1536]{2,1,0:T(8,128)(2,1)S(1)} %get-tuple-element.262), channel_id=1, source_target_pairs={{0,16},{8,24},{16,0},{24,8},{1,17},{9,25},{17,1},{25,9},{2,18},{10... | collective-permute-start | bytes 884744 | tf_op jit(solution)/shard_map/ppermute | solution.py:500
  479.9 49.1 %all-to-all-start.4 = ((bf16[4,96,2,768]{3,2,1,0:T(2,128)(2,1)}), bf16[4,96,2,768]{3,2,1,0:T(2,128)(2,1)S(1)}, u32[]{:S(2)}, u32[]{:S(2)}) async-start(bf16[4,96,2,768]{3,2,1,0:T(2,128)(2,1)} %bitcast.173), calls=%async_computation.5 | async-start | bytes 2359296 | tf_op jit(solution)/shard_map/all_to_all | solution.py:635
  505.8 10.9 %collective-permute-start.23 = (bf16[24,3072]{1,0:T(8,128)(2,1)S(1)}, bf16[24,3072]{1,0:T(8,128)(2,1)S(1)}, u32[]{:S(2)}, u32[]{:S(2)}) collective-permute-start(bf16[24,3072]{1,0:T(8,128)(2,1)S(1)} %copy-done.21), channel_id=1, source_target_pairs={{0,4},{2,6},{4,0},{6,2},{1,5},{3,7},{5,1},{7,3},{8,12},{10,14},{12... | collective-permute-start | bytes 442376 | tf_op jit(solution)/shard_map/ppermute | solution.py:500
  531.8 24.6 %collective-permute-start.25 = (bf16[16,24,2304]{2,1,0:T(8,128)(2,1)}, bf16[16,24,2304]{2,1,0:T(8,128)(2,1)}, u32[]{:S(2)}, u32[]{:S(2)}) collective-permute-start(bf16[16,24,2304]{2,1,0:T(8,128)(2,1)} %dynamic-slice_bitcast_fusion.1), channel_id=1, source_target_pairs={{0,1},{1,0},{2,3},{3,2},{4,5},{5,4},{6,7},{7,6},{8,9},{9,8},{10,11... | collective-permute-start | bytes 5308424 | tf_op jit(solution)/shard_map/ppermute | solution.py:500
  543.3 9.5 %collective-permute-start.27 = (f32[18,768]{1,0:T(8,128)S(1)}, f32[18,768]{1,0:T(8,128)S(1)}, u32[]{:S(2)}, u32[]{:S(2)}) collective-permute-start(f32[18,768]{1,0:T(8,128)S(1)} %concatenate.23), channel_id=1, source_target_pairs={{0,1},{1,0},{2,3},{3,2},{4,5},{5,4},{6,7},{7,6},{8,9},{9,8},{10,11... | collective-permute-start | bytes 165896 | tf_op jit(solution)/shard_map/ppermute | solution.py:500
  549.2 45.9 %all-to-all-start.5 = ((bf16[4,100,2,768]{3,2,1,0:T(2,128)(2,1)}), bf16[4,100,2,768]{3,2,1,0:T(2,128)(2,1)S(1)}, u32[]{:S(2)}, u32[]{:S(2)}) async-start(bf16[4,100,2,768]{3,2,1,0:T(2,128)(2,1)} %bitcast.172), calls=%async_computation.6 | async-start | bytes 2457600 | tf_op jit(solution)/shard_map/all_to_all | solution.py:635
  552.8 8.1 %collective-permute-start.30 = (f32[18,768]{1,0:T(8,128)S(1)}, f32[18,768]{1,0:T(8,128)S(1)}, u32[]{:S(2)}, u32[]{:S(2)}) collective-permute-start(f32[18,768]{1,0:T(8,128)S(1)} %add.218), channel_id=1, source_target_pairs={{0,24},{8,16},{16,8},{24,0},{1,25},{9,17},{17,9},{25,1},{2,26},{10... | collective-permute-start | bytes 165896 | tf_op jit(solution)/shard_map/ppermute | solution.py:500
  554.3 9.8 %collective-permute-start.29 = (f32[18,768]{1,0:T(8,128)S(1)}, f32[18,768]{1,0:T(8,128)S(1)}, u32[]{:S(2)}, u32[]{:S(2)}) collective-permute-start(f32[18,768]{1,0:T(8,128)S(1)} %add.218), channel_id=1, source_target_pairs={{0,16},{8,24},{16,0},{24,8},{1,17},{9,25},{17,1},{25,9},{2,18},{10... | collective-permute-start | bytes 165896 | tf_op jit(solution)/shard_map/ppermute | solution.py:500
  555.8 8.3 %collective-permute-start.28 = (f32[18,768]{1,0:T(8,128)S(1)}, f32[18,768]{1,0:T(8,128)S(1)}, u32[]{:S(2)}, u32[]{:S(2)}) collective-permute-start(f32[18,768]{1,0:T(8,128)S(1)} %add.218), channel_id=1, source_target_pairs={{0,8},{8,0},{16,24},{24,16},{1,9},{9,1},{17,25},{25,17},{2,10},{10... | collective-permute-start | bytes 165896 | tf_op jit(solution)/shard_map/ppermute | solution.py:500
  558.9 13.2 %collective-permute-start.26 = (bf16[4,24,2304]{2,1,0:T(8,128)(2,1)S(1)}, bf16[4,24,2304]{2,1,0:T(8,128)(2,1)S(1)}, u32[]{:S(2)}, u32[]{:S(2)}) collective-permute-start(bf16[4,24,2304]{2,1,0:T(8,128)(2,1)S(1)} %get-tuple-element.253), channel_id=1, source_target_pairs={{0,8},{8,0},{16,24},{24,16},{1,9},{9,1},{17,25},{25,17},{2,10},{10... | collective-permute-start | bytes 1327112 | tf_op jit(solution)/shard_map/ppermute | solution.py:500
  560.4 19.3 %collective-permute-start.32 = (bf16[4,24,2304]{2,1,0:T(8,128)(2,1)S(1)}, bf16[4,24,2304]{2,1,0:T(8,128)(2,1)S(1)}, u32[]{:S(2)}, u32[]{:S(2)}) collective-permute-start(bf16[4,24,2304]{2,1,0:T(8,128)(2,1)S(1)} %get-tuple-element.254), channel_id=1, source_target_pairs={{0,24},{8,16},{16,8},{24,0},{1,25},{9,17},{17,9},{25,1},{2,26},{10... | collective-permute-start | bytes 1327112 | tf_op jit(solution)/shard_map/ppermute | solution.py:500
  560.9 20.2 %collective-permute-start.31 = (bf16[4,24,2304]{2,1,0:T(8,128)(2,1)S(1)}, bf16[4,24,2304]{2,1,0:T(8,128)(2,1)S(1)}, u32[]{:S(2)}, u32[]{:S(2)}) collective-permute-start(bf16[4,24,2304]{2,1,0:T(8,128)(2,1)S(1)} %get-tuple-element.255), channel_id=1, source_target_pairs={{0,16},{8,24},{16,0},{24,8},{1,17},{9,25},{17,1},{25,9},{2,18},{10... | collective-permute-start | bytes 1327112 | tf_op jit(solution)/shard_map/ppermute | solution.py:500
  581.3 22.5 %collective-permute-start.35 = (f32[18,768]{1,0:T(8,128)S(1)}, f32[18,768]{1,0:T(8,128)S(1)}, u32[]{:S(2)}, u32[]{:S(2)}) collective-permute-start(f32[18,768]{1,0:T(8,128)S(1)} %add_add_fusion.1), channel_id=1, source_target_pairs={{0,6},{2,4},{4,2},{6,0},{1,7},{3,5},{5,3},{7,1},{8,14},{10,12},{12... | collective-permute-start | bytes 165896 | tf_op jit(solution)/shard_map/ppermute | solution.py:500
  584.9 19.2 %collective-permute-start.34 = (f32[18,768]{1,0:T(8,128)S(1)}, f32[18,768]{1,0:T(8,128)S(1)}, u32[]{:S(2)}, u32[]{:S(2)}) collective-permute-start(f32[18,768]{1,0:T(8,128)S(1)} %add_add_fusion.1), channel_id=1, source_target_pairs={{0,4},{2,6},{4,0},{6,2},{1,5},{3,7},{5,1},{7,3},{8,12},{10,14},{12... | collective-permute-start | bytes 165896 | tf_op jit(solution)/shard_map/ppermute | solution.py:500
  584.9 19.2 %collective-permute-start.33 = (f32[18,768]{1,0:T(8,128)S(1)}, f32[18,768]{1,0:T(8,128)}, u32[]{:S(2)}, u32[]{:S(2)}) collective-permute-start(f32[18,768]{1,0:T(8,128)S(1)} %add_add_fusion.1), channel_id=1, source_target_pairs={{0,2},{2,0},{4,6},{6,4},{1,3},{3,1},{5,7},{7,5},{8,10},{10,8},{12,... | collective-permute-start | bytes 165896 | tf_op jit(solution)/shard_map/ppermute | solution.py:500
  595.2 12.3 %collective-permute-start.36 = (bf16[24,3840]{1,0:T(8,128)(2,1)}, bf16[24,3840]{1,0:T(8,128)(2,1)S(1)}, u32[]{:S(2)}, u32[]{:S(2)}) collective-permute-start(bf16[24,3840]{1,0:T(8,128)(2,1)} %get-tuple-element.263), channel_id=1, source_target_pairs={{0,2},{2,0},{4,6},{6,4},{1,3},{3,1},{5,7},{7,5},{8,10},{10,8},{12,... | collective-permute-start | bytes 552968 | tf_op jit(solution)/shard_map/ppermute | solution.py:500
  596.3 12.3 %collective-permute-start.37 = (bf16[24,3840]{1,0:T(8,128)(2,1)}, bf16[24,3840]{1,0:T(8,128)(2,1)}, u32[]{:S(2)}, u32[]{:S(2)}) collective-permute-start(bf16[24,3840]{1,0:T(8,128)(2,1)} %get-tuple-element.264), channel_id=1, source_target_pairs={{0,4},{2,6},{4,0},{6,2},{1,5},{3,7},{5,1},{7,3},{8,12},{10,14},{12... | collective-permute-start | bytes 552968 | tf_op jit(solution)/shard_map/ppermute | solution.py:500
  603.8 7.7 %collective-permute-start.38 = (bf16[24,3840]{1,0:T(8,128)(2,1)}, bf16[24,3840]{1,0:T(8,128)(2,1)S(1)}, u32[]{:S(2)}, u32[]{:S(2)}) collective-permute-start(bf16[24,3840]{1,0:T(8,128)(2,1)} %get-tuple-element.265), channel_id=1, source_target_pairs={{0,6},{2,4},{4,2},{6,0},{1,7},{3,5},{5,3},{7,1},{8,14},{10,12},{12... | collective-permute-start | bytes 552968 | tf_op jit(solution)/shard_map/ppermute | solution.py:500
  (32 other events, 320.6 us)
Sparse Core Ops, SparseCore 0:
  42.3 117.5 all-gather.1
  306.5 172.2 reduce-scatter.1

commit v3 on v2

--- a/solution.py
+++ b/solution.py
@@ -444,9 +444,10 @@
     return call(end_kernel, 7, blocks, [blk(3 * D), blk(D), blk(D), once(1, D), column(D, 3 * D, 0)], [blk(D), once(8, D)],
                 (sds(T, D), sds(8, D, t=F32)))(dqkv, x, g1, gain, w)
 
-def wg_kernel(*refs, starts, counts, halves, rows):
+def wg_kernel(core_ref, *refs, starts, counts, halves, rows):
     n = sum(counts)
-    a_refs, b_refs, out_ref, t_refs = refs[:n], refs[n:2 * n], refs[2 * n], refs[2 * n + 1:]
+    many_out = 2 if rows else 1
+    a_refs, b_refs, out_refs, t_refs = refs[:n], refs[n:2 * n], refs[2 * n:2 * n + many_out], refs[2 * n + many_out:]
     step = pl.program_id(0)
     at = 0
     for i, many in enumerate(counts):
@@ -462,12 +463,14 @@
             res = sum(mm(t_ref[...], b_refs[n_at][...], 1, 0) for t_ref, n_at in zip(t_refs, mine))
             if rows:
                 parts = res.reshape(-1, halves, rows, res.shape[-1])
-                for h in range(halves):
-                    out_ref[h] = parts[:, h].reshape(-1, res.shape[-1]).astype(BF)
+                low, high = [parts[:, h].reshape(-1, res.shape[-1]) for h in range(2)]
+                first = core_ref[0, 0] == 0
+                out_refs[0][...] = jnp.where(first, low, high).astype(BF)
+                out_refs[1][...] = jnp.where(first, high, low).astype(BF)
             else:
-                out_ref[0] = res.astype(BF)
-
-def weight_grads(pairs, halves, rows, us):
+                out_refs[0][...] = res.astype(BF)
+
+def weight_grads(pairs, core, halves, rows, us):
     D = pairs[0][0][0].shape[1]
     starts, steps, specs, b_specs = [], 0, [], []
     for many_a, many_b in pairs:
@@ -478,17 +481,19 @@
             b_specs.append(chunk_spec(a.shape[0], D, steps, chunks))
         steps += chunks
     cols = steps * D
-    fits = rows % 8 == 0
-    groups = halves if fits else 1
+    fits = rows % 8 == 0 and halves == 2
+    groups = 2 if fits else 1
     counts = [len(many_a) for many_a, _ in pairs]
     lefts = [a for many_a, _ in pairs for a in many_a]
     rights = [b for _, many_b in pairs for b in many_b]
     out = call(partial(wg_kernel, starts=starts, counts=counts, halves=halves, rows=rows if fits else 0), us, steps,
-        specs + b_specs, [pl.BlockSpec((groups, D // groups, D), lambda j: (0, 0, j))], (sds(groups, D // groups, cols),),
-        [pltpu.VMEM((D, a.shape[0]), BF) for a in pairs[0][0]])(*lefts, *rights)[0]
+        [pl.BlockSpec(memory_space=pltpu.SMEM)] + specs + b_specs,
+        [pl.BlockSpec((D // groups, D), lambda j: (0, j))] * groups, [sds(D // groups, cols)] * groups,
+        [pltpu.VMEM((D, a.shape[0]), BF) for a in pairs[0][0]])(core.reshape(1, 1), *lefts, *rights)
     if fits:
-        return out.reshape(halves, -1, rows, cols)
-    return jnp.swapaxes(out.reshape(-1, halves, rows, cols), 0, 1)
+        return [part.reshape(-1, rows, cols) for part in out]
+    parts = jnp.swapaxes(out[0].reshape(-1, halves, rows, cols), 0, 1)
+    return [lax.dynamic_index_in_dim(parts, core ^ d, 0, keepdims=False) for d in range(halves)]
 
 def chunk_spec(rows, cols, start, many):
     return pl.BlockSpec((rows, cols), lambda j: (0, jnp.clip(j - start, 0, many - 1)))
@@ -533,15 +538,19 @@
     return out
 
 
-def near_first(array, axis):
-    size = lax.axis_size(axis)
-    step = 1
-    while step < size:
-        blocks = array.reshape((-1, 2) + array.shape[1:])
-        mine = (lax.axis_index(axis) // step) % 2
-        send = lax.dynamic_index_in_dim(blocks, 1 - mine, 1, keepdims=False).astype(BF)
-        keep = lax.dynamic_index_in_dim(blocks, mine, 1, keepdims=False)
-        array = keep.astype(F32) + partner(send, axis, step).astype(F32)
+def bit_step(array, axis, step, hold):
+    blocks = array.reshape((-1, 2) + array.shape[1:])
+    mine = (lax.axis_index(axis) // step) % 2
+    send = lax.dynamic_index_in_dim(blocks, 1 - mine, 1, keepdims=False)
+    keep = lax.dynamic_index_in_dim(blocks, mine, 1, keepdims=False)
+    came = after(partner(send, axis, step), hold)
+    return (keep.astype(F32) + came.astype(F32)).astype(BF)
+
+
+def later_bits(array, axis, hold):
+    step = 2
+    while step < lax.axis_size(axis):
+        array = bit_step(array, axis, step, hold)
         step *= 2
     return array[0]
 
@@ -701,7 +710,12 @@
             frames=frames,
         )
         back_s = partial(spatial_backward, gain=gain[1], w=s_all, first=first_places, **sizes_s)
-        grads_of = partial(weight_grads, halves=halves, rows=own_rows)
+        core = lax.axis_index("tensor")
+
+        def grads_of(pairs, us):
+            pieces = weight_grads(pairs, core, halves, own_rows, us)
+            return [(share * p).astype(BF) for p in pieces] if share != 1.0 else pieces
+
         d_m = (share * d_m if share != 1.0 else d_m).astype(BF).reshape(-1, in_cols)
         d_m = lax.psum_scatter(d_m, ALL, scatter_dimension=0, tiled=True)
         back = send_back(out)
@@ -710,38 +724,36 @@
         d_qkv_s, g1_a, g1_b, dz_a, dz_b, sums_s = back_s(g2, tied, qkv_s, x1, part=1, held=half)
         sums_s = sums_s + half[5]
         tied = after(d_qkv_s, *back[2:3])
-        d_s = share * grads_of([([a_s], [tied]), ([db], [o_s])], us=12)
-        tied = after(dz_a, d_s)
-        d_s = split_off(d_s, "tensor")
+        d_s = grads_of([([a_s], [tied]), ([db], [o_s])], us=12)
+        tied = after(dz_a, *d_s)
+        d_s = exchange(d_s, "tensor")
         dy_a, do_a, sums_y = temporal_pull(tied, t_all)
         dy_b, do_b, sums_yb = temporal_pull(after(dz_b, dy_a), t_all)
         d_s = added(d_s, dy_b).astype(BF)
         tied = after(dy_b, d_s, *back[3:])
         d_s = split_off(by_shard(d_s), "shard")
-        d_r = share * grads_of([([dy_a, tied], [o_a, o_b]), ([y_a, y_b], [dz_a, dz_b])], us=6)
-        tied = after(do_a, d_r)
-        d_r = split_off(d_r, "tensor")
+        d_r = grads_of([([dy_a, tied], [o_a, o_b]), ([y_a, y_b], [dz_a, dz_b])], us=6)
+        tied = after(do_a, *d_r)
+        d_r = exchange(d_r, "tensor")
         d_qkv_a, sums_q = temporal_backward(tied, qkv_a, probs_a, **sizes)
-        d_s = added(d_s, d_qkv_a).astype(BF)
         d_r = added(d_r, d_qkv_a).astype(BF)
-        tied = after(d_qkv_a, d_r, d_s)
-        d_s = split_off(d_s, "context")
-        into_a, sums_x = temporal_end(tied, x_a, g1_a, gain[0], t_all)
+        into_a, sums_x = temporal_end(after(d_qkv_a, d_r), x_a, g1_a, gain[0], t_all)
+        d_s = added(d_s, into_a).astype(BF)
         swap_a = by_place(into_a, first_places)
         into_a = from_clips(swap_a)
-        tied = after(do_b, swap_a, d_r, d_m)
+        tied = after(do_b, swap_a, d_s)
+        d_s = split_off(d_s, "context")
+        d_qkv_b, sums_qb = temporal_backward(tied, qkv_b, probs_b, **sizes)
+        d_r_first = bit_step(by_shard(d_r), "shard", 1, d_qkv_b)
+        d_q = grads_of([([at_a, at_b], [d_qkv_a, after(d_qkv_b, d_r_first)])], us=9)
         d_m = d_m.astype(F32)
-        d_r = split_off(by_shard(d_r), "shard")
-        d_qkv_b, sums_qb = temporal_backward(tied, qkv_b, probs_b, **sizes)
-        d_s = added(d_s, d_qkv_b)
-        d_r = added(d_r, d_qkv_b).astype(BF)
-        tied = after(d_qkv_b, d_r, d_s)
-        d_q = share * grads_of([([at_a, at_b], [d_qkv_a, tied])], us=9)
-        tied, d_q = lax.optimization_barrier((d_qkv_b, d_q, into_a))[:2]
-        d_q = split_off(d_q, "tensor")
+        d_r = later_bits(d_r_first, "shard", d_q[0])
+        tied = lax.optimization_barrier((d_qkv_b, *d_q, into_a, d_r, d_m))[0]
+        d_q = exchange(d_q, "tensor")
         into_b, sums_xb = temporal_end(tied, x_b, g1_b, gain[0], t_all)
         swap_b = by_place(into_b, places - first_places)
-        into_b = from_clips(after(swap_b, into_a))
+        d_s = added(d_s, into_b)
+        into_b = from_clips(after(swap_b, into_a, d_s))
         t, m = sums_y + sums_yb + sums_q + sums_qb + sums_x + sums_xb, sums_m
         rows = [v[n : n + 1] for n in (0, 1) for v in (t, sums_s, m)] + [t[2:4], sums_s[2:4]]
         rows = rows + [t[4:5], m[3:4], m[2:3], sums_s[4:5], d_hidden.reshape(-1, width)]
@@ -752,7 +764,7 @@
         output = sent_back([after(piece, d_q) for piece in back])
         small = plus_others(after(small, d_q), "context")
         d_q = shed(jnp.concatenate((d_r, d_q), axis=-1), "context")
-        into = jnp.swapaxes(jnp.concatenate((into_a, after(into_b, output)), axis=1), 1, 2)
+        into = jnp.swapaxes(jnp.concatenate((into_a, after(into_b, output, d_q)), axis=1), 1, 2)
         return output, into, (d_q, d_s, d_m, small)
 
     given = (rows_a, rows_b, pull_a, pull_b)

time: 627 us -> 605 us (0.965)
  waiting for transfers between devices: 107 us -> 87.3 us
    ppermute x39 -> x36, waiting for transfers between devices: 80.5 us -> 60.3 us  [exchange(): lax.ppermute(pieces[d], axis, [(i, i ^ d) for i in range(size)])]
    all_to_all x2, starting transfers between devices: 7.6 us -> 17.6 us  [from_clips(): lax.all_to_all(array, 'context', split_axis=0, concat_axis=0, tiled=True)]
    ppermute x39 -> x36, starting transfers between devices: 51.8 us -> 42.4 us  [exchange(): lax.ppermute(pieces[d], axis, [(i, i ^ d) for i in range(size)])]
    squeeze x7 -> x3, local copies, waits for them, and re-layouts: 9.8 us -> 2.02 us  [split_off(): lax.dynamic_index_in_dim(array, place ^ d, 0, keepdims=False)]
  transfers between devices with their start and end apart: 47 -> 46, of which waited for: 15 -> 10; matrix products, arithmetic and copies ran while one was open for 15% -> 15% of each run, Pallas kernels for 37% -> 39%
where the time goes in v3:
time: 605 us; the launch traced here: 599 us
  Pallas kernels  306 us (51%)
  waiting for transfers between devices  87.3 us (14%)
  starting transfers between devices  86.2 us (14%)
  local copies, waits for them, and re-layouts  56.9 us (9%)
  other arithmetic  47 us (8%)
  between operations  15.7 us (3%)
    pallas_call x1, Pallas kernels, mlp(): pl.pallas_call(partial(mlp_kernel, rb=rb, chunks=chunks, frames=frames),...  75.2 us
    ppermute x36, waiting for transfers between devices, exchange(): lax.ppermute(pieces[d], axis, [(i, i ^ d) for i in range(size)])  60.3 us
    pallas_call x2, Pallas kernels, spatial_backward(): pl.pallas_call(partial(sb_kernel, fb=fb, real=real, head=head, scale=scal...  49.3 us
    pallas_call x2, Pallas kernels, temporal_forward(): call(partial(tf_kernel, fb=fb, nb=nb, frames=frames, slot=LANES // frames...  48.1 us
    ppermute x36, starting transfers between devices, exchange(): lax.ppermute(pieces[d], axis, [(i, i ^ d) for i in range(size)])  42.4 us
    pallas_call x2, Pallas kernels, temporal_backward(): call(partial(tb_kernel, fb=fb, nb=nb, frames=frames, slot=LANES // frames...  40.7 us
    pallas_call x3, Pallas kernels, weight_grads(): call(partial(wg_kernel, starts=starts, counts=counts, halves=halves, rows...  38.8 us
    all_to_all x4, waiting for transfers between devices, to_clips(): lax.all_to_all(array, 'context', split_axis=0, concat_axis=0, tiled=True)  26.9 us
  transfers between devices with their start and end apart: 46, of which 10 were waited for; matrix products, arithmetic and copies ran while one was open for 15% of the time, Pallas kernels for 39%

profile of v3, /device:TPU:0, one launch (start us, length us, event | category | flops | bytes accessed | tf_op | source)
XLA Modules:
  0.0 599.0 jit_solution(8159449886639553364)
XLA Ops:
  12.0 3.0 collective-permute-start.2
  15.1 2.6 collective-permute-start.1
  21.8 3.2 slice.135
  32.2 8.7 %collective-permute-done.1 = bf16[24,6912]{1,0:T(8,128)(2,1)S(1)} collective-permute-done((bf16[24,6912]{1,0:T(8,128)(2,1)S(1)}, bf16[24,6912]{1,0:T(8,128)(2,1)S(1)}, u32[]{:S(2)}, u32[]{:S(2)}) %collective-permute-start.1) | collective-permute-done | bytes 331808 | tf_op jit(solution)/shard_map/ppermute | solution.py:505
  42.2 8.6 %all-to-all-start = ((bf16[4,96,2,768]{3,2,1,0:T(2,128)(2,1)}), bf16[4,96,2,768]{3,2,1,0:T(2,128)(2,1)S(1)}, u32[]{:S(2)}, u32[]{:S(2)}) async-start(bf16[4,96,2,768]{3,2,1,0:T(2,128)(2,1)} %bitcast.197), calls=%async_computation | async-start | bytes 2359296 | tf_op jit(solution)/shard_map/all_to_all | solution.py:629
  55.2 18.3 %collective-permute-done.5 = bf16[4,24,3840]{2,1,0:T(8,128)(2,1)S(1)} collective-permute-done((bf16[4,24,3840]{2,1,0:T(8,128)(2,1)}, bf16[4,24,3840]{2,1,0:T(8,128)(2,1)S(1)}, u32[]{:S(2)}, u32[]{:S(2)}) %collective-permute-start.5) | collective-permute-done | bytes 737312 | tf_op jit(solution)/shard_map/ppermute | solution.py:505
  73.5 11.1 %all-to-all-done = bf16[4,96,2,768]{3,2,1,0:T(2,128)(2,1)S(1)} async-done(((bf16[4,96,2,768]{3,2,1,0:T(2,128)(2,1)}), bf16[4,96,2,768]{3,2,1,0:T(2,128)(2,1)S(1)}, u32[]{:S(2)}, u32[]{:S(2)}) %all-to-all-start) | async-done | bytes 1179680 | tf_op jit(solution)/shard_map/all_to_all | solution.py:629
  84.6 4.7 collective-permute-done.4
  93.8 2.5 collective-permute-start.8
  97.8 5.4 all-to-all-start.1
  103.2 2.5 copy.45
  105.7 2.2 select_bitcast_fusion.1
  108.4 3.0 copy.46
  111.4 22.6 %shard_map.271 = (bf16[768,768]{1,0:T(8,128)(2,1)}, bf16[768,2304]{1,0:T(8,128)(2,1)}, f32[768,128]{1,0:T(8,128)}, bf16[768,768]{1,0:T(8,128)(2,1)}, bf16[768,768]{1,0:T(8,128)(2,1)}, /*index=5*/f32[768,768]{1,0:T(8,128)}) custom-call(bf16[768,768]{1,0:T(8,128)(2,1)} %bitcast.209, f32[1,768]{1,0:T(1,128)} %get-tuple-element.302.gain_ref, ...), custom_call_target="tpu_custom_call" | custom-call | flops 22000001024 | tf_op jit(solution)/shard_map/pallas_call | solution.py:352
  134.9 3.0 collective-permute-done.7
  142.5 15.8 %all-to-all-done.1 = bf16[4,100,2,768]{3,2,1,0:T(2,128)(2,1)} async-done(((bf16[4,100,2,768]{3,2,1,0:T(2,128)(2,1)}), bf16[4,100,2,768]{3,2,1,0:T(2,128)(2,1)}, u32[]{:S(2)}, u32[]{:S(2)}) %all-to-all-start.1) | async-done | bytes 1228832 | tf_op jit(solution)/shard_map/all_to_all | solution.py:629
  158.3 3.7 all-to-all-start.2
  164.7 25.5 %shard_map.272 = (bf16[896,768]{1,0:T(8,128)(2,1)}, bf16[896,2304]{1,0:T(8,128)(2,1)}, f32[896,128]{1,0:T(8,128)}, bf16[896,768]{1,0:T(8,128)(2,1)}, bf16[896,768]{1,0:T(8,128)(2,1)}, /*index=5*/f32[896,768]{1,0:T(8,128)}) custom-call(bf16[896,768]{1,0:T(8,128)(2,1)} %bitcast.204, f32[1,768]{1,0:T(1,128)} %get-tuple-element.302.gain_ref, ...), custom_call_target="tpu_custom_call" | custom-call | flops 22000001024 | tf_op jit(solution)/shard_map/pallas_call | solution.py:352
  190.1 5.1 all-to-all-start.3
  198.7 2.6 copy.48
  201.3 25.5 %shard_map.273 = (bf16[1664,768]{1,0:T(8,128)(2,1)}, bf16[1664,2304]{1,0:T(8,128)(2,1)}, bf16[1664,768]{1,0:T(8,128)(2,1)}, f32[1664,768]{1,0:T(8,128)}, f32[1664,768]{1,0:T(8,128)}) custom-call(f32[768,768]{1,0:T(8,128)} %get-tuple-element.126.xa_ref, f32[896,768]{1,0:T(8,128)} %get-tuple-element.135.xb_ref, f32[1,768]{1,0:T(1,128)} %get-tuple-element.303.gain_ref, ...), custom_call_target="tpu_custom_call" | custom-call | flops 30000001024 | tf_op jit(solution)/shard_map/pallas_call | solution.py:207
  229.3 75.2 %shard_map.274 = (bf16[1664,768]{1,0:T(8,128)(2,1)}, f32[1664,768]{1,0:T(8,128)}, bf16[1664,768]{1,0:T(8,128)(2,1)}, bf16[16,2,96,1536]{3,2,1,0:T(8,128)(2,1)}, f32[1,3072]{1,0:T(1,128)}, /*index=5*/f32[8,768]{1,0:T(8,128)}) custom-call(f32[1664,768]{1,0:T(8,128)} %get-tuple-element.137.x_ref, bf16[768,768]{1,0:T(8,128)(2,1)} %bitcast.211, ...), custom_call_target="tpu_custom_call" | custom-call | flops 74999996416 | tf_op jit(solution)/shard_map/pallas_call | solution.py:114
  310.5 2.4 collective-permute-start.13
  312.8 24.5 %shard_map.275 = (bf16[1664,2304]{1,0:T(8,128)(2,1)}, f32[768,768]{1,0:T(8,128)}, f32[896,768]{1,0:T(8,128)}, bf16[768,768]{1,0:T(8,128)(2,1)}, bf16[896,768]{1,0:T(8,128)(2,1)}, /*index=5*/f32[8,768]{1,0:T(8,128)}) custom-call(f32[1664,768]{1,0:T(8,128)} %get-tuple-element.143.g2_ref, bf16[1664,768]{1,0:T(8,128)(2,1)} %get-tuple-element.148.db_ref.refs_1_, ...), custom_call_target="tpu_custom_call" | custom-call | flops 24000000000 | tf_op jit(solution)/shard_map/pallas_call | solution.py:272
  337.4 24.8 %shard_map.276 = (bf16[1664,2304]{1,0:T(8,128)(2,1)}, f32[768,768]{1,0:T(8,128)}, f32[896,768]{1,0:T(8,128)}, bf16[768,768]{1,0:T(8,128)(2,1)}, bf16[896,768]{1,0:T(8,128)(2,1)}, /*index=5*/f32[8,768]{1,0:T(8,128)}) custom-call(f32[1664,768]{1,0:T(8,128)} %get-tuple-element.143.g2_ref,, ...), custom_call_target="tpu_custom_call", output_to_operand_aliasing={{0}: (7, {}), {1}: (8, {}), {2}: (9, {}), {3}: (10, {}), {4... | custom-call | flops 24000000000 | tf_op jit(solution)/shard_map/pallas_call | solution.py:272
  362.2 16.3 %shard_map.277 = (bf16[384,3072]{1,0:T(8,128)(2,1)}, bf16[384,3072]{1,0:T(8,128)(2,1)}) custom-call(s32[1,1]{1,0:T(1,128)} %bitcast.41.core_ref, bf16[1664,768]{1,0:T(8,128)(2,1)} %get-tuple-element.154.refs_0_, bf16[1664,768]{1,0:T(8,128)(2,1)} %get-tuple-element.148.db_ref.refs_1_, bf16[1664,2304]{1,0:T(8,128)(2,1)} %get-tuple-element.156.refs_2_, ...), custom_call_target="tpu_custom_call" | custom-call | flops 12000000000 | tf_op jit(solution)/shard_map/pallas_call | solution.py:489
  384.2 5.3 shard_map.278
  390.1 5.6 shard_map.279
  395.6 3.3 add_convert_fusion
  398.9 2.5 collective-permute-done.11
  401.4 11.3 %shard_map.280 = (bf16[384,1536]{1,0:T(8,128)(2,1)}, bf16[384,1536]{1,0:T(8,128)(2,1)}) custom-call(s32[1,1]{1,0:T(1,128)} %bitcast.41.core_ref, bf16[768,768]{1,0:T(8,128)(2,1)} %get-tuple-element.162.refs_0_, bf16[896,768]{1,0:T(8,128)(2,1)} %get-tuple-element.167.refs_1_, bf16[768,768]{1,0:T(8,128)(2,1)} %get-tuple-element.168.refs_2_, ...), custom_call_target="tpu_custom_call" | custom-call | flops 6000000000 | tf_op jit(solution)/shard_map/pallas_call | solution.py:489
  417.6 19.0 %shard_map.281 = (bf16[768,2304]{1,0:T(8,128)(2,1)}, f32[8,768]{1,0:T(8,128)}) custom-call(bf16[768,768]{1,0:T(8,128)(2,1)} %get-tuple-element.174.do_ref, bf16[768,2304]{1,0:T(8,128)(2,1)} %get-tuple-element.175.qkv_ref, f32[768,128]{1,0:T(8,128)} %get-tuple-element.176.p_ref), custom_call_target="tpu_custom_call" | custom-call | flops 20000000000 | tf_op jit(solution)/shard_map/pallas_call | solution.py:429
  442.1 8.4 %shard_map.282 = (bf16[768,768]{1,0:T(8,128)(2,1)}, f32[8,768]{1,0:T(8,128)}) custom-call(bf16[768,2304]{1,0:T(8,128)(2,1)} %get-tuple-element.180.dqkv_ref.refs_2_, bf16[768,768]{1,0:T(8,128)(2,1)} %bitcast.210, f32[768,768]{1,0:T(8,128)} %get-tuple-element.181.g1_ref, f32[1,768]{1,0:T(1,128)} %get-tuple-element.302.gain_ref, bf16[768,3840]{1,0:T(8,128)(2,1)} %bitcast.182), custom_call_target="tpu_custom_call" | custom-call | flops 7000000000 | tf_op jit(solution)/shard_map/pallas_call | solution.py:444
  450.6 3.5 copy.75
  454.1 13.4 %all-to-all-start.4 = ((bf16[4,96,2,768]{3,2,1,0:T(2,128)(2,1)}), bf16[4,96,2,768]{3,2,1,0:T(2,128)(2,1)}, u32[]{:S(2)}, u32[]{:S(2)}) async-start(bf16[4,96,2,768]{3,2,1,0:T(2,128)(2,1)} %bitcast.198), calls=%async_computation.4 | async-start | bytes 2359296 | tf_op jit(solution)/shard_map/all_to_all | solution.py:644
  470.9 3.0 collective-permute-start.29
  475.4 21.8 %shard_map.283 = (bf16[896,2304]{1,0:T(8,128)(2,1)}, f32[8,768]{1,0:T(8,128)}) custom-call(bf16[896,768]{1,0:T(8,128)(2,1)} %get-tuple-element.186.do_ref, bf16[896,2304]{1,0:T(8,128)(2,1)} %get-tuple-element.187.qkv_ref, f32[896,128]{1,0:T(8,128)} %get-tuple-element.188.p_ref), custom_call_target="tpu_custom_call" | custom-call | flops 20000000000 | tf_op jit(solution)/shard_map/pallas_call | solution.py:429
  500.0 11.2 %shard_map.284 = (bf16[384,2304]{1,0:T(8,128)(2,1)}, bf16[384,2304]{1,0:T(8,128)(2,1)}) custom-call(s32[1,1]{1,0:T(1,128)} %bitcast.41.core_ref, bf16[768,768]{1,0:T(8,128)(2,1)} %get-tuple-element.141.refs_0_, bf16[896,768]{1,0:T(8,128)(2,1)} %get-tuple-element.142.refs_1_, bf16[768,2304]{1,0:T(8,128)(2,1)} %get-tuple-element.180.dqkv_ref.refs_2_, ...), custom_call_target="tpu_custom_call" | custom-call | flops 8999999488 | tf_op jit(solution)/shard_map/pallas_call | solution.py:489
  511.4 9.1 %shard_map.285 = (bf16[896,768]{1,0:T(8,128)(2,1)}, f32[8,768]{1,0:T(8,128)}) custom-call(bf16[896,2304]{1,0:T(8,128)(2,1)} %get-tuple-element.196.refs_3_.dqkv_ref, bf16[896,768]{1,0:T(8,128)(2,1)} %bitcast.205, f32[896,768]{1,0:T(8,128)} %get-tuple-element.197.g1_ref, f32[1,768]{1,0:T(1,128)} %get-tuple-element.302.gain_ref, bf16[768,3840]{1,0:T(8,128)(2,1)} %bitcast.183), custom_call_target="tpu_custom_call" | custom-call | flops 7000000000 | tf_op jit(solution)/shard_map/pallas_call | solution.py:444
  526.8 4.2 all-to-all-start.5
  531.0 2.4 add_convert_fusion.1
  541.6 18.1 %collective-permute-done.25 = f32[18,768]{1,0:T(8,128)S(1)} collective-permute-done((f32[18,768]{1,0:T(8,128)S(1)}, f32[18,768]{1,0:T(8,128)S(1)}, u32[]{:S(2)}, u32[]{:S(2)}) %collective-permute-start.25) | collective-permute-done | bytes 55328 | tf_op jit(solution)/shard_map/ppermute | solution.py:505
  560.0 3.8 collective-permute-start.37
  566.0 2.8 collective-permute-start.33
  568.8 2.5 fusion.7
  571.3 6.1 %maximum_bitcast_fusion = bf16[4,2,196,768]{3,1,2,0:T(2,128)(2,1)} fusion(bf16[1,196,2,768]{3,2,1,0:T(2,128)(2,1)S(1)} %get-tuple-element.253, bf16[1,196,2,768]{3,2,1,0:T(2,128)(2,1)S(1)} %get-tuple-element.252, bf16[1,196,2,768]{3,2,1,0:T(2,128)(2,1)S(1)} %get-tuple-element.251, bf16[1,196,2,768]{3,2,1,0:T(2,128)(2,1)S(1)} %get-tuple-element.250), kind=kLoop, calls=%fused_computation.7 | loop fusion | flops 3612672 | bytes 4816896 | tf_op jit(solution)/shard_map/transpose | solution.py:656
  580.0 4.7 collective-permute-done.34
  586.2 5.8 maximum_bitcast_fusion.1
  (233 shorter events, 93.1 us)
Async XLA Ops:
  7.2 222.1 %all-gather.2.cloned.1.call-start = ((), (), s32[]{:S(2)}) async-start(), calls=%async_computation.7 | async-start | bytes 9732096 | tf_op jit(solution)/shard_map/all_gather | solution.py:683
  12.0 20.2 %collective-permute-start.2 = (bf16[24,6912]{1,0:T(8,128)(2,1)S(1)}, bf16[24,6912]{1,0:T(8,128)(2,1)S(1)}, u32[]{:S(2)}, u32[]{:S(2)}) collective-permute-start(bf16[24,6912]{1,0:T(8,128)(2,1)S(1)} %convert_dynamic-update-slice_fusion), channel_id=1, source_target_pairs={{0,2},{2,0},{4,6},{6,4},{1,3},{3,1},{5,7},{7,5},{8,10},{10,8},{12,... | collective-permute-start | bytes 995336 | tf_op jit(solution)/shard_map/ppermute | solution.py:505
  15.1 25.8 %collective-permute-start.1 = (bf16[24,6912]{1,0:T(8,128)(2,1)S(1)}, bf16[24,6912]{1,0:T(8,128)(2,1)S(1)}, u32[]{:S(2)}, u32[]{:S(2)}) collective-permute-start(bf16[24,6912]{1,0:T(8,128)(2,1)S(1)} %convert_dynamic-update-slice_fusion), channel_id=1, source_target_pairs={{0,4},{2,6},{4,0},{6,2},{1,5},{3,7},{5,1},{7,3},{8,12},{10,14},{12... | collective-permute-start | bytes 995336 | tf_op jit(solution)/shard_map/ppermute | solution.py:505
  17.6 23.3 %collective-permute-start = (bf16[24,6912]{1,0:T(8,128)(2,1)S(1)}, bf16[24,6912]{1,0:T(8,128)(2,1)}, u32[]{:S(2)}, u32[]{:S(2)}) collective-permute-start(bf16[24,6912]{1,0:T(8,128)(2,1)S(1)} %convert_dynamic-update-slice_fusion), channel_id=1, source_target_pairs={{0,6},{2,4},{4,2},{6,0},{1,7},{3,5},{5,3},{7,1},{8,14},{10,12},{12... | collective-permute-start | bytes 995336 | tf_op jit(solution)/shard_map/ppermute | solution.py:505
  42.2 42.4 %all-to-all-start = ((bf16[4,96,2,768]{3,2,1,0:T(2,128)(2,1)}), bf16[4,96,2,768]{3,2,1,0:T(2,128)(2,1)S(1)}, u32[]{:S(2)}, u32[]{:S(2)}) async-start(bf16[4,96,2,768]{3,2,1,0:T(2,128)(2,1)} %bitcast.197), calls=%async_computation | async-start | bytes 2359296 | tf_op jit(solution)/shard_map/all_to_all | solution.py:629
  51.8 21.7 %collective-permute-start.5 = (bf16[4,24,3840]{2,1,0:T(8,128)(2,1)}, bf16[4,24,3840]{2,1,0:T(8,128)(2,1)S(1)}, u32[]{:S(2)}, u32[]{:S(2)}) collective-permute-start(bf16[4,24,3840]{2,1,0:T(8,128)(2,1)} %slice.179), channel_id=1, source_target_pairs={{0,8},{8,0},{16,24},{24,16},{1,9},{9,1},{17,25},{25,17},{2,10},{10... | collective-permute-start | bytes 2211848 | tf_op jit(solution)/shard_map/ppermute | solution.py:505
  53.2 36.0 %collective-permute-start.4 = (bf16[4,24,3840]{2,1,0:T(8,128)(2,1)}, bf16[4,24,3840]{2,1,0:T(8,128)(2,1)}, u32[]{:S(2)}, u32[]{:S(2)}) collective-permute-start(bf16[4,24,3840]{2,1,0:T(8,128)(2,1)} %slice.179), channel_id=1, source_target_pairs={{0,16},{8,24},{16,0},{24,8},{1,17},{9,25},{17,1},{25,9},{2,18},{10... | collective-permute-start | bytes 2211848 | tf_op jit(solution)/shard_map/ppermute | solution.py:505
  54.8 34.5 %collective-permute-start.3 = (bf16[4,24,3840]{2,1,0:T(8,128)(2,1)}, bf16[4,24,3840]{2,1,0:T(8,128)(2,1)}, u32[]{:S(2)}, u32[]{:S(2)}) collective-permute-start(bf16[4,24,3840]{2,1,0:T(8,128)(2,1)} %slice.179), channel_id=1, source_target_pairs={{0,24},{8,16},{16,8},{24,0},{1,25},{9,17},{17,9},{25,1},{2,26},{10... | collective-permute-start | bytes 2211848 | tf_op jit(solution)/shard_map/ppermute | solution.py:505
  92.9 12.7 %collective-permute-start.6 = (bf16[4,4,24,3840]{3,2,1,0:T(8,128)(2,1)}, bf16[4,4,24,3840]{3,2,1,0:T(8,128)(2,1)}, u32[]{:S(2)}, u32[]{:S(2)}) collective-permute-start(bf16[4,4,24,3840]{3,2,1,0:T(8,128)(2,1)} %pad_maximum_fusion.2), channel_id=1, source_target_pairs={{0,1},{1,0},{2,3},{3,2},{4,5},{5,4},{6,7},{7,6},{8,9},{9,8},{10,11... | collective-permute-start | bytes 8847368 | tf_op jit(solution)/shard_map/ppermute | solution.py:505
  93.8 40.2 %collective-permute-start.9 = (bf16[4,24,3072]{2,1,0:T(8,128)(2,1)}, bf16[4,24,3072]{2,1,0:T(8,128)(2,1)S(1)}, u32[]{:S(2)}, u32[]{:S(2)}) collective-permute-start(bf16[4,24,3072]{2,1,0:T(8,128)(2,1)} %slice.180), channel_id=1, source_target_pairs={{0,8},{8,0},{16,24},{24,16},{1,9},{9,1},{17,25},{25,17},{2,10},{10... | collective-permute-start | bytes 1769480 | tf_op jit(solution)/shard_map/ppermute | solution.py:505
  93.8 40.2 %collective-permute-start.8 = (bf16[4,24,3072]{2,1,0:T(8,128)(2,1)}, bf16[4,24,3072]{2,1,0:T(8,128)(2,1)}, u32[]{:S(2)}, u32[]{:S(2)}) collective-permute-start(bf16[4,24,3072]{2,1,0:T(8,128)(2,1)} %slice.180), channel_id=1, source_target_pairs={{0,16},{8,24},{16,0},{24,8},{1,17},{9,25},{17,1},{25,9},{2,18},{10... | collective-permute-start | bytes 1769480 | tf_op jit(solution)/shard_map/ppermute | solution.py:505
  96.3 41.5 %collective-permute-start.7 = (bf16[4,24,3072]{2,1,0:T(8,128)(2,1)}, bf16[4,24,3072]{2,1,0:T(8,128)(2,1)}, u32[]{:S(2)}, u32[]{:S(2)}) collective-permute-start(bf16[4,24,3072]{2,1,0:T(8,128)(2,1)} %slice.180), channel_id=1, source_target_pairs={{0,24},{8,16},{16,8},{24,0},{1,25},{9,17},{17,9},{25,1},{2,26},{10... | collective-permute-start | bytes 1769480 | tf_op jit(solution)/shard_map/ppermute | solution.py:505
  97.8 60.5 %all-to-all-start.1 = ((bf16[4,100,2,768]{3,2,1,0:T(2,128)(2,1)}), bf16[4,100,2,768]{3,2,1,0:T(2,128)(2,1)}, u32[]{:S(2)}, u32[]{:S(2)}) async-start(bf16[4,100,2,768]{3,2,1,0:T(2,128)(2,1)} %bitcast.187), calls=%async_computation.1 | async-start | bytes 2457600 | tf_op jit(solution)/shard_map/all_to_all | solution.py:629
  141.3 55.0 %collective-permute-start.10 = (bf16[4,4,24,3072]{3,2,1,0:T(8,128)(2,1)}, bf16[4,4,24,3072]{3,2,1,0:T(8,128)(2,1)}, u32[]{:S(2)}, u32[]{:S(2)}) collective-permute-start(bf16[4,4,24,3072]{3,2,1,0:T(8,128)(2,1)} %pad_maximum_fusion.3), channel_id=1, source_target_pairs={{0,1},{1,0},{2,3},{3,2},{4,5},{5,4},{6,7},{7,6},{8,9},{9,8},{10,11... | collective-permute-start | bytes 7077896 | tf_op jit(solution)/shard_map/ppermute | solution.py:505
  158.3 31.8 %all-to-all-start.2 = ((bf16[4,96,2,768]{3,2,1,0:T(2,128)(2,1)}), bf16[4,96,2,768]{3,2,1,0:T(2,128)(2,1)S(1)}, u32[]{:S(2)}, u32[]{:S(2)}) async-start(bf16[4,96,2,768]{3,2,1,0:T(2,128)(2,1)} %bitcast.26), calls=%async_computation.2 | async-start | bytes 2359296 | tf_op jit(solution)/shard_map/all_to_all | solution.py:629
  190.1 36.6 %all-to-all-start.3 = ((bf16[4,100,2,768]{3,2,1,0:T(2,128)(2,1)}), bf16[4,100,2,768]{3,2,1,0:T(2,128)(2,1)}, u32[]{:S(2)}, u32[]{:S(2)}) async-start(bf16[4,100,2,768]{3,2,1,0:T(2,128)(2,1)} %bitcast.186), calls=%async_computation.3 | async-start | bytes 2457600 | tf_op jit(solution)/shard_map/all_to_all | solution.py:629
  195.2 316.1 %reduce-scatter.2.cloned.1.call-start = ((), (), s32[]{:S(2)}) async-start(), calls=%async_computation.8 | async-start | bytes 9732096 | tf_op jit(solution)/shard_map/reduce_scatter | solution.py:720
  308.4 29.0 %collective-permute-start.12 = (bf16[196,2,768]{2,1,0:T(2,128)(2,1)S(1)}, bf16[196,2,768]{2,1,0:T(2,128)(2,1)S(1)}, u32[]{:S(2)}, u32[]{:S(2)}) collective-permute-start(bf16[196,2,768]{2,1,0:T(2,128)(2,1)S(1)} %bitcast.216), channel_id=1, source_target_pairs={{0,2},{2,0},{4,6},{6,4},{1,3},{3,1},{5,7},{7,5},{8,10},{10,8},{12,... | collective-permute-start | bytes 1806344 | tf_op jit(solution)/shard_map/ppermute | solution.py:505
  310.5 51.7 %collective-permute-start.13 = (bf16[196,2,768]{2,1,0:T(2,128)(2,1)S(1)}, bf16[196,2,768]{2,1,0:T(2,128)(2,1)S(1)}, u32[]{:S(2)}, u32[]{:S(2)}) collective-permute-start(bf16[196,2,768]{2,1,0:T(2,128)(2,1)S(1)} %bitcast.215), channel_id=1, source_target_pairs={{0,4},{2,6},{4,0},{6,2},{1,5},{3,7},{5,1},{7,3},{8,12},{10,14},{12... | collective-permute-start | bytes 1806344 | tf_op jit(solution)/shard_map/ppermute | solution.py:505
  378.5 17.1 %collective-permute-start.14 = (bf16[16,24,3072]{2,1,0:T(8,128)(2,1)}, bf16[16,24,3072]{2,1,0:T(8,128)(2,1)}, u32[]{:S(2)}, u32[]{:S(2)}) collective-permute-start(bf16[16,24,3072]{2,1,0:T(8,128)(2,1)} %bitcast.222), channel_id=1, source_target_pairs={{0,1},{1,0},{2,3},{3,2},{4,5},{5,4},{6,7},{7,6},{8,9},{9,8},{10,11... | collective-permute-start | bytes 7077896 | tf_op jit(solution)/shard_map/ppermute | solution.py:505
  382.5 18.9 %collective-permute-start.11 = (bf16[196,2,768]{2,1,0:T(2,128)(2,1)}, bf16[196,2,768]{2,1,0:T(2,128)(2,1)S(1)}, u32[]{:S(2)}, u32[]{:S(2)}) collective-permute-start(bf16[196,2,768]{2,1,0:T(2,128)(2,1)} %bitcast.164), channel_id=1, source_target_pairs={{0,6},{2,4},{4,2},{6,0},{1,7},{3,5},{5,3},{7,1},{8,14},{10,12},{12... | collective-permute-start | bytes 1806344 | tf_op jit(solution)/shard_map/ppermute | solution.py:505
  412.8 23.8 %collective-permute-start.15 = (bf16[16,24,1536]{2,1,0:T(8,128)(2,1)}, bf16[16,24,1536]{2,1,0:T(8,128)(2,1)S(1)}, u32[]{:S(2)}, u32[]{:S(2)}) collective-permute-start(bf16[16,24,1536]{2,1,0:T(8,128)(2,1)} %bitcast.224), channel_id=1, source_target_pairs={{0,1},{1,0},{2,3},{3,2},{4,5},{5,4},{6,7},{7,6},{8,9},{9,8},{10,11... | collective-permute-start | bytes 3538952 | tf_op jit(solution)/shard_map/ppermute | solution.py:505
  414.1 53.5 %collective-permute-start.16 = (bf16[4,24,3072]{2,1,0:T(8,128)(2,1)}, bf16[4,24,3072]{2,1,0:T(8,128)(2,1)}, u32[]{:S(2)}, u32[]{:S(2)}) collective-permute-start(bf16[4,24,3072]{2,1,0:T(8,128)(2,1)} %get-tuple-element.254), channel_id=1, source_target_pairs={{0,8},{8,0},{16,24},{24,16},{1,9},{9,1},{17,25},{25,17},{2,10},{10... | collective-permute-start | bytes 1769480 | tf_op jit(solution)/shard_map/ppermute | solution.py:505
  415.7 51.9 %collective-permute-start.18 = (bf16[4,24,3072]{2,1,0:T(8,128)(2,1)}, bf16[4,24,3072]{2,1,0:T(8,128)(2,1)}, u32[]{:S(2)}, u32[]{:S(2)}) collective-permute-start(bf16[4,24,3072]{2,1,0:T(8,128)(2,1)} %get-tuple-element.255), channel_id=1, source_target_pairs={{0,24},{8,16},{16,8},{24,0},{1,25},{9,17},{17,9},{25,1},{2,26},{10... | collective-permute-start | bytes 1769480 | tf_op jit(solution)/shard_map/ppermute | solution.py:505
  417.0 50.6 %collective-permute-start.17 = (bf16[4,24,3072]{2,1,0:T(8,128)(2,1)}, bf16[4,24,3072]{2,1,0:T(8,128)(2,1)}, u32[]{:S(2)}, u32[]{:S(2)}) collective-permute-start(bf16[4,24,3072]{2,1,0:T(8,128)(2,1)} %get-tuple-element.256), channel_id=1, source_target_pairs={{0,16},{8,24},{16,0},{24,8},{1,17},{9,25},{17,1},{25,9},{2,18},{10... | collective-permute-start | bytes 1769480 | tf_op jit(solution)/shard_map/ppermute | solution.py:505
  440.4 56.8 %collective-permute-start.19 = (bf16[2,4,24,1536]{3,2,1,0:T(8,128)(2,1)}, bf16[2,4,24,1536]{3,2,1,0:T(8,128)(2,1)}, u32[]{:S(2)}, u32[]{:S(2)}) collective-permute-start(bf16[2,4,24,1536]{3,2,1,0:T(8,128)(2,1)} %dynamic-slice_bitcast_fusion), channel_id=1, source_target_pairs={{0,8},{8,0},{16,24},{24,16},{1,9},{9,1},{17,25},{25,17},{2,10},{10... | collective-permute-start | bytes 1769480 | tf_op jit(solution)/shard_map/ppermute | solution.py:525
  454.1 57.1 %all-to-all-start.4 = ((bf16[4,96,2,768]{3,2,1,0:T(2,128)(2,1)}), bf16[4,96,2,768]{3,2,1,0:T(2,128)(2,1)}, u32[]{:S(2)}, u32[]{:S(2)}) async-start(bf16[4,96,2,768]{3,2,1,0:T(2,128)(2,1)} %bitcast.198), calls=%async_computation.4 | async-start | bytes 2359296 | tf_op jit(solution)/shard_map/all_to_all | solution.py:644
  470.9 49.6 %collective-permute-start.29 = (bf16[24,3072]{1,0:T(8,128)(2,1)}, bf16[24,3072]{1,0:T(8,128)(2,1)S(1)}, u32[]{:S(2)}, u32[]{:S(2)}) collective-permute-start(bf16[24,3072]{1,0:T(8,128)(2,1)} %get-tuple-element.271), channel_id=1, source_target_pairs={{0,2},{2,0},{4,6},{6,4},{1,3},{3,1},{5,7},{7,5},{8,10},{10,8},{12,... | collective-permute-start | bytes 442376 | tf_op jit(solution)/shard_map/ppermute | solution.py:505
  473.9 46.6 %collective-permute-start.31 = (bf16[24,3072]{1,0:T(8,128)(2,1)S(1)}, bf16[24,3072]{1,0:T(8,128)(2,1)S(1)}, u32[]{:S(2)}, u32[]{:S(2)}) collective-permute-start(bf16[24,3072]{1,0:T(8,128)(2,1)S(1)} %get-tuple-element.272), channel_id=1, source_target_pairs={{0,6},{2,4},{4,2},{6,0},{1,7},{3,5},{5,3},{7,1},{8,14},{10,12},{12... | collective-permute-start | bytes 442376 | tf_op jit(solution)/shard_map/ppermute | solution.py:505
  475.3 45.3 %collective-permute-start.30 = (bf16[24,3072]{1,0:T(8,128)(2,1)S(1)}, bf16[24,3072]{1,0:T(8,128)(2,1)}, u32[]{:S(2)}, u32[]{:S(2)}) collective-permute-start(bf16[24,3072]{1,0:T(8,128)(2,1)S(1)} %get-tuple-element.273), channel_id=1, source_target_pairs={{0,4},{2,6},{4,0},{6,2},{1,5},{3,7},{5,1},{7,3},{8,12},{10,14},{12... | collective-permute-start | bytes 442376 | tf_op jit(solution)/shard_map/ppermute | solution.py:505
  498.4 12.7 %collective-permute-start.21 = (bf16[1,4,24,1536]{3,2,1,0:T(8,128)(2,1)S(1)}, bf16[1,4,24,1536]{3,2,1,0:T(8,128)(2,1)S(1)}, u32[]{:S(2)}, u32[]{:S(2)}) collective-permute-start(bf16[1,4,24,1536]{3,2,1,0:T(8,128)(2,1)S(1)} %constant_dynamic-slice_fusion.1), channel_id=1, source_target_pairs={{0,16},{8,24},{16,0},{24,8},{1,17},{9,25},{17,1},{25,9},{2,18},{10... | collective-permute-start | bytes 884744 | tf_op jit(solution)/shard_map/ppermute | solution.py:525
  511.1 19.9 %collective-permute-start.20 = (bf16[16,24,2304]{2,1,0:T(8,128)(2,1)}, bf16[16,24,2304]{2,1,0:T(8,128)(2,1)}, u32[]{:S(2)}, u32[]{:S(2)}) collective-permute-start(bf16[16,24,2304]{2,1,0:T(8,128)(2,1)} %bitcast.223), channel_id=1, source_target_pairs={{0,1},{1,0},{2,3},{3,2},{4,5},{5,4},{6,7},{7,6},{8,9},{9,8},{10,11... | collective-permute-start | bytes 5308424 | tf_op jit(solution)/shard_map/ppermute | solution.py:505
  523.5 10.0 %collective-permute-start.23 = (f32[18,768]{1,0:T(8,128)S(1)}, f32[18,768]{1,0:T(8,128)S(1)}, u32[]{:S(2)}, u32[]{:S(2)}) collective-permute-start(f32[18,768]{1,0:T(8,128)S(1)} %concatenate.23), channel_id=1, source_target_pairs={{0,1},{1,0},{2,3},{3,2},{4,5},{5,4},{6,7},{7,6},{8,9},{9,8},{10,11... | collective-permute-start | bytes 165896 | tf_op jit(solution)/shard_map/ppermute | solution.py:505
  526.8 59.4 %all-to-all-start.5 = ((bf16[4,100,2,768]{3,2,1,0:T(2,128)(2,1)}), bf16[4,100,2,768]{3,2,1,0:T(2,128)(2,1)S(1)}, u32[]{:S(2)}, u32[]{:S(2)}) async-start(bf16[4,100,2,768]{3,2,1,0:T(2,128)(2,1)} %bitcast.159), calls=%async_computation.6 | async-start | bytes 2457600 | tf_op jit(solution)/shard_map/all_to_all | solution.py:644
  533.5 6.1 %collective-permute-start.26 = (f32[18,768]{1,0:T(8,128)S(1)}, f32[18,768]{1,0:T(8,128)S(1)}, u32[]{:S(2)}, u32[]{:S(2)}) collective-permute-start(f32[18,768]{1,0:T(8,128)S(1)} %add.213), channel_id=1, source_target_pairs={{0,24},{8,16},{16,8},{24,0},{1,25},{9,17},{17,9},{25,1},{2,26},{10... | collective-permute-start | bytes 165896 | tf_op jit(solution)/shard_map/ppermute | solution.py:505
  534.0 25.7 %collective-permute-start.22 = (bf16[4,24,2304]{2,1,0:T(8,128)(2,1)S(1)}, bf16[4,24,2304]{2,1,0:T(8,128)(2,1)S(1)}, u32[]{:S(2)}, u32[]{:S(2)}) collective-permute-start(bf16[4,24,2304]{2,1,0:T(8,128)(2,1)S(1)} %get-tuple-element.261), channel_id=1, source_target_pairs={{0,8},{8,0},{16,24},{24,16},{1,9},{9,1},{17,25},{25,17},{2,10},{10... | collective-permute-start | bytes 1327112 | tf_op jit(solution)/shard_map/ppermute | solution.py:505
  535.7 24.0 %collective-permute-start.28 = (bf16[4,24,2304]{2,1,0:T(8,128)(2,1)S(1)}, bf16[4,24,2304]{2,1,0:T(8,128)(2,1)S(1)}, u32[]{:S(2)}, u32[]{:S(2)}) collective-permute-start(bf16[4,24,2304]{2,1,0:T(8,128)(2,1)S(1)} %get-tuple-element.262), channel_id=1, source_target_pairs={{0,24},{8,16},{16,8},{24,0},{1,25},{9,17},{17,9},{25,1},{2,26},{10... | collective-permute-start | bytes 1327112 | tf_op jit(solution)/shard_map/ppermute | solution.py:505
  537.1 31.7 %copy-start.15 = (bf16[196,2,768]{2,1,0:T(2,128)(2,1)S(1)}, bf16[196,2,768]{2,1,0:T(2,128)(2,1)}, u32[]{:S(2)}) copy-start(bf16[196,2,768]{2,1,0:T(2,128)(2,1)} %copy-done.14) | copy-start | bytes 1806340
  537.1 31.7 %copy-start.17 = (bf16[196,2,768]{2,1,0:T(2,128)(2,1)S(1)}, bf16[196,2,768]{2,1,0:T(2,128)(2,1)}, u32[]{:S(2)}) copy-start(bf16[196,2,768]{2,1,0:T(2,128)(2,1)} %copy-done.16) | copy-start | bytes 1806340
  537.1 22.6 %collective-permute-start.27 = (bf16[4,24,2304]{2,1,0:T(8,128)(2,1)S(1)}, bf16[4,24,2304]{2,1,0:T(8,128)(2,1)S(1)}, u32[]{:S(2)}, u32[]{:S(2)}) collective-permute-start(bf16[4,24,2304]{2,1,0:T(8,128)(2,1)S(1)} %get-tuple-element.263), channel_id=1, source_target_pairs={{0,16},{8,24},{16,0},{24,8},{1,17},{9,25},{17,1},{25,9},{2,18},{10... | collective-permute-start | bytes 1327112 | tf_op jit(solution)/shard_map/ppermute | solution.py:505
  537.6 22.1 %collective-permute-start.25 = (f32[18,768]{1,0:T(8,128)S(1)}, f32[18,768]{1,0:T(8,128)S(1)}, u32[]{:S(2)}, u32[]{:S(2)}) collective-permute-start(f32[18,768]{1,0:T(8,128)S(1)} %add.213), channel_id=1, source_target_pairs={{0,16},{8,24},{16,0},{24,8},{1,17},{9,25},{17,1},{25,9},{2,18},{10... | collective-permute-start | bytes 165896 | tf_op jit(solution)/shard_map/ppermute | solution.py:505
  539.6 20.1 %collective-permute-start.24 = (f32[18,768]{1,0:T(8,128)S(1)}, f32[18,768]{1,0:T(8,128)S(1)}, u32[]{:S(2)}, u32[]{:S(2)}) collective-permute-start(f32[18,768]{1,0:T(8,128)S(1)} %add.213), channel_id=1, source_target_pairs={{0,8},{8,0},{16,24},{24,16},{1,9},{9,1},{17,25},{25,17},{2,10},{10... | collective-permute-start | bytes 165896 | tf_op jit(solution)/shard_map/ppermute | solution.py:505
  560.0 17.4 %collective-permute-start.37 = (f32[18,768]{1,0:T(8,128)S(1)}, f32[18,768]{1,0:T(8,128)S(1)}, u32[]{:S(2)}, u32[]{:S(2)}) collective-permute-start(f32[18,768]{1,0:T(8,128)S(1)} %add_add_fusion.1), channel_id=1, source_target_pairs={{0,6},{2,4},{4,2},{6,0},{1,7},{3,5},{5,3},{7,1},{8,14},{10,12},{12... | collective-permute-start | bytes 165896 | tf_op jit(solution)/shard_map/ppermute | solution.py:505
  563.7 13.8 %collective-permute-start.36 = (f32[18,768]{1,0:T(8,128)S(1)}, f32[18,768]{1,0:T(8,128)S(1)}, u32[]{:S(2)}, u32[]{:S(2)}) collective-permute-start(f32[18,768]{1,0:T(8,128)S(1)} %add_add_fusion.1), channel_id=1, source_target_pairs={{0,4},{2,6},{4,0},{6,2},{1,5},{3,7},{5,1},{7,3},{8,12},{10,14},{12... | collective-permute-start | bytes 165896 | tf_op jit(solution)/shard_map/ppermute | solution.py:505
  563.9 13.6 %collective-permute-start.35 = (f32[18,768]{1,0:T(8,128)S(1)}, f32[18,768]{1,0:T(8,128)S(1)}, u32[]{:S(2)}, u32[]{:S(2)}) collective-permute-start(f32[18,768]{1,0:T(8,128)S(1)} %add_add_fusion.1), channel_id=1, source_target_pairs={{0,2},{2,0},{4,6},{6,4},{1,3},{3,1},{5,7},{7,5},{8,10},{10,8},{12,... | collective-permute-start | bytes 165896 | tf_op jit(solution)/shard_map/ppermute | solution.py:505
  564.5 15.5 %collective-permute-start.32 = (bf16[24,3840]{1,0:T(8,128)(2,1)S(1)}, bf16[24,3840]{1,0:T(8,128)(2,1)S(1)}, u32[]{:S(2)}, u32[]{:S(2)}) collective-permute-start(bf16[24,3840]{1,0:T(8,128)(2,1)S(1)} %get-tuple-element.268), channel_id=1, source_target_pairs={{0,2},{2,0},{4,6},{6,4},{1,3},{3,1},{5,7},{7,5},{8,10},{10,8},{12,... | collective-permute-start | bytes 552968 | tf_op jit(solution)/shard_map/ppermute | solution.py:505
  566.0 14.0 %collective-permute-start.33 = (bf16[24,3840]{1,0:T(8,128)(2,1)S(1)}, bf16[24,3840]{1,0:T(8,128)(2,1)S(1)}, u32[]{:S(2)}, u32[]{:S(2)}) collective-permute-start(bf16[24,3840]{1,0:T(8,128)(2,1)S(1)} %get-tuple-element.269), channel_id=1, source_target_pairs={{0,4},{2,6},{4,0},{6,2},{1,5},{3,7},{5,1},{7,3},{8,12},{10,14},{12... | collective-permute-start | bytes 552968 | tf_op jit(solution)/shard_map/ppermute | solution.py:505
  577.4 7.3 %collective-permute-start.34 = (bf16[24,3840]{1,0:T(8,128)(2,1)S(1)}, bf16[24,3840]{1,0:T(8,128)(2,1)S(1)}, u32[]{:S(2)}, u32[]{:S(2)}) collective-permute-start(bf16[24,3840]{1,0:T(8,128)(2,1)S(1)} %get-tuple-element.270), channel_id=1, source_target_pairs={{0,6},{2,4},{4,2},{6,0},{1,7},{3,5},{5,3},{7,1},{8,14},{10,12},{12... | collective-permute-start | bytes 552968 | tf_op jit(solution)/shard_map/ppermute | solution.py:505
  (37 other events, 385.9 us)
Sparse Core Ops, SparseCore 0:
  42.3 117.7 all-gather.1
  306.5 178.2 reduce-scatter.1

commit v4 on v3

--- a/solution.py
+++ b/solution.py
@@ -620,7 +620,7 @@
     clips = held // across if spread else held
     share = 1.0 if spread else 1.0 / across
     frames = frames_held * across
-    first_places = places // 32 * 16
+    first_places = -(-places // 32) * 16
     cuts = (slice(0, first_places), slice(first_places, places))
 
     def to_clips(array):

time: 605 us -> 601 us (level)
    ppermute x36, waiting for transfers between devices: 60.3 us -> 51.3 us  [exchange(): lax.ppermute(pieces[d], axis, [(i, i ^ d) for i in range(size)])]
where the time goes in v4:
time: 601 us; the launch traced here: 594 us
  Pallas kernels  306 us (51%)
  starting transfers between devices  86 us (14%)
  waiting for transfers between devices  81.4 us (14%)
  local copies, waits for them, and re-layouts  57.9 us (10%)
  other arithmetic  47.4 us (8%)
  between operations  15.8 us (3%)
    pallas_call x1, Pallas kernels, mlp(): pl.pallas_call(partial(mlp_kernel, rb=rb, chunks=chunks, frames=frames),...  75 us
    ppermute x36, waiting for transfers between devices, exchange(): lax.ppermute(pieces[d], axis, [(i, i ^ d) for i in range(size)])  51.3 us
    pallas_call x2, Pallas kernels, spatial_backward(): pl.pallas_call(partial(sb_kernel, fb=fb, real=real, head=head, scale=scal...  49.5 us
    pallas_call x2, Pallas kernels, temporal_forward(): call(partial(tf_kernel, fb=fb, nb=nb, frames=frames, slot=LANES // frames...  48.1 us
    ppermute x36, starting transfers between devices, exchange(): lax.ppermute(pieces[d], axis, [(i, i ^ d) for i in range(size)])  43 us
    pallas_call x2, Pallas kernels, temporal_backward(): call(partial(tb_kernel, fb=fb, nb=nb, frames=frames, slot=LANES // frames...  40.8 us
    pallas_call x3, Pallas kernels, weight_grads(): call(partial(wg_kernel, starts=starts, counts=counts, halves=halves, rows...  38.8 us
    all_to_all x4, waiting for transfers between devices, to_clips(): lax.all_to_all(array, 'context', split_axis=0, concat_axis=0, tiled=True)  29.8 us
  transfers between devices with their start and end apart: 46, of which 10 were waited for; matrix products, arithmetic and copies ran while one was open for 15% of the time, Pallas kernels for 39%

profile of v4, /device:TPU:0, one launch (start us, length us, event | category | flops | bytes accessed | tf_op | source)
XLA Modules:
  0.0 594.0 jit_solution(6047347914369087522)
XLA Ops:
  12.0 3.0 collective-permute-start.2
  15.1 2.6 collective-permute-start.1
  21.8 3.1 slice.136
  24.9 2.0 slice.135
  28.6 2.1 slice.137
  32.1 8.8 %collective-permute-done.1 = bf16[24,6912]{1,0:T(8,128)(2,1)S(1)} collective-permute-done((bf16[24,6912]{1,0:T(8,128)(2,1)S(1)}, bf16[24,6912]{1,0:T(8,128)(2,1)S(1)}, u32[]{:S(2)}, u32[]{:S(2)}) %collective-permute-start.1) | collective-permute-done | bytes 331808 | tf_op jit(solution)/shard_map/ppermute | solution.py:505
  42.2 8.6 %all-to-all-start = ((bf16[4,112,2,768]{3,2,1,0:T(2,128)(2,1)}), bf16[4,112,2,768]{3,2,1,0:T(2,128)(2,1)S(1)}, u32[]{:S(2)}, u32[]{:S(2)}) async-start(bf16[4,112,2,768]{3,2,1,0:T(2,128)(2,1)} %bitcast.185), calls=%async_computation | async-start | bytes 2752512 | tf_op jit(solution)/shard_map/all_to_all | solution.py:629
  55.2 18.3 %collective-permute-done.5 = bf16[4,24,3840]{2,1,0:T(8,128)(2,1)S(1)} collective-permute-done((bf16[4,24,3840]{2,1,0:T(8,128)(2,1)}, bf16[4,24,3840]{2,1,0:T(8,128)(2,1)S(1)}, u32[]{:S(2)}, u32[]{:S(2)}) %collective-permute-start.5) | collective-permute-done | bytes 737312 | tf_op jit(solution)/shard_map/ppermute | solution.py:505
  73.5 15.3 %all-to-all-done = bf16[4,112,2,768]{3,2,1,0:T(2,128)(2,1)S(1)} async-done(((bf16[4,112,2,768]{3,2,1,0:T(2,128)(2,1)}), bf16[4,112,2,768]{3,2,1,0:T(2,128)(2,1)S(1)}, u32[]{:S(2)}, u32[]{:S(2)}) %all-to-all-start) | async-done | bytes 1376288 | tf_op jit(solution)/shard_map/all_to_all | solution.py:629
  97.9 4.6 all-to-all-start.1
  102.5 2.6 copy.45
  105.1 2.2 select_bitcast_fusion.1
  107.9 3.0 copy.46
  110.8 25.5 %shard_map.271 = (bf16[896,768]{1,0:T(8,128)(2,1)}, bf16[896,2304]{1,0:T(8,128)(2,1)}, f32[896,128]{1,0:T(8,128)}, bf16[896,768]{1,0:T(8,128)(2,1)}, bf16[896,768]{1,0:T(8,128)(2,1)}, /*index=5*/f32[896,768]{1,0:T(8,128)}) custom-call(bf16[896,768]{1,0:T(8,128)(2,1)} %bitcast.204, f32[1,768]{1,0:T(1,128)} %get-tuple-element.302.gain_ref, ...), custom_call_target="tpu_custom_call" | custom-call | flops 22000001024 | tf_op jit(solution)/shard_map/pallas_call | solution.py:352
  140.6 3.3 all-to-all-done.1
  143.9 4.0 all-to-all-start.2
  151.7 22.7 %shard_map.272 = (bf16[768,768]{1,0:T(8,128)(2,1)}, bf16[768,2304]{1,0:T(8,128)(2,1)}, f32[768,128]{1,0:T(8,128)}, bf16[768,768]{1,0:T(8,128)(2,1)}, bf16[768,768]{1,0:T(8,128)(2,1)}, /*index=5*/f32[768,768]{1,0:T(8,128)}) custom-call(bf16[768,768]{1,0:T(8,128)(2,1)} %bitcast.209, f32[1,768]{1,0:T(1,128)} %get-tuple-element.302.gain_ref, ...), custom_call_target="tpu_custom_call" | custom-call | flops 22000001024 | tf_op jit(solution)/shard_map/pallas_call | solution.py:352
  174.4 11.3 %all-to-all-done.2 = bf16[4,112,2,768]{3,2,1,0:T(2,128)(2,1)S(1)} async-done(((bf16[4,112,2,768]{3,2,1,0:T(2,128)(2,1)}), bf16[4,112,2,768]{3,2,1,0:T(2,128)(2,1)S(1)}, u32[]{:S(2)}, u32[]{:S(2)}) %all-to-all-start.2) | async-done | bytes 1376288 | tf_op jit(solution)/shard_map/all_to_all | solution.py:629
  185.7 4.3 all-to-all-start.3
  193.6 2.6 copy.48
  196.2 25.5 %shard_map.273 = (bf16[1664,768]{1,0:T(8,128)(2,1)}, bf16[1664,2304]{1,0:T(8,128)(2,1)}, bf16[1664,768]{1,0:T(8,128)(2,1)}, f32[1664,768]{1,0:T(8,128)}, f32[1664,768]{1,0:T(8,128)}) custom-call(f32[896,768]{1,0:T(8,128)} %get-tuple-element.126.xa_ref, f32[768,768]{1,0:T(8,128)} %get-tuple-element.135.xb_ref, f32[1,768]{1,0:T(1,128)} %get-tuple-element.303.gain_ref, ...), custom_call_target="tpu_custom_call" | custom-call | flops 30000001024 | tf_op jit(solution)/shard_map/pallas_call | solution.py:207
  224.1 75.0 %shard_map.274 = (bf16[1664,768]{1,0:T(8,128)(2,1)}, f32[1664,768]{1,0:T(8,128)}, bf16[1664,768]{1,0:T(8,128)(2,1)}, bf16[16,2,96,1536]{3,2,1,0:T(8,128)(2,1)}, f32[1,3072]{1,0:T(1,128)}, /*index=5*/f32[8,768]{1,0:T(8,128)}) custom-call(f32[1664,768]{1,0:T(8,128)} %get-tuple-element.137.x_ref, bf16[896,768]{1,0:T(8,128)(2,1)} %bitcast.206, ...), custom_call_target="tpu_custom_call" | custom-call | flops 74999996416 | tf_op jit(solution)/shard_map/pallas_call | solution.py:114
  302.9 2.0 collective-permute-start.12
  304.9 2.4 collective-permute-start.13
  307.3 24.6 %shard_map.275 = (bf16[1664,2304]{1,0:T(8,128)(2,1)}, f32[896,768]{1,0:T(8,128)}, f32[768,768]{1,0:T(8,128)}, bf16[896,768]{1,0:T(8,128)(2,1)}, bf16[768,768]{1,0:T(8,128)(2,1)}, /*index=5*/f32[8,768]{1,0:T(8,128)}) custom-call(f32[1664,768]{1,0:T(8,128)} %get-tuple-element.143.g2_ref, bf16[1664,768]{1,0:T(8,128)(2,1)} %get-tuple-element.148.db_ref.refs_1_, ...), custom_call_target="tpu_custom_call" | custom-call | flops 24000000000 | tf_op jit(solution)/shard_map/pallas_call | solution.py:272
  331.9 25.0 %shard_map.276 = (bf16[1664,2304]{1,0:T(8,128)(2,1)}, f32[896,768]{1,0:T(8,128)}, f32[768,768]{1,0:T(8,128)}, bf16[896,768]{1,0:T(8,128)(2,1)}, bf16[768,768]{1,0:T(8,128)(2,1)}, /*index=5*/f32[8,768]{1,0:T(8,128)}) custom-call(f32[1664,768]{1,0:T(8,128)} %get-tuple-element.143.g2_ref,, ...), custom_call_target="tpu_custom_call", output_to_operand_aliasing={{0}: (7, {}), {1}: (8, {}), {2}: (9, {}), {3}: (10, {}), {4... | custom-call | flops 24000000000 | tf_op jit(solution)/shard_map/pallas_call | solution.py:272
  356.9 16.3 %shard_map.277 = (bf16[384,3072]{1,0:T(8,128)(2,1)}, bf16[384,3072]{1,0:T(8,128)(2,1)}) custom-call(s32[1,1]{1,0:T(1,128)} %bitcast.41.core_ref, bf16[1664,768]{1,0:T(8,128)(2,1)} %get-tuple-element.154.refs_0_, bf16[1664,768]{1,0:T(8,128)(2,1)} %get-tuple-element.148.db_ref.refs_1_, bf16[1664,2304]{1,0:T(8,128)(2,1)} %get-tuple-element.156.refs_2_, ...), custom_call_target="tpu_custom_call" | custom-call | flops 12000000000 | tf_op jit(solution)/shard_map/pallas_call | solution.py:489
  380.1 5.6 shard_map.278
  386.3 5.1 shard_map.279
  391.4 3.3 add_convert_fusion
  395.7 11.3 %shard_map.280 = (bf16[384,1536]{1,0:T(8,128)(2,1)}, bf16[384,1536]{1,0:T(8,128)(2,1)}) custom-call(s32[1,1]{1,0:T(1,128)} %bitcast.41.core_ref, bf16[896,768]{1,0:T(8,128)(2,1)} %get-tuple-element.162.refs_0_, bf16[768,768]{1,0:T(8,128)(2,1)} %get-tuple-element.167.refs_1_, bf16[896,768]{1,0:T(8,128)(2,1)} %get-tuple-element.168.refs_2_, ...), custom_call_target="tpu_custom_call" | custom-call | flops 6000000000 | tf_op jit(solution)/shard_map/pallas_call | solution.py:489
  411.8 22.1 %shard_map.281 = (bf16[896,2304]{1,0:T(8,128)(2,1)}, f32[8,768]{1,0:T(8,128)}) custom-call(bf16[896,768]{1,0:T(8,128)(2,1)} %get-tuple-element.174.do_ref, bf16[896,2304]{1,0:T(8,128)(2,1)} %get-tuple-element.175.qkv_ref, f32[896,128]{1,0:T(8,128)} %get-tuple-element.176.p_ref), custom_call_target="tpu_custom_call" | custom-call | flops 20000000000 | tf_op jit(solution)/shard_map/pallas_call | solution.py:429
  434.9 1.9 add_convert_fusion.2
  439.5 8.9 %shard_map.282 = (bf16[896,768]{1,0:T(8,128)(2,1)}, f32[8,768]{1,0:T(8,128)}) custom-call(bf16[896,2304]{1,0:T(8,128)(2,1)} %get-tuple-element.180.dqkv_ref.refs_2_, bf16[896,768]{1,0:T(8,128)(2,1)} %bitcast.205, f32[896,768]{1,0:T(8,128)} %get-tuple-element.181.g1_ref, f32[1,768]{1,0:T(1,128)} %get-tuple-element.302.gain_ref, bf16[768,3840]{1,0:T(8,128)(2,1)} %bitcast.182), custom_call_target="tpu_custom_call" | custom-call | flops 7000000000 | tf_op jit(solution)/shard_map/pallas_call | solution.py:444
  448.4 3.5 copy.74
  452.0 14.0 %all-to-all-start.4 = ((bf16[4,112,2,768]{3,2,1,0:T(2,128)(2,1)}), bf16[4,112,2,768]{3,2,1,0:T(2,128)(2,1)}, u32[]{:S(2)}, u32[]{:S(2)}) async-start(bf16[4,112,2,768]{3,2,1,0:T(2,128)(2,1)} %bitcast.186), calls=%async_computation.4 | async-start | bytes 2752512 | tf_op jit(solution)/shard_map/all_to_all | solution.py:644
  469.4 3.0 collective-permute-start.29
  473.9 18.8 %shard_map.283 = (bf16[768,2304]{1,0:T(8,128)(2,1)}, f32[8,768]{1,0:T(8,128)}) custom-call(bf16[768,768]{1,0:T(8,128)(2,1)} %get-tuple-element.186.do_ref, bf16[768,2304]{1,0:T(8,128)(2,1)} %get-tuple-element.187.qkv_ref, f32[768,128]{1,0:T(8,128)} %get-tuple-element.188.p_ref), custom_call_target="tpu_custom_call" | custom-call | flops 20000000000 | tf_op jit(solution)/shard_map/pallas_call | solution.py:429
  495.5 11.2 %shard_map.284 = (bf16[384,2304]{1,0:T(8,128)(2,1)}, bf16[384,2304]{1,0:T(8,128)(2,1)}) custom-call(s32[1,1]{1,0:T(1,128)} %bitcast.41.core_ref, bf16[896,768]{1,0:T(8,128)(2,1)} %get-tuple-element.141.refs_0_, bf16[768,768]{1,0:T(8,128)(2,1)} %get-tuple-element.142.refs_1_, bf16[896,2304]{1,0:T(8,128)(2,1)} %get-tuple-element.180.dqkv_ref.refs_2_, ...), custom_call_target="tpu_custom_call" | custom-call | flops 8999999488 | tf_op jit(solution)/shard_map/pallas_call | solution.py:489
  507.1 8.1 %shard_map.285 = (bf16[768,768]{1,0:T(8,128)(2,1)}, f32[8,768]{1,0:T(8,128)}) custom-call(bf16[768,2304]{1,0:T(8,128)(2,1)} %get-tuple-element.196.refs_3_.dqkv_ref, bf16[768,768]{1,0:T(8,128)(2,1)} %bitcast.210, f32[768,768]{1,0:T(8,128)} %get-tuple-element.197.g1_ref, f32[1,768]{1,0:T(1,128)} %get-tuple-element.302.gain_ref, bf16[768,3840]{1,0:T(8,128)(2,1)} %bitcast.183), custom_call_target="tpu_custom_call" | custom-call | flops 7000000000 | tf_op jit(solution)/shard_map/pallas_call | solution.py:444
  521.3 4.2 all-to-all-start.5
  536.5 18.1 %collective-permute-done.25 = f32[18,768]{1,0:T(8,128)S(1)} collective-permute-done((f32[18,768]{1,0:T(8,128)S(1)}, f32[18,768]{1,0:T(8,128)S(1)}, u32[]{:S(2)}, u32[]{:S(2)}) %collective-permute-start.25) | collective-permute-done | bytes 55328 | tf_op jit(solution)/shard_map/ppermute | solution.py:505
  554.9 3.8 collective-permute-start.37
  560.9 2.8 collective-permute-start.33
  563.7 2.5 fusion.7
  566.2 6.1 %maximum_bitcast_fusion = bf16[4,2,196,768]{3,1,2,0:T(2,128)(2,1)} fusion(bf16[1,196,2,768]{3,2,1,0:T(2,128)(2,1)S(1)} %get-tuple-element.253, bf16[1,196,2,768]{3,2,1,0:T(2,128)(2,1)S(1)} %get-tuple-element.252, bf16[1,196,2,768]{3,2,1,0:T(2,128)(2,1)S(1)} %get-tuple-element.251, bf16[1,196,2,768]{3,2,1,0:T(2,128)(2,1)S(1)} %get-tuple-element.250), kind=kLoop, calls=%fused_computation.7 | loop fusion | flops 3612672 | bytes 4816896 | tf_op jit(solution)/shard_map/transpose | solution.py:656
  574.9 4.7 collective-permute-done.34
  581.1 5.9 maximum_bitcast_fusion.1
  (239 shorter events, 93.0 us)
Async XLA Ops:
  7.2 216.9 %all-gather.2.cloned.1.call-start = ((), (), s32[]{:S(2)}) async-start(), calls=%async_computation.7 | async-start | bytes 9732096 | tf_op jit(solution)/shard_map/all_gather | solution.py:683
  12.0 20.0 %collective-permute-start.2 = (bf16[24,6912]{1,0:T(8,128)(2,1)S(1)}, bf16[24,6912]{1,0:T(8,128)(2,1)S(1)}, u32[]{:S(2)}, u32[]{:S(2)}) collective-permute-start(bf16[24,6912]{1,0:T(8,128)(2,1)S(1)} %convert_dynamic-update-slice_fusion), channel_id=1, source_target_pairs={{0,2},{2,0},{4,6},{6,4},{1,3},{3,1},{5,7},{7,5},{8,10},{10,8},{12,... | collective-permute-start | bytes 995336 | tf_op jit(solution)/shard_map/ppermute | solution.py:505
  15.1 25.8 %collective-permute-start.1 = (bf16[24,6912]{1,0:T(8,128)(2,1)S(1)}, bf16[24,6912]{1,0:T(8,128)(2,1)S(1)}, u32[]{:S(2)}, u32[]{:S(2)}) collective-permute-start(bf16[24,6912]{1,0:T(8,128)(2,1)S(1)} %convert_dynamic-update-slice_fusion), channel_id=1, source_target_pairs={{0,4},{2,6},{4,0},{6,2},{1,5},{3,7},{5,1},{7,3},{8,12},{10,14},{12... | collective-permute-start | bytes 995336 | tf_op jit(solution)/shard_map/ppermute | solution.py:505
  17.6 23.3 %collective-permute-start = (bf16[24,6912]{1,0:T(8,128)(2,1)S(1)}, bf16[24,6912]{1,0:T(8,128)(2,1)}, u32[]{:S(2)}, u32[]{:S(2)}) collective-permute-start(bf16[24,6912]{1,0:T(8,128)(2,1)S(1)} %convert_dynamic-update-slice_fusion), channel_id=1, source_target_pairs={{0,6},{2,4},{4,2},{6,0},{1,7},{3,5},{5,3},{7,1},{8,14},{10,12},{12... | collective-permute-start | bytes 995336 | tf_op jit(solution)/shard_map/ppermute | solution.py:505
  42.2 46.6 %all-to-all-start = ((bf16[4,112,2,768]{3,2,1,0:T(2,128)(2,1)}), bf16[4,112,2,768]{3,2,1,0:T(2,128)(2,1)S(1)}, u32[]{:S(2)}, u32[]{:S(2)}) async-start(bf16[4,112,2,768]{3,2,1,0:T(2,128)(2,1)} %bitcast.185), calls=%async_computation | async-start | bytes 2752512 | tf_op jit(solution)/shard_map/all_to_all | solution.py:629
  51.8 21.7 %collective-permute-start.5 = (bf16[4,24,3840]{2,1,0:T(8,128)(2,1)}, bf16[4,24,3840]{2,1,0:T(8,128)(2,1)S(1)}, u32[]{:S(2)}, u32[]{:S(2)}) collective-permute-start(bf16[4,24,3840]{2,1,0:T(8,128)(2,1)} %slice.179), channel_id=1, source_target_pairs={{0,8},{8,0},{16,24},{24,16},{1,9},{9,1},{17,25},{25,17},{2,10},{10... | collective-permute-start | bytes 2211848 | tf_op jit(solution)/shard_map/ppermute | solution.py:505
  53.2 35.5 %collective-permute-start.4 = (bf16[4,24,3840]{2,1,0:T(8,128)(2,1)}, bf16[4,24,3840]{2,1,0:T(8,128)(2,1)}, u32[]{:S(2)}, u32[]{:S(2)}) collective-permute-start(bf16[4,24,3840]{2,1,0:T(8,128)(2,1)} %slice.179), channel_id=1, source_target_pairs={{0,16},{8,24},{16,0},{24,8},{1,17},{9,25},{17,1},{25,9},{2,18},{10... | collective-permute-start | bytes 2211848 | tf_op jit(solution)/shard_map/ppermute | solution.py:505
  54.8 35.1 %collective-permute-start.3 = (bf16[4,24,3840]{2,1,0:T(8,128)(2,1)}, bf16[4,24,3840]{2,1,0:T(8,128)(2,1)}, u32[]{:S(2)}, u32[]{:S(2)}) collective-permute-start(bf16[4,24,3840]{2,1,0:T(8,128)(2,1)} %slice.179), channel_id=1, source_target_pairs={{0,24},{8,16},{16,8},{24,0},{1,25},{9,17},{17,9},{25,1},{2,26},{10... | collective-permute-start | bytes 2211848 | tf_op jit(solution)/shard_map/ppermute | solution.py:505
  93.5 11.6 %collective-permute-start.6 = (bf16[4,4,24,3840]{3,2,1,0:T(8,128)(2,1)}, bf16[4,4,24,3840]{3,2,1,0:T(8,128)(2,1)}, u32[]{:S(2)}, u32[]{:S(2)}) collective-permute-start(bf16[4,4,24,3840]{3,2,1,0:T(8,128)(2,1)} %pad_maximum_fusion.2), channel_id=1, source_target_pairs={{0,1},{1,0},{2,3},{3,2},{4,5},{5,4},{6,7},{7,6},{8,9},{9,8},{10,11... | collective-permute-start | bytes 8847368 | tf_op jit(solution)/shard_map/ppermute | solution.py:505
  94.4 41.9 %collective-permute-start.9 = (bf16[4,24,3072]{2,1,0:T(8,128)(2,1)}, bf16[4,24,3072]{2,1,0:T(8,128)(2,1)S(1)}, u32[]{:S(2)}, u32[]{:S(2)}) collective-permute-start(bf16[4,24,3072]{2,1,0:T(8,128)(2,1)} %slice.180), channel_id=1, source_target_pairs={{0,8},{8,0},{16,24},{24,16},{1,9},{9,1},{17,25},{25,17},{2,10},{10... | collective-permute-start | bytes 1769480 | tf_op jit(solution)/shard_map/ppermute | solution.py:505
  95.9 40.4 %collective-permute-start.8 = (bf16[4,24,3072]{2,1,0:T(8,128)(2,1)}, bf16[4,24,3072]{2,1,0:T(8,128)(2,1)}, u32[]{:S(2)}, u32[]{:S(2)}) collective-permute-start(bf16[4,24,3072]{2,1,0:T(8,128)(2,1)} %slice.180), channel_id=1, source_target_pairs={{0,16},{8,24},{16,0},{24,8},{1,17},{9,25},{17,1},{25,9},{2,18},{10... | collective-permute-start | bytes 1769480 | tf_op jit(solution)/shard_map/ppermute | solution.py:505
  97.4 39.7 %collective-permute-start.7 = (bf16[4,24,3072]{2,1,0:T(8,128)(2,1)}, bf16[4,24,3072]{2,1,0:T(8,128)(2,1)}, u32[]{:S(2)}, u32[]{:S(2)}) collective-permute-start(bf16[4,24,3072]{2,1,0:T(8,128)(2,1)} %slice.180), channel_id=1, source_target_pairs={{0,24},{8,16},{16,8},{24,0},{1,25},{9,17},{17,9},{25,1},{2,26},{10... | collective-permute-start | bytes 1769480 | tf_op jit(solution)/shard_map/ppermute | solution.py:505
  97.9 46.1 %all-to-all-start.1 = ((bf16[4,84,2,768]{3,2,1,0:T(2,128)(2,1)}), bf16[4,84,2,768]{3,2,1,0:T(2,128)(2,1)}, u32[]{:S(2)}, u32[]{:S(2)}) async-start(bf16[4,84,2,768]{3,2,1,0:T(2,128)(2,1)} %bitcast.199), calls=%async_computation.1 | async-start | bytes 2064384 | tf_op jit(solution)/shard_map/all_to_all | solution.py:629
  140.6 50.6 %collective-permute-start.10 = (bf16[4,4,24,3072]{3,2,1,0:T(8,128)(2,1)}, bf16[4,4,24,3072]{3,2,1,0:T(8,128)(2,1)}, u32[]{:S(2)}, u32[]{:S(2)}) collective-permute-start(bf16[4,4,24,3072]{3,2,1,0:T(8,128)(2,1)} %pad_maximum_fusion.3), channel_id=1, source_target_pairs={{0,1},{1,0},{2,3},{3,2},{4,5},{5,4},{6,7},{7,6},{8,9},{9,8},{10,11... | collective-permute-start | bytes 7077896 | tf_op jit(solution)/shard_map/ppermute | solution.py:505
  143.9 41.7 %all-to-all-start.2 = ((bf16[4,112,2,768]{3,2,1,0:T(2,128)(2,1)}), bf16[4,112,2,768]{3,2,1,0:T(2,128)(2,1)S(1)}, u32[]{:S(2)}, u32[]{:S(2)}) async-start(bf16[4,112,2,768]{3,2,1,0:T(2,128)(2,1)} %bitcast.26), calls=%async_computation.2 | async-start | bytes 2752512 | tf_op jit(solution)/shard_map/all_to_all | solution.py:629
  185.7 36.0 %all-to-all-start.3 = ((bf16[4,84,2,768]{3,2,1,0:T(2,128)(2,1)}), bf16[4,84,2,768]{3,2,1,0:T(2,128)(2,1)}, u32[]{:S(2)}, u32[]{:S(2)}) async-start(bf16[4,84,2,768]{3,2,1,0:T(2,128)(2,1)} %bitcast.198), calls=%async_computation.3 | async-start | bytes 2064384 | tf_op jit(solution)/shard_map/all_to_all | solution.py:629
  189.9 317.0 %reduce-scatter.2.cloned.1.call-start = ((), (), s32[]{:S(2)}) async-start(), calls=%async_computation.8 | async-start | bytes 9732096 | tf_op jit(solution)/shard_map/reduce_scatter | solution.py:720
  302.9 28.9 %collective-permute-start.12 = (bf16[196,2,768]{2,1,0:T(2,128)(2,1)S(1)}, bf16[196,2,768]{2,1,0:T(2,128)(2,1)S(1)}, u32[]{:S(2)}, u32[]{:S(2)}) collective-permute-start(bf16[196,2,768]{2,1,0:T(2,128)(2,1)S(1)} %bitcast.216), channel_id=1, source_target_pairs={{0,2},{2,0},{4,6},{6,4},{1,3},{3,1},{5,7},{7,5},{8,10},{10,8},{12,... | collective-permute-start | bytes 1806344 | tf_op jit(solution)/shard_map/ppermute | solution.py:505
  304.9 52.0 %collective-permute-start.13 = (bf16[196,2,768]{2,1,0:T(2,128)(2,1)S(1)}, bf16[196,2,768]{2,1,0:T(2,128)(2,1)S(1)}, u32[]{:S(2)}, u32[]{:S(2)}) collective-permute-start(bf16[196,2,768]{2,1,0:T(2,128)(2,1)S(1)} %bitcast.215), channel_id=1, source_target_pairs={{0,4},{2,6},{4,0},{6,2},{1,5},{3,7},{5,1},{7,3},{8,12},{10,14},{12... | collective-permute-start | bytes 1806344 | tf_op jit(solution)/shard_map/ppermute | solution.py:505
  373.2 18.2 %collective-permute-start.14 = (bf16[16,24,3072]{2,1,0:T(8,128)(2,1)}, bf16[16,24,3072]{2,1,0:T(8,128)(2,1)}, u32[]{:S(2)}, u32[]{:S(2)}) collective-permute-start(bf16[16,24,3072]{2,1,0:T(8,128)(2,1)} %bitcast.222), channel_id=1, source_target_pairs={{0,1},{1,0},{2,3},{3,2},{4,5},{5,4},{6,7},{7,6},{8,9},{9,8},{10,11... | collective-permute-start | bytes 7077896 | tf_op jit(solution)/shard_map/ppermute | solution.py:505
  377.2 18.5 %collective-permute-start.11 = (bf16[196,2,768]{2,1,0:T(2,128)(2,1)}, bf16[196,2,768]{2,1,0:T(2,128)(2,1)S(1)}, u32[]{:S(2)}, u32[]{:S(2)}) collective-permute-start(bf16[196,2,768]{2,1,0:T(2,128)(2,1)} %bitcast.164), channel_id=1, source_target_pairs={{0,6},{2,4},{4,2},{6,0},{1,7},{3,5},{5,3},{7,1},{8,14},{10,12},{12... | collective-permute-start | bytes 1806344 | tf_op jit(solution)/shard_map/ppermute | solution.py:505
  407.0 26.9 %collective-permute-start.15 = (bf16[16,24,1536]{2,1,0:T(8,128)(2,1)}, bf16[16,24,1536]{2,1,0:T(8,128)(2,1)S(1)}, u32[]{:S(2)}, u32[]{:S(2)}) collective-permute-start(bf16[16,24,1536]{2,1,0:T(8,128)(2,1)} %bitcast.224), channel_id=1, source_target_pairs={{0,1},{1,0},{2,3},{3,2},{4,5},{5,4},{6,7},{7,6},{8,9},{9,8},{10,11... | collective-permute-start | bytes 3538952 | tf_op jit(solution)/shard_map/ppermute | solution.py:505
  408.3 57.7 %collective-permute-start.16 = (bf16[4,24,3072]{2,1,0:T(8,128)(2,1)}, bf16[4,24,3072]{2,1,0:T(8,128)(2,1)}, u32[]{:S(2)}, u32[]{:S(2)}) collective-permute-start(bf16[4,24,3072]{2,1,0:T(8,128)(2,1)} %get-tuple-element.254), channel_id=1, source_target_pairs={{0,8},{8,0},{16,24},{24,16},{1,9},{9,1},{17,25},{25,17},{2,10},{10... | collective-permute-start | bytes 1769480 | tf_op jit(solution)/shard_map/ppermute | solution.py:505
  409.9 56.1 %collective-permute-start.18 = (bf16[4,24,3072]{2,1,0:T(8,128)(2,1)}, bf16[4,24,3072]{2,1,0:T(8,128)(2,1)}, u32[]{:S(2)}, u32[]{:S(2)}) collective-permute-start(bf16[4,24,3072]{2,1,0:T(8,128)(2,1)} %get-tuple-element.255), channel_id=1, source_target_pairs={{0,24},{8,16},{16,8},{24,0},{1,25},{9,17},{17,9},{25,1},{2,26},{10... | collective-permute-start | bytes 1769480 | tf_op jit(solution)/shard_map/ppermute | solution.py:505
  411.2 54.7 %collective-permute-start.17 = (bf16[4,24,3072]{2,1,0:T(8,128)(2,1)}, bf16[4,24,3072]{2,1,0:T(8,128)(2,1)}, u32[]{:S(2)}, u32[]{:S(2)}) collective-permute-start(bf16[4,24,3072]{2,1,0:T(8,128)(2,1)} %get-tuple-element.256), channel_id=1, source_target_pairs={{0,16},{8,24},{16,0},{24,8},{1,17},{9,25},{17,1},{25,9},{2,18},{10... | collective-permute-start | bytes 1769480 | tf_op jit(solution)/shard_map/ppermute | solution.py:505
  437.8 54.9 %collective-permute-start.19 = (bf16[2,4,24,1536]{3,2,1,0:T(8,128)(2,1)}, bf16[2,4,24,1536]{3,2,1,0:T(8,128)(2,1)}, u32[]{:S(2)}, u32[]{:S(2)}) collective-permute-start(bf16[2,4,24,1536]{3,2,1,0:T(8,128)(2,1)} %dynamic-slice_bitcast_fusion), channel_id=1, source_target_pairs={{0,8},{8,0},{16,24},{24,16},{1,9},{9,1},{17,25},{25,17},{2,10},{10... | collective-permute-start | bytes 1769480 | tf_op jit(solution)/shard_map/ppermute | solution.py:525
  452.0 55.0 %all-to-all-start.4 = ((bf16[4,112,2,768]{3,2,1,0:T(2,128)(2,1)}), bf16[4,112,2,768]{3,2,1,0:T(2,128)(2,1)}, u32[]{:S(2)}, u32[]{:S(2)}) async-start(bf16[4,112,2,768]{3,2,1,0:T(2,128)(2,1)} %bitcast.186), calls=%async_computation.4 | async-start | bytes 2752512 | tf_op jit(solution)/shard_map/all_to_all | solution.py:644
  469.4 45.8 %collective-permute-start.29 = (bf16[24,3072]{1,0:T(8,128)(2,1)}, bf16[24,3072]{1,0:T(8,128)(2,1)S(1)}, u32[]{:S(2)}, u32[]{:S(2)}) collective-permute-start(bf16[24,3072]{1,0:T(8,128)(2,1)} %get-tuple-element.271), channel_id=1, source_target_pairs={{0,2},{2,0},{4,6},{6,4},{1,3},{3,1},{5,7},{7,5},{8,10},{10,8},{12,... | collective-permute-start | bytes 442376 | tf_op jit(solution)/shard_map/ppermute | solution.py:505
  472.4 42.8 %collective-permute-start.31 = (bf16[24,3072]{1,0:T(8,128)(2,1)}, bf16[24,3072]{1,0:T(8,128)(2,1)S(1)}, u32[]{:S(2)}, u32[]{:S(2)}) collective-permute-start(bf16[24,3072]{1,0:T(8,128)(2,1)} %get-tuple-element.272), channel_id=1, source_target_pairs={{0,6},{2,4},{4,2},{6,0},{1,7},{3,5},{5,3},{7,1},{8,14},{10,12},{12... | collective-permute-start | bytes 442376 | tf_op jit(solution)/shard_map/ppermute | solution.py:505
  473.8 41.4 %collective-permute-start.30 = (bf16[24,3072]{1,0:T(8,128)(2,1)}, bf16[24,3072]{1,0:T(8,128)(2,1)}, u32[]{:S(2)}, u32[]{:S(2)}) collective-permute-start(bf16[24,3072]{1,0:T(8,128)(2,1)} %get-tuple-element.273), channel_id=1, source_target_pairs={{0,4},{2,6},{4,0},{6,2},{1,5},{3,7},{5,1},{7,3},{8,12},{10,14},{12... | collective-permute-start | bytes 442376 | tf_op jit(solution)/shard_map/ppermute | solution.py:505
  493.9 12.7 %collective-permute-start.21 = (bf16[1,4,24,1536]{3,2,1,0:T(8,128)(2,1)S(1)}, bf16[1,4,24,1536]{3,2,1,0:T(8,128)(2,1)S(1)}, u32[]{:S(2)}, u32[]{:S(2)}) collective-permute-start(bf16[1,4,24,1536]{3,2,1,0:T(8,128)(2,1)S(1)} %constant_dynamic-slice_fusion.1), channel_id=1, source_target_pairs={{0,16},{8,24},{16,0},{24,8},{1,17},{9,25},{17,1},{25,9},{2,18},{10... | collective-permute-start | bytes 884744 | tf_op jit(solution)/shard_map/ppermute | solution.py:525
  506.7 18.8 %collective-permute-start.20 = (bf16[16,24,2304]{2,1,0:T(8,128)(2,1)}, bf16[16,24,2304]{2,1,0:T(8,128)(2,1)}, u32[]{:S(2)}, u32[]{:S(2)}) collective-permute-start(bf16[16,24,2304]{2,1,0:T(8,128)(2,1)} %bitcast.223), channel_id=1, source_target_pairs={{0,1},{1,0},{2,3},{3,2},{4,5},{5,4},{6,7},{7,6},{8,9},{9,8},{10,11... | collective-permute-start | bytes 5308424 | tf_op jit(solution)/shard_map/ppermute | solution.py:505
  518.3 9.1 %collective-permute-start.23 = (f32[18,768]{1,0:T(8,128)S(1)}, f32[18,768]{1,0:T(8,128)}, u32[]{:S(2)}, u32[]{:S(2)}) collective-permute-start(f32[18,768]{1,0:T(8,128)S(1)} %concatenate.23), channel_id=1, source_target_pairs={{0,1},{1,0},{2,3},{3,2},{4,5},{5,4},{6,7},{7,6},{8,9},{9,8},{10,11... | collective-permute-start | bytes 165896 | tf_op jit(solution)/shard_map/ppermute | solution.py:505
  521.3 59.9 %all-to-all-start.5 = ((bf16[4,84,2,768]{3,2,1,0:T(2,128)(2,1)}), bf16[4,84,2,768]{3,2,1,0:T(2,128)(2,1)S(1)}, u32[]{:S(2)}, u32[]{:S(2)}) async-start(bf16[4,84,2,768]{3,2,1,0:T(2,128)(2,1)} %bitcast.160), calls=%async_computation.6 | async-start | bytes 2064384 | tf_op jit(solution)/shard_map/all_to_all | solution.py:644
  528.3 6.1 %collective-permute-start.26 = (f32[18,768]{1,0:T(8,128)S(1)}, f32[18,768]{1,0:T(8,128)S(1)}, u32[]{:S(2)}, u32[]{:S(2)}) collective-permute-start(f32[18,768]{1,0:T(8,128)S(1)} %add.213), channel_id=1, source_target_pairs={{0,24},{8,16},{16,8},{24,0},{1,25},{9,17},{17,9},{25,1},{2,26},{10... | collective-permute-start | bytes 165896 | tf_op jit(solution)/shard_map/ppermute | solution.py:505
  529.5 25.1 %collective-permute-start.22 = (bf16[4,24,2304]{2,1,0:T(8,128)(2,1)S(1)}, bf16[4,24,2304]{2,1,0:T(8,128)(2,1)S(1)}, u32[]{:S(2)}, u32[]{:S(2)}) collective-permute-start(bf16[4,24,2304]{2,1,0:T(8,128)(2,1)S(1)} %get-tuple-element.261), channel_id=1, source_target_pairs={{0,8},{8,0},{16,24},{24,16},{1,9},{9,1},{17,25},{25,17},{2,10},{10... | collective-permute-start | bytes 1327112 | tf_op jit(solution)/shard_map/ppermute | solution.py:505
  530.8 23.8 %collective-permute-start.28 = (bf16[4,24,2304]{2,1,0:T(8,128)(2,1)S(1)}, bf16[4,24,2304]{2,1,0:T(8,128)(2,1)S(1)}, u32[]{:S(2)}, u32[]{:S(2)}) collective-permute-start(bf16[4,24,2304]{2,1,0:T(8,128)(2,1)S(1)} %get-tuple-element.262), channel_id=1, source_target_pairs={{0,24},{8,16},{16,8},{24,0},{1,25},{9,17},{17,9},{25,1},{2,26},{10... | collective-permute-start | bytes 1327112 | tf_op jit(solution)/shard_map/ppermute | solution.py:505
  532.0 31.7 %copy-start.18 = (bf16[196,2,768]{2,1,0:T(2,128)(2,1)S(1)}, bf16[196,2,768]{2,1,0:T(2,128)(2,1)}, u32[]{:S(2)}) copy-start(bf16[196,2,768]{2,1,0:T(2,128)(2,1)} %copy-done.17) | copy-start | bytes 1806340
  532.0 31.7 %copy-start.20 = (bf16[196,2,768]{2,1,0:T(2,128)(2,1)S(1)}, bf16[196,2,768]{2,1,0:T(2,128)(2,1)}, u32[]{:S(2)}) copy-start(bf16[196,2,768]{2,1,0:T(2,128)(2,1)} %copy-done.19) | copy-start | bytes 1806340
  532.0 22.6 %collective-permute-start.27 = (bf16[4,24,2304]{2,1,0:T(8,128)(2,1)S(1)}, bf16[4,24,2304]{2,1,0:T(8,128)(2,1)S(1)}, u32[]{:S(2)}, u32[]{:S(2)}) collective-permute-start(bf16[4,24,2304]{2,1,0:T(8,128)(2,1)S(1)} %get-tuple-element.263), channel_id=1, source_target_pairs={{0,16},{8,24},{16,0},{24,8},{1,17},{9,25},{17,1},{25,9},{2,18},{10... | collective-permute-start | bytes 1327112 | tf_op jit(solution)/shard_map/ppermute | solution.py:505
  533.1 21.5 %collective-permute-start.25 = (f32[18,768]{1,0:T(8,128)S(1)}, f32[18,768]{1,0:T(8,128)S(1)}, u32[]{:S(2)}, u32[]{:S(2)}) collective-permute-start(f32[18,768]{1,0:T(8,128)S(1)} %add.213), channel_id=1, source_target_pairs={{0,16},{8,24},{16,0},{24,8},{1,17},{9,25},{17,1},{25,9},{2,18},{10... | collective-permute-start | bytes 165896 | tf_op jit(solution)/shard_map/ppermute | solution.py:505
  534.4 20.1 %collective-permute-start.24 = (f32[18,768]{1,0:T(8,128)S(1)}, f32[18,768]{1,0:T(8,128)S(1)}, u32[]{:S(2)}, u32[]{:S(2)}) collective-permute-start(f32[18,768]{1,0:T(8,128)S(1)} %add.213), channel_id=1, source_target_pairs={{0,8},{8,0},{16,24},{24,16},{1,9},{9,1},{17,25},{25,17},{2,10},{10... | collective-permute-start | bytes 165896 | tf_op jit(solution)/shard_map/ppermute | solution.py:505
  554.9 17.4 %collective-permute-start.37 = (f32[18,768]{1,0:T(8,128)S(1)}, f32[18,768]{1,0:T(8,128)S(1)}, u32[]{:S(2)}, u32[]{:S(2)}) collective-permute-start(f32[18,768]{1,0:T(8,128)S(1)} %add_add_fusion.1), channel_id=1, source_target_pairs={{0,6},{2,4},{4,2},{6,0},{1,7},{3,5},{5,3},{7,1},{8,14},{10,12},{12... | collective-permute-start | bytes 165896 | tf_op jit(solution)/shard_map/ppermute | solution.py:505
  558.6 13.8 %collective-permute-start.36 = (f32[18,768]{1,0:T(8,128)S(1)}, f32[18,768]{1,0:T(8,128)S(1)}, u32[]{:S(2)}, u32[]{:S(2)}) collective-permute-start(f32[18,768]{1,0:T(8,128)S(1)} %add_add_fusion.1), channel_id=1, source_target_pairs={{0,4},{2,6},{4,0},{6,2},{1,5},{3,7},{5,1},{7,3},{8,12},{10,14},{12... | collective-permute-start | bytes 165896 | tf_op jit(solution)/shard_map/ppermute | solution.py:505
  558.7 13.7 %collective-permute-start.35 = (f32[18,768]{1,0:T(8,128)S(1)}, f32[18,768]{1,0:T(8,128)S(1)}, u32[]{:S(2)}, u32[]{:S(2)}) collective-permute-start(f32[18,768]{1,0:T(8,128)S(1)} %add_add_fusion.1), channel_id=1, source_target_pairs={{0,2},{2,0},{4,6},{6,4},{1,3},{3,1},{5,7},{7,5},{8,10},{10,8},{12,... | collective-permute-start | bytes 165896 | tf_op jit(solution)/shard_map/ppermute | solution.py:505
  559.4 15.5 %collective-permute-start.32 = (bf16[24,3840]{1,0:T(8,128)(2,1)S(1)}, bf16[24,3840]{1,0:T(8,128)(2,1)S(1)}, u32[]{:S(2)}, u32[]{:S(2)}) collective-permute-start(bf16[24,3840]{1,0:T(8,128)(2,1)S(1)} %get-tuple-element.268), channel_id=1, source_target_pairs={{0,2},{2,0},{4,6},{6,4},{1,3},{3,1},{5,7},{7,5},{8,10},{10,8},{12,... | collective-permute-start | bytes 552968 | tf_op jit(solution)/shard_map/ppermute | solution.py:505
  560.9 14.0 %collective-permute-start.33 = (bf16[24,3840]{1,0:T(8,128)(2,1)S(1)}, bf16[24,3840]{1,0:T(8,128)(2,1)S(1)}, u32[]{:S(2)}, u32[]{:S(2)}) collective-permute-start(bf16[24,3840]{1,0:T(8,128)(2,1)S(1)} %get-tuple-element.269), channel_id=1, source_target_pairs={{0,4},{2,6},{4,0},{6,2},{1,5},{3,7},{5,1},{7,3},{8,12},{10,14},{12... | collective-permute-start | bytes 552968 | tf_op jit(solution)/shard_map/ppermute | solution.py:505
  572.3 7.3 %collective-permute-start.34 = (bf16[24,3840]{1,0:T(8,128)(2,1)S(1)}, bf16[24,3840]{1,0:T(8,128)(2,1)S(1)}, u32[]{:S(2)}, u32[]{:S(2)}) collective-permute-start(bf16[24,3840]{1,0:T(8,128)(2,1)S(1)} %get-tuple-element.270), channel_id=1, source_target_pairs={{0,6},{2,4},{4,2},{6,0},{1,7},{3,5},{5,3},{7,1},{8,14},{10,12},{12... | collective-permute-start | bytes 552968 | tf_op jit(solution)/shard_map/ppermute | solution.py:505
  (40 other events, 387.7 us)
Sparse Core Ops, SparseCore 0:
  42.3 126.9 all-gather.1
  301.1 178.6 reduce-scatter.1

commit v5 on v4

--- a/solution.py
+++ b/solution.py
@@ -680,10 +680,10 @@
     first = collect(jnp.concatenate((t_own, s_own), axis=1), "context", hold=early)
     t_first, s_first = first[..., : t_own.shape[1]], first[..., t_own.shape[1] :]
     rows_a = to_clips(after(clip_parts[0], first))
-    mlp_all = lax.all_gather(after(mlp_own, first), ALL, axis=0, tiled=True)
-    mlp_all = mlp_all.reshape(-1, halves, 2 * in_rows, in_cols)
     t_chips = collect(t_first, "shard", hold=(rows_a,))
     t_all = collect(t_chips, "tensor", 2).reshape(-1, t_own.shape[1])
+    mlp_all = lax.all_gather(after(mlp_own, t_chips), ALL, axis=0, tiled=True)
+    mlp_all = mlp_all.reshape(-1, halves, 2 * in_rows, in_cols)
     rows_b = to_clips(after(clip_parts[1], rows_a))
     pull_a = to_clips(after(pull_parts[0], rows_b))
     pull_b = to_clips(after(pull_parts[1], pull_a))

time: 601 us -> 618 us (1.028)
  waiting for transfers between devices: 81.4 us -> 96.5 us
    all_to_all x4, waiting for transfers between devices: 29.8 us -> 44.2 us  [to_clips(): lax.all_to_all(array, 'context', split_axis=0, concat_axis=0, tiled=True)]
  transfers between devices with their start and end apart: 46 -> 46, of which waited for: 10 -> 10; matrix products, arithmetic and copies ran while one was open for 15% -> 14% of each run, Pallas kernels for 39% -> 38%
where the time goes in v5:
time: 618 us; the launch traced here: 612 us
  Pallas kernels  305 us (49%)
  waiting for transfers between devices  96.5 us (16%)
  starting transfers between devices  87.8 us (14%)
  local copies, waits for them, and re-layouts  56.8 us (9%)
  other arithmetic  49.3 us (8%)
  between operations  15.8 us (3%)
    pallas_call x1, Pallas kernels, mlp(): pl.pallas_call(partial(mlp_kernel, rb=rb, chunks=chunks, frames=frames),...  75 us
    ppermute x36, waiting for transfers between devices, exchange(): lax.ppermute(pieces[d], axis, [(i, i ^ d) for i in range(size)])  52.1 us
    pallas_call x2, Pallas kernels, spatial_backward(): pl.pallas_call(partial(sb_kernel, fb=fb, real=real, head=head, scale=scal...  49.5 us
    pallas_call x2, Pallas kernels, temporal_forward(): call(partial(tf_kernel, fb=fb, nb=nb, frames=frames, slot=LANES // frames...  48.1 us
    all_to_all x4, waiting for transfers between devices, to_clips(): lax.all_to_all(array, 'context', split_axis=0, concat_axis=0, tiled=True)  44.2 us
    ppermute x36, starting transfers between devices, exchange(): lax.ppermute(pieces[d], axis, [(i, i ^ d) for i in range(size)])  42.6 us
    pallas_call x2, Pallas kernels, temporal_backward(): call(partial(tb_kernel, fb=fb, nb=nb, frames=frames, slot=LANES // frames...  40.8 us
    pallas_call x3, Pallas kernels, weight_grads(): call(partial(wg_kernel, starts=starts, counts=counts, halves=halves, rows...  38.8 us
  transfers between devices with their start and end apart: 46, of which 10 were waited for; matrix products, arithmetic and copies ran while one was open for 14% of the time, Pallas kernels for 38%

profile of v5, /device:TPU:0, one launch (start us, length us, event | category | flops | bytes accessed | tf_op | source)
XLA Modules:
  0.0 611.5 jit_solution(2796489847298050490)
XLA Ops:
  12.0 3.0 collective-permute-start.2
  15.0 2.6 collective-permute-start.1
  20.3 3.1 slice.136
  23.4 2.0 slice.135
  27.1 2.1 slice.137
  30.4 10.5 %collective-permute-done.1 = bf16[24,6912]{1,0:T(8,128)(2,1)S(1)} collective-permute-done((bf16[24,6912]{1,0:T(8,128)(2,1)S(1)}, bf16[24,6912]{1,0:T(8,128)(2,1)S(1)}, u32[]{:S(2)}, u32[]{:S(2)}) %collective-permute-start.1) | collective-permute-done | bytes 331808 | tf_op jit(solution)/shard_map/ppermute | solution.py:505
  42.1 8.6 %all-to-all-start = ((bf16[4,112,2,768]{3,2,1,0:T(2,128)(2,1)}), bf16[4,112,2,768]{3,2,1,0:T(2,128)(2,1)S(1)}, u32[]{:S(2)}, u32[]{:S(2)}) async-start(bf16[4,112,2,768]{3,2,1,0:T(2,128)(2,1)} %bitcast.185), calls=%async_computation | async-start | bytes 2752512 | tf_op jit(solution)/shard_map/all_to_all | solution.py:629
  57.9 13.4 %collective-permute-done.5 = bf16[4,24,3840]{2,1,0:T(8,128)(2,1)S(1)} collective-permute-done((bf16[4,24,3840]{2,1,0:T(8,128)(2,1)}, bf16[4,24,3840]{2,1,0:T(8,128)(2,1)S(1)}, u32[]{:S(2)}, u32[]{:S(2)}) %collective-permute-start.5) | collective-permute-done | bytes 737312 | tf_op jit(solution)/shard_map/ppermute | solution.py:505
  71.3 11.1 %all-to-all-done = bf16[4,112,2,768]{3,2,1,0:T(2,128)(2,1)S(1)} async-done(((bf16[4,112,2,768]{3,2,1,0:T(2,128)(2,1)}), bf16[4,112,2,768]{3,2,1,0:T(2,128)(2,1)S(1)}, u32[]{:S(2)}, u32[]{:S(2)}) %all-to-all-start) | async-done | bytes 1376288 | tf_op jit(solution)/shard_map/all_to_all | solution.py:629
  82.4 3.4 collective-permute-done.4
  94.8 5.2 all-to-all-start.1
  99.9 2.6 copy.45
  102.6 2.2 select_bitcast_fusion.1
  105.3 3.0 copy.46
  108.3 25.4 %shard_map.271 = (bf16[896,768]{1,0:T(8,128)(2,1)}, bf16[896,2304]{1,0:T(8,128)(2,1)}, f32[896,128]{1,0:T(8,128)}, bf16[896,768]{1,0:T(8,128)(2,1)}, bf16[896,768]{1,0:T(8,128)(2,1)}, /*index=5*/f32[896,768]{1,0:T(8,128)}) custom-call(bf16[896,768]{1,0:T(8,128)(2,1)} %bitcast.204, f32[1,768]{1,0:T(1,128)} %get-tuple-element.302.gain_ref, ...), custom_call_target="tpu_custom_call" | custom-call | flops 22000001024 | tf_op jit(solution)/shard_map/pallas_call | solution.py:352
  138.1 5.6 all-to-all-start.2
  147.5 22.6 %shard_map.272 = (bf16[768,768]{1,0:T(8,128)(2,1)}, bf16[768,2304]{1,0:T(8,128)(2,1)}, f32[768,128]{1,0:T(8,128)}, bf16[768,768]{1,0:T(8,128)(2,1)}, bf16[768,768]{1,0:T(8,128)(2,1)}, /*index=5*/f32[768,768]{1,0:T(8,128)}) custom-call(bf16[768,768]{1,0:T(8,128)(2,1)} %bitcast.209, f32[1,768]{1,0:T(1,128)} %get-tuple-element.302.gain_ref, ...), custom_call_target="tpu_custom_call" | custom-call | flops 22000001024 | tf_op jit(solution)/shard_map/pallas_call | solution.py:352
  170.1 33.2 %all-to-all-done.2 = bf16[4,112,2,768]{3,2,1,0:T(2,128)(2,1)S(1)} async-done(((bf16[4,112,2,768]{3,2,1,0:T(2,128)(2,1)}), bf16[4,112,2,768]{3,2,1,0:T(2,128)(2,1)S(1)}, u32[]{:S(2)}, u32[]{:S(2)}) %all-to-all-start.2) | async-done | bytes 1376288 | tf_op jit(solution)/shard_map/all_to_all | solution.py:629
  203.3 4.3 all-to-all-start.3
  211.2 2.6 copy.48
  213.8 25.5 %shard_map.273 = (bf16[1664,768]{1,0:T(8,128)(2,1)}, bf16[1664,2304]{1,0:T(8,128)(2,1)}, bf16[1664,768]{1,0:T(8,128)(2,1)}, f32[1664,768]{1,0:T(8,128)}, f32[1664,768]{1,0:T(8,128)}) custom-call(f32[896,768]{1,0:T(8,128)} %get-tuple-element.126.xa_ref, f32[768,768]{1,0:T(8,128)} %get-tuple-element.135.xb_ref, f32[1,768]{1,0:T(1,128)} %get-tuple-element.303.gain_ref, ...), custom_call_target="tpu_custom_call" | custom-call | flops 30000001024 | tf_op jit(solution)/shard_map/pallas_call | solution.py:207
  241.7 75.0 %shard_map.274 = (bf16[1664,768]{1,0:T(8,128)(2,1)}, f32[1664,768]{1,0:T(8,128)}, bf16[1664,768]{1,0:T(8,128)(2,1)}, bf16[16,2,96,1536]{3,2,1,0:T(8,128)(2,1)}, f32[1,3072]{1,0:T(1,128)}, /*index=5*/f32[8,768]{1,0:T(8,128)}) custom-call(f32[1664,768]{1,0:T(8,128)} %get-tuple-element.137.x_ref, bf16[896,768]{1,0:T(8,128)(2,1)} %bitcast.206, ...), custom_call_target="tpu_custom_call" | custom-call | flops 74999996416 | tf_op jit(solution)/shard_map/pallas_call | solution.py:114
  320.5 2.0 collective-permute-start.12
  322.5 2.4 collective-permute-start.13
  324.9 24.6 %shard_map.275 = (bf16[1664,2304]{1,0:T(8,128)(2,1)}, f32[896,768]{1,0:T(8,128)}, f32[768,768]{1,0:T(8,128)}, bf16[896,768]{1,0:T(8,128)(2,1)}, bf16[768,768]{1,0:T(8,128)(2,1)}, /*index=5*/f32[8,768]{1,0:T(8,128)}) custom-call(f32[1664,768]{1,0:T(8,128)} %get-tuple-element.143.g2_ref, bf16[1664,768]{1,0:T(8,128)(2,1)} %get-tuple-element.148.db_ref.refs_1_, ...), custom_call_target="tpu_custom_call" | custom-call | flops 24000000000 | tf_op jit(solution)/shard_map/pallas_call | solution.py:272
  349.5 25.0 %shard_map.276 = (bf16[1664,2304]{1,0:T(8,128)(2,1)}, f32[896,768]{1,0:T(8,128)}, f32[768,768]{1,0:T(8,128)}, bf16[896,768]{1,0:T(8,128)(2,1)}, bf16[768,768]{1,0:T(8,128)(2,1)}, /*index=5*/f32[8,768]{1,0:T(8,128)}) custom-call(f32[1664,768]{1,0:T(8,128)} %get-tuple-element.143.g2_ref,, ...), custom_call_target="tpu_custom_call", output_to_operand_aliasing={{0}: (7, {}), {1}: (8, {}), {2}: (9, {}), {3}: (10, {}), {4... | custom-call | flops 24000000000 | tf_op jit(solution)/shard_map/pallas_call | solution.py:272
  374.5 16.3 %shard_map.277 = (bf16[384,3072]{1,0:T(8,128)(2,1)}, bf16[384,3072]{1,0:T(8,128)(2,1)}) custom-call(s32[1,1]{1,0:T(1,128)} %bitcast.41.core_ref, bf16[1664,768]{1,0:T(8,128)(2,1)} %get-tuple-element.154.refs_0_, bf16[1664,768]{1,0:T(8,128)(2,1)} %get-tuple-element.148.db_ref.refs_1_, bf16[1664,2304]{1,0:T(8,128)(2,1)} %get-tuple-element.156.refs_2_, ...), custom_call_target="tpu_custom_call" | custom-call | flops 12000000000 | tf_op jit(solution)/shard_map/pallas_call | solution.py:489
  397.1 5.5 shard_map.278
  403.2 5.1 shard_map.279
  408.3 3.3 add_convert_fusion
  413.2 11.3 %shard_map.280 = (bf16[384,1536]{1,0:T(8,128)(2,1)}, bf16[384,1536]{1,0:T(8,128)(2,1)}) custom-call(s32[1,1]{1,0:T(1,128)} %bitcast.41.core_ref, bf16[896,768]{1,0:T(8,128)(2,1)} %get-tuple-element.162.refs_0_, bf16[768,768]{1,0:T(8,128)(2,1)} %get-tuple-element.167.refs_1_, bf16[896,768]{1,0:T(8,128)(2,1)} %get-tuple-element.168.refs_2_, ...), custom_call_target="tpu_custom_call" | custom-call | flops 6000000000 | tf_op jit(solution)/shard_map/pallas_call | solution.py:489
  429.3 22.0 %shard_map.281 = (bf16[896,2304]{1,0:T(8,128)(2,1)}, f32[8,768]{1,0:T(8,128)}) custom-call(bf16[896,768]{1,0:T(8,128)(2,1)} %get-tuple-element.174.do_ref, bf16[896,2304]{1,0:T(8,128)(2,1)} %get-tuple-element.175.qkv_ref, f32[896,128]{1,0:T(8,128)} %get-tuple-element.176.p_ref), custom_call_target="tpu_custom_call" | custom-call | flops 20000000000 | tf_op jit(solution)/shard_map/pallas_call | solution.py:429
  452.4 1.9 add_convert_fusion.2
  456.9 8.9 %shard_map.282 = (bf16[896,768]{1,0:T(8,128)(2,1)}, f32[8,768]{1,0:T(8,128)}) custom-call(bf16[896,2304]{1,0:T(8,128)(2,1)} %get-tuple-element.180.dqkv_ref.refs_2_, bf16[896,768]{1,0:T(8,128)(2,1)} %bitcast.205, f32[896,768]{1,0:T(8,128)} %get-tuple-element.181.g1_ref, f32[1,768]{1,0:T(1,128)} %get-tuple-element.302.gain_ref, bf16[768,3840]{1,0:T(8,128)(2,1)} %bitcast.182), custom_call_target="tpu_custom_call" | custom-call | flops 7000000000 | tf_op jit(solution)/shard_map/pallas_call | solution.py:444
  465.8 3.5 copy.74
  469.3 14.0 %all-to-all-start.4 = ((bf16[4,112,2,768]{3,2,1,0:T(2,128)(2,1)}), bf16[4,112,2,768]{3,2,1,0:T(2,128)(2,1)}, u32[]{:S(2)}, u32[]{:S(2)}) async-start(bf16[4,112,2,768]{3,2,1,0:T(2,128)(2,1)} %bitcast.186), calls=%async_computation.4 | async-start | bytes 2752512 | tf_op jit(solution)/shard_map/all_to_all | solution.py:644
  486.8 3.0 collective-permute-start.29
  491.3 18.8 %shard_map.283 = (bf16[768,2304]{1,0:T(8,128)(2,1)}, f32[8,768]{1,0:T(8,128)}) custom-call(bf16[768,768]{1,0:T(8,128)(2,1)} %get-tuple-element.186.do_ref, bf16[768,2304]{1,0:T(8,128)(2,1)} %get-tuple-element.187.qkv_ref, f32[768,128]{1,0:T(8,128)} %get-tuple-element.188.p_ref), custom_call_target="tpu_custom_call" | custom-call | flops 20000000000 | tf_op jit(solution)/shard_map/pallas_call | solution.py:429
  512.9 11.2 %shard_map.284 = (bf16[384,2304]{1,0:T(8,128)(2,1)}, bf16[384,2304]{1,0:T(8,128)(2,1)}) custom-call(s32[1,1]{1,0:T(1,128)} %bitcast.41.core_ref, bf16[896,768]{1,0:T(8,128)(2,1)} %get-tuple-element.141.refs_0_, bf16[768,768]{1,0:T(8,128)(2,1)} %get-tuple-element.142.refs_1_, bf16[896,2304]{1,0:T(8,128)(2,1)} %get-tuple-element.180.dqkv_ref.refs_2_, ...), custom_call_target="tpu_custom_call" | custom-call | flops 8999999488 | tf_op jit(solution)/shard_map/pallas_call | solution.py:489
  524.4 8.1 %shard_map.285 = (bf16[768,768]{1,0:T(8,128)(2,1)}, f32[8,768]{1,0:T(8,128)}) custom-call(bf16[768,2304]{1,0:T(8,128)(2,1)} %get-tuple-element.196.refs_3_.dqkv_ref, bf16[768,768]{1,0:T(8,128)(2,1)} %bitcast.210, f32[768,768]{1,0:T(8,128)} %get-tuple-element.197.g1_ref, f32[1,768]{1,0:T(1,128)} %get-tuple-element.302.gain_ref, bf16[768,3840]{1,0:T(8,128)(2,1)} %bitcast.183), custom_call_target="tpu_custom_call" | custom-call | flops 7000000000 | tf_op jit(solution)/shard_map/pallas_call | solution.py:444
  538.7 4.2 all-to-all-start.5
  553.9 18.2 %collective-permute-done.25 = f32[18,768]{1,0:T(8,128)S(1)} collective-permute-done((f32[18,768]{1,0:T(8,128)S(1)}, f32[18,768]{1,0:T(8,128)S(1)}, u32[]{:S(2)}, u32[]{:S(2)}) %collective-permute-start.25) | collective-permute-done | bytes 55328 | tf_op jit(solution)/shard_map/ppermute | solution.py:505
  572.4 3.8 collective-permute-start.37
  578.3 2.9 collective-permute-start.33
  581.2 2.5 fusion.7
  583.7 6.1 maximum_bitcast_fusion
  592.4 4.7 collective-permute-done.34
  598.6 5.9 maximum_bitcast_fusion.1
  (239 shorter events, 93.7 us)
Async XLA Ops:
  12.0 18.4 %collective-permute-start.2 = (bf16[24,6912]{1,0:T(8,128)(2,1)S(1)}, bf16[24,6912]{1,0:T(8,128)(2,1)S(1)}, u32[]{:S(2)}, u32[]{:S(2)}) collective-permute-start(bf16[24,6912]{1,0:T(8,128)(2,1)S(1)} %convert_dynamic-update-slice_fusion), channel_id=1, source_target_pairs={{0,2},{2,0},{4,6},{6,4},{1,3},{3,1},{5,7},{7,5},{8,10},{10,8},{12,... | collective-permute-start | bytes 995336 | tf_op jit(solution)/shard_map/ppermute | solution.py:505
  15.0 25.8 %collective-permute-start.1 = (bf16[24,6912]{1,0:T(8,128)(2,1)S(1)}, bf16[24,6912]{1,0:T(8,128)(2,1)S(1)}, u32[]{:S(2)}, u32[]{:S(2)}) collective-permute-start(bf16[24,6912]{1,0:T(8,128)(2,1)S(1)} %convert_dynamic-update-slice_fusion), channel_id=1, source_target_pairs={{0,4},{2,6},{4,0},{6,2},{1,5},{3,7},{5,1},{7,3},{8,12},{10,14},{12... | collective-permute-start | bytes 995336 | tf_op jit(solution)/shard_map/ppermute | solution.py:505
  17.6 23.3 %collective-permute-start = (bf16[24,6912]{1,0:T(8,128)(2,1)S(1)}, bf16[24,6912]{1,0:T(8,128)(2,1)}, u32[]{:S(2)}, u32[]{:S(2)}) collective-permute-start(bf16[24,6912]{1,0:T(8,128)(2,1)S(1)} %convert_dynamic-update-slice_fusion), channel_id=1, source_target_pairs={{0,6},{2,4},{4,2},{6,0},{1,7},{3,5},{5,3},{7,1},{8,14},{10,12},{12... | collective-permute-start | bytes 995336 | tf_op jit(solution)/shard_map/ppermute | solution.py:505
  42.1 40.2 %all-to-all-start = ((bf16[4,112,2,768]{3,2,1,0:T(2,128)(2,1)}), bf16[4,112,2,768]{3,2,1,0:T(2,128)(2,1)S(1)}, u32[]{:S(2)}, u32[]{:S(2)}) async-start(bf16[4,112,2,768]{3,2,1,0:T(2,128)(2,1)} %bitcast.185), calls=%async_computation | async-start | bytes 2752512 | tf_op jit(solution)/shard_map/all_to_all | solution.py:629
  50.8 190.9 %all-gather.2.cloned.1.call-start = ((), (), s32[]{:S(2)}) async-start(), calls=%async_computation.7 | async-start | bytes 9732096 | tf_op jit(solution)/shard_map/all_gather | solution.py:685
  51.7 19.6 %collective-permute-start.5 = (bf16[4,24,3840]{2,1,0:T(8,128)(2,1)}, bf16[4,24,3840]{2,1,0:T(8,128)(2,1)S(1)}, u32[]{:S(2)}, u32[]{:S(2)}) collective-permute-start(bf16[4,24,3840]{2,1,0:T(8,128)(2,1)} %slice.179), channel_id=1, source_target_pairs={{0,8},{8,0},{16,24},{24,16},{1,9},{9,1},{17,25},{25,17},{2,10},{10... | collective-permute-start | bytes 2211848 | tf_op jit(solution)/shard_map/ppermute | solution.py:505
  53.2 32.6 %collective-permute-start.4 = (bf16[4,24,3840]{2,1,0:T(8,128)(2,1)}, bf16[4,24,3840]{2,1,0:T(8,128)(2,1)}, u32[]{:S(2)}, u32[]{:S(2)}) collective-permute-start(bf16[4,24,3840]{2,1,0:T(8,128)(2,1)} %slice.179), channel_id=1, source_target_pairs={{0,16},{8,24},{16,0},{24,8},{1,17},{9,25},{17,1},{25,9},{2,18},{10... | collective-permute-start | bytes 2211848 | tf_op jit(solution)/shard_map/ppermute | solution.py:505
  54.7 31.1 %collective-permute-start.3 = (bf16[4,24,3840]{2,1,0:T(8,128)(2,1)}, bf16[4,24,3840]{2,1,0:T(8,128)(2,1)}, u32[]{:S(2)}, u32[]{:S(2)}) collective-permute-start(bf16[4,24,3840]{2,1,0:T(8,128)(2,1)} %slice.179), channel_id=1, source_target_pairs={{0,24},{8,16},{16,8},{24,0},{1,25},{9,17},{17,9},{25,1},{2,26},{10... | collective-permute-start | bytes 2211848 | tf_op jit(solution)/shard_map/ppermute | solution.py:505
  90.3 12.3 %collective-permute-start.6 = (bf16[4,4,24,3840]{3,2,1,0:T(8,128)(2,1)}, bf16[4,4,24,3840]{3,2,1,0:T(8,128)(2,1)}, u32[]{:S(2)}, u32[]{:S(2)}) collective-permute-start(bf16[4,4,24,3840]{3,2,1,0:T(8,128)(2,1)} %pad_maximum_fusion.2), channel_id=1, source_target_pairs={{0,1},{1,0},{2,3},{3,2},{4,5},{5,4},{6,7},{7,6},{8,9},{9,8},{10,11... | collective-permute-start | bytes 8847368 | tf_op jit(solution)/shard_map/ppermute | solution.py:505
  91.3 42.5 %collective-permute-start.9 = (bf16[4,24,3072]{2,1,0:T(8,128)(2,1)}, bf16[4,24,3072]{2,1,0:T(8,128)(2,1)S(1)}, u32[]{:S(2)}, u32[]{:S(2)}) collective-permute-start(bf16[4,24,3072]{2,1,0:T(8,128)(2,1)} %slice.180), channel_id=1, source_target_pairs={{0,8},{8,0},{16,24},{24,16},{1,9},{9,1},{17,25},{25,17},{2,10},{10... | collective-permute-start | bytes 1769480 | tf_op jit(solution)/shard_map/ppermute | solution.py:505
  92.5 41.3 %collective-permute-start.8 = (bf16[4,24,3072]{2,1,0:T(8,128)(2,1)}, bf16[4,24,3072]{2,1,0:T(8,128)(2,1)}, u32[]{:S(2)}, u32[]{:S(2)}) collective-permute-start(bf16[4,24,3072]{2,1,0:T(8,128)(2,1)} %slice.180), channel_id=1, source_target_pairs={{0,16},{8,24},{16,0},{24,8},{1,17},{9,25},{17,1},{25,9},{2,18},{10... | collective-permute-start | bytes 1769480 | tf_op jit(solution)/shard_map/ppermute | solution.py:505
  93.3 41.2 %collective-permute-start.7 = (bf16[4,24,3072]{2,1,0:T(8,128)(2,1)}, bf16[4,24,3072]{2,1,0:T(8,128)(2,1)}, u32[]{:S(2)}, u32[]{:S(2)}) collective-permute-start(bf16[4,24,3072]{2,1,0:T(8,128)(2,1)} %slice.180), channel_id=1, source_target_pairs={{0,24},{8,16},{16,8},{24,0},{1,25},{9,17},{17,9},{25,1},{2,26},{10... | collective-permute-start | bytes 1769480 | tf_op jit(solution)/shard_map/ppermute | solution.py:505
  94.8 43.3 %all-to-all-start.1 = ((bf16[4,84,2,768]{3,2,1,0:T(2,128)(2,1)}), bf16[4,84,2,768]{3,2,1,0:T(2,128)(2,1)}, u32[]{:S(2)}, u32[]{:S(2)}) async-start(bf16[4,84,2,768]{3,2,1,0:T(2,128)(2,1)} %bitcast.199), calls=%async_computation.1 | async-start | bytes 2064384 | tf_op jit(solution)/shard_map/all_to_all | solution.py:629
  138.1 70.8 %collective-permute-start.10 = (bf16[4,4,24,3072]{3,2,1,0:T(8,128)(2,1)}, bf16[4,4,24,3072]{3,2,1,0:T(8,128)(2,1)}, u32[]{:S(2)}, u32[]{:S(2)}) collective-permute-start(bf16[4,4,24,3072]{3,2,1,0:T(8,128)(2,1)} %pad_maximum_fusion.3), channel_id=1, source_target_pairs={{0,1},{1,0},{2,3},{3,2},{4,5},{5,4},{6,7},{7,6},{8,9},{9,8},{10,11... | collective-permute-start | bytes 7077896 | tf_op jit(solution)/shard_map/ppermute | solution.py:505
  138.1 65.2 %all-to-all-start.2 = ((bf16[4,112,2,768]{3,2,1,0:T(2,128)(2,1)}), bf16[4,112,2,768]{3,2,1,0:T(2,128)(2,1)S(1)}, u32[]{:S(2)}, u32[]{:S(2)}) async-start(bf16[4,112,2,768]{3,2,1,0:T(2,128)(2,1)} %bitcast.26), calls=%async_computation.2 | async-start | bytes 2752512 | tf_op jit(solution)/shard_map/all_to_all | solution.py:629
  203.3 36.0 %all-to-all-start.3 = ((bf16[4,84,2,768]{3,2,1,0:T(2,128)(2,1)}), bf16[4,84,2,768]{3,2,1,0:T(2,128)(2,1)}, u32[]{:S(2)}, u32[]{:S(2)}) async-start(bf16[4,84,2,768]{3,2,1,0:T(2,128)(2,1)} %bitcast.198), calls=%async_computation.3 | async-start | bytes 2064384 | tf_op jit(solution)/shard_map/all_to_all | solution.py:629
  207.5 316.8 %reduce-scatter.2.cloned.1.call-start = ((), (), s32[]{:S(2)}) async-start(), calls=%async_computation.8 | async-start | bytes 9732096 | tf_op jit(solution)/shard_map/reduce_scatter | solution.py:720
  320.5 28.9 %collective-permute-start.12 = (bf16[196,2,768]{2,1,0:T(2,128)(2,1)S(1)}, bf16[196,2,768]{2,1,0:T(2,128)(2,1)S(1)}, u32[]{:S(2)}, u32[]{:S(2)}) collective-permute-start(bf16[196,2,768]{2,1,0:T(2,128)(2,1)S(1)} %bitcast.216), channel_id=1, source_target_pairs={{0,2},{2,0},{4,6},{6,4},{1,3},{3,1},{5,7},{7,5},{8,10},{10,8},{12,... | collective-permute-start | bytes 1806344 | tf_op jit(solution)/shard_map/ppermute | solution.py:505
  322.5 51.9 %collective-permute-start.13 = (bf16[196,2,768]{2,1,0:T(2,128)(2,1)S(1)}, bf16[196,2,768]{2,1,0:T(2,128)(2,1)S(1)}, u32[]{:S(2)}, u32[]{:S(2)}) collective-permute-start(bf16[196,2,768]{2,1,0:T(2,128)(2,1)S(1)} %bitcast.215), channel_id=1, source_target_pairs={{0,4},{2,6},{4,0},{6,2},{1,5},{3,7},{5,1},{7,3},{8,12},{10,14},{12... | collective-permute-start | bytes 1806344 | tf_op jit(solution)/shard_map/ppermute | solution.py:505
  390.8 17.5 %collective-permute-start.14 = (bf16[16,24,3072]{2,1,0:T(8,128)(2,1)}, bf16[16,24,3072]{2,1,0:T(8,128)(2,1)}, u32[]{:S(2)}, u32[]{:S(2)}) collective-permute-start(bf16[16,24,3072]{2,1,0:T(8,128)(2,1)} %bitcast.222), channel_id=1, source_target_pairs={{0,1},{1,0},{2,3},{3,2},{4,5},{5,4},{6,7},{7,6},{8,9},{9,8},{10,11... | collective-permute-start | bytes 7077896 | tf_op jit(solution)/shard_map/ppermute | solution.py:505
  394.8 18.4 %collective-permute-start.11 = (bf16[196,2,768]{2,1,0:T(2,128)(2,1)}, bf16[196,2,768]{2,1,0:T(2,128)(2,1)S(1)}, u32[]{:S(2)}, u32[]{:S(2)}) collective-permute-start(bf16[196,2,768]{2,1,0:T(2,128)(2,1)} %bitcast.164), channel_id=1, source_target_pairs={{0,6},{2,4},{4,2},{6,0},{1,7},{3,5},{5,3},{7,1},{8,14},{10,12},{12... | collective-permute-start | bytes 1806344 | tf_op jit(solution)/shard_map/ppermute | solution.py:505
  424.5 26.8 %collective-permute-start.15 = (bf16[16,24,1536]{2,1,0:T(8,128)(2,1)}, bf16[16,24,1536]{2,1,0:T(8,128)(2,1)S(1)}, u32[]{:S(2)}, u32[]{:S(2)}) collective-permute-start(bf16[16,24,1536]{2,1,0:T(8,128)(2,1)} %bitcast.224), channel_id=1, source_target_pairs={{0,1},{1,0},{2,3},{3,2},{4,5},{5,4},{6,7},{7,6},{8,9},{9,8},{10,11... | collective-permute-start | bytes 3538952 | tf_op jit(solution)/shard_map/ppermute | solution.py:505
  425.8 57.6 %collective-permute-start.16 = (bf16[4,24,3072]{2,1,0:T(8,128)(2,1)}, bf16[4,24,3072]{2,1,0:T(8,128)(2,1)}, u32[]{:S(2)}, u32[]{:S(2)}) collective-permute-start(bf16[4,24,3072]{2,1,0:T(8,128)(2,1)} %get-tuple-element.254), channel_id=1, source_target_pairs={{0,8},{8,0},{16,24},{24,16},{1,9},{9,1},{17,25},{25,17},{2,10},{10... | collective-permute-start | bytes 1769480 | tf_op jit(solution)/shard_map/ppermute | solution.py:505
  427.4 56.0 %collective-permute-start.18 = (bf16[4,24,3072]{2,1,0:T(8,128)(2,1)}, bf16[4,24,3072]{2,1,0:T(8,128)(2,1)}, u32[]{:S(2)}, u32[]{:S(2)}) collective-permute-start(bf16[4,24,3072]{2,1,0:T(8,128)(2,1)} %get-tuple-element.255), channel_id=1, source_target_pairs={{0,24},{8,16},{16,8},{24,0},{1,25},{9,17},{17,9},{25,1},{2,26},{10... | collective-permute-start | bytes 1769480 | tf_op jit(solution)/shard_map/ppermute | solution.py:505
  428.7 54.7 %collective-permute-start.17 = (bf16[4,24,3072]{2,1,0:T(8,128)(2,1)}, bf16[4,24,3072]{2,1,0:T(8,128)(2,1)}, u32[]{:S(2)}, u32[]{:S(2)}) collective-permute-start(bf16[4,24,3072]{2,1,0:T(8,128)(2,1)} %get-tuple-element.256), channel_id=1, source_target_pairs={{0,16},{8,24},{16,0},{24,8},{1,17},{9,25},{17,1},{25,9},{2,18},{10... | collective-permute-start | bytes 1769480 | tf_op jit(solution)/shard_map/ppermute | solution.py:505
  455.2 54.9 %collective-permute-start.19 = (bf16[2,4,24,1536]{3,2,1,0:T(8,128)(2,1)}, bf16[2,4,24,1536]{3,2,1,0:T(8,128)(2,1)}, u32[]{:S(2)}, u32[]{:S(2)}) collective-permute-start(bf16[2,4,24,1536]{3,2,1,0:T(8,128)(2,1)} %dynamic-slice_bitcast_fusion), channel_id=1, source_target_pairs={{0,8},{8,0},{16,24},{24,16},{1,9},{9,1},{17,25},{25,17},{2,10},{10... | collective-permute-start | bytes 1769480 | tf_op jit(solution)/shard_map/ppermute | solution.py:525
  469.3 55.0 %all-to-all-start.4 = ((bf16[4,112,2,768]{3,2,1,0:T(2,128)(2,1)}), bf16[4,112,2,768]{3,2,1,0:T(2,128)(2,1)}, u32[]{:S(2)}, u32[]{:S(2)}) async-start(bf16[4,112,2,768]{3,2,1,0:T(2,128)(2,1)} %bitcast.186), calls=%async_computation.4 | async-start | bytes 2752512 | tf_op jit(solution)/shard_map/all_to_all | solution.py:644
  486.8 45.8 %collective-permute-start.29 = (bf16[24,3072]{1,0:T(8,128)(2,1)}, bf16[24,3072]{1,0:T(8,128)(2,1)S(1)}, u32[]{:S(2)}, u32[]{:S(2)}) collective-permute-start(bf16[24,3072]{1,0:T(8,128)(2,1)} %get-tuple-element.271), channel_id=1, source_target_pairs={{0,2},{2,0},{4,6},{6,4},{1,3},{3,1},{5,7},{7,5},{8,10},{10,8},{12,... | collective-permute-start | bytes 442376 | tf_op jit(solution)/shard_map/ppermute | solution.py:505
  489.8 42.7 %collective-permute-start.31 = (bf16[24,3072]{1,0:T(8,128)(2,1)}, bf16[24,3072]{1,0:T(8,128)(2,1)S(1)}, u32[]{:S(2)}, u32[]{:S(2)}) collective-permute-start(bf16[24,3072]{1,0:T(8,128)(2,1)} %get-tuple-element.272), channel_id=1, source_target_pairs={{0,6},{2,4},{4,2},{6,0},{1,7},{3,5},{5,3},{7,1},{8,14},{10,12},{12... | collective-permute-start | bytes 442376 | tf_op jit(solution)/shard_map/ppermute | solution.py:505
  491.3 41.3 %collective-permute-start.30 = (bf16[24,3072]{1,0:T(8,128)(2,1)}, bf16[24,3072]{1,0:T(8,128)(2,1)}, u32[]{:S(2)}, u32[]{:S(2)}) collective-permute-start(bf16[24,3072]{1,0:T(8,128)(2,1)} %get-tuple-element.273), channel_id=1, source_target_pairs={{0,4},{2,6},{4,0},{6,2},{1,5},{3,7},{5,1},{7,3},{8,12},{10,14},{12... | collective-permute-start | bytes 442376 | tf_op jit(solution)/shard_map/ppermute | solution.py:505
  511.3 12.8 %collective-permute-start.21 = (bf16[1,4,24,1536]{3,2,1,0:T(8,128)(2,1)S(1)}, bf16[1,4,24,1536]{3,2,1,0:T(8,128)(2,1)S(1)}, u32[]{:S(2)}, u32[]{:S(2)}) collective-permute-start(bf16[1,4,24,1536]{3,2,1,0:T(8,128)(2,1)S(1)} %constant_dynamic-slice_fusion.1), channel_id=1, source_target_pairs={{0,16},{8,24},{16,0},{24,8},{1,17},{9,25},{17,1},{25,9},{2,18},{10... | collective-permute-start | bytes 884744 | tf_op jit(solution)/shard_map/ppermute | solution.py:525
  524.1 18.8 %collective-permute-start.20 = (bf16[16,24,2304]{2,1,0:T(8,128)(2,1)}, bf16[16,24,2304]{2,1,0:T(8,128)(2,1)}, u32[]{:S(2)}, u32[]{:S(2)}) collective-permute-start(bf16[16,24,2304]{2,1,0:T(8,128)(2,1)} %bitcast.223), channel_id=1, source_target_pairs={{0,1},{1,0},{2,3},{3,2},{4,5},{5,4},{6,7},{7,6},{8,9},{9,8},{10,11... | collective-permute-start | bytes 5308424 | tf_op jit(solution)/shard_map/ppermute | solution.py:505
  535.7 9.1 %collective-permute-start.23 = (f32[18,768]{1,0:T(8,128)S(1)}, f32[18,768]{1,0:T(8,128)}, u32[]{:S(2)}, u32[]{:S(2)}) collective-permute-start(f32[18,768]{1,0:T(8,128)S(1)} %concatenate.23), channel_id=1, source_target_pairs={{0,1},{1,0},{2,3},{3,2},{4,5},{5,4},{6,7},{7,6},{8,9},{9,8},{10,11... | collective-permute-start | bytes 165896 | tf_op jit(solution)/shard_map/ppermute | solution.py:505
  538.7 59.9 %all-to-all-start.5 = ((bf16[4,84,2,768]{3,2,1,0:T(2,128)(2,1)}), bf16[4,84,2,768]{3,2,1,0:T(2,128)(2,1)S(1)}, u32[]{:S(2)}, u32[]{:S(2)}) async-start(bf16[4,84,2,768]{3,2,1,0:T(2,128)(2,1)} %bitcast.160), calls=%async_computation.6 | async-start | bytes 2064384 | tf_op jit(solution)/shard_map/all_to_all | solution.py:644
  545.8 6.1 %collective-permute-start.26 = (f32[18,768]{1,0:T(8,128)S(1)}, f32[18,768]{1,0:T(8,128)S(1)}, u32[]{:S(2)}, u32[]{:S(2)}) collective-permute-start(f32[18,768]{1,0:T(8,128)S(1)} %add.213), channel_id=1, source_target_pairs={{0,24},{8,16},{16,8},{24,0},{1,25},{9,17},{17,9},{25,1},{2,26},{10... | collective-permute-start | bytes 165896 | tf_op jit(solution)/shard_map/ppermute | solution.py:505
  546.8 25.3 %collective-permute-start.22 = (bf16[4,24,2304]{2,1,0:T(8,128)(2,1)S(1)}, bf16[4,24,2304]{2,1,0:T(8,128)(2,1)S(1)}, u32[]{:S(2)}, u32[]{:S(2)}) collective-permute-start(bf16[4,24,2304]{2,1,0:T(8,128)(2,1)S(1)} %get-tuple-element.261), channel_id=1, source_target_pairs={{0,8},{8,0},{16,24},{24,16},{1,9},{9,1},{17,25},{25,17},{2,10},{10... | collective-permute-start | bytes 1327112 | tf_op jit(solution)/shard_map/ppermute | solution.py:505
  548.2 24.0 %collective-permute-start.28 = (bf16[4,24,2304]{2,1,0:T(8,128)(2,1)S(1)}, bf16[4,24,2304]{2,1,0:T(8,128)(2,1)S(1)}, u32[]{:S(2)}, u32[]{:S(2)}) collective-permute-start(bf16[4,24,2304]{2,1,0:T(8,128)(2,1)S(1)} %get-tuple-element.262), channel_id=1, source_target_pairs={{0,24},{8,16},{16,8},{24,0},{1,25},{9,17},{17,9},{25,1},{2,26},{10... | collective-permute-start | bytes 1327112 | tf_op jit(solution)/shard_map/ppermute | solution.py:505
  549.6 31.6 %copy-start.18 = (bf16[196,2,768]{2,1,0:T(2,128)(2,1)S(1)}, bf16[196,2,768]{2,1,0:T(2,128)(2,1)}, u32[]{:S(2)}) copy-start(bf16[196,2,768]{2,1,0:T(2,128)(2,1)} %copy-done.17) | copy-start | bytes 1806340
  549.6 31.6 %copy-start.20 = (bf16[196,2,768]{2,1,0:T(2,128)(2,1)S(1)}, bf16[196,2,768]{2,1,0:T(2,128)(2,1)}, u32[]{:S(2)}) copy-start(bf16[196,2,768]{2,1,0:T(2,128)(2,1)} %copy-done.19) | copy-start | bytes 1806340
  549.6 22.5 %collective-permute-start.27 = (bf16[4,24,2304]{2,1,0:T(8,128)(2,1)S(1)}, bf16[4,24,2304]{2,1,0:T(8,128)(2,1)S(1)}, u32[]{:S(2)}, u32[]{:S(2)}) collective-permute-start(bf16[4,24,2304]{2,1,0:T(8,128)(2,1)S(1)} %get-tuple-element.263), channel_id=1, source_target_pairs={{0,16},{8,24},{16,0},{24,8},{1,17},{9,25},{17,1},{25,9},{2,18},{10... | collective-permute-start | bytes 1327112 | tf_op jit(solution)/shard_map/ppermute | solution.py:505
  550.4 21.7 %collective-permute-start.25 = (f32[18,768]{1,0:T(8,128)S(1)}, f32[18,768]{1,0:T(8,128)S(1)}, u32[]{:S(2)}, u32[]{:S(2)}) collective-permute-start(f32[18,768]{1,0:T(8,128)S(1)} %add.213), channel_id=1, source_target_pairs={{0,16},{8,24},{16,0},{24,8},{1,17},{9,25},{17,1},{25,9},{2,18},{10... | collective-permute-start | bytes 165896 | tf_op jit(solution)/shard_map/ppermute | solution.py:505
  551.9 20.2 %collective-permute-start.24 = (f32[18,768]{1,0:T(8,128)S(1)}, f32[18,768]{1,0:T(8,128)S(1)}, u32[]{:S(2)}, u32[]{:S(2)}) collective-permute-start(f32[18,768]{1,0:T(8,128)S(1)} %add.213), channel_id=1, source_target_pairs={{0,8},{8,0},{16,24},{24,16},{1,9},{9,1},{17,25},{25,17},{2,10},{10... | collective-permute-start | bytes 165896 | tf_op jit(solution)/shard_map/ppermute | solution.py:505
  572.4 17.4 %collective-permute-start.37 = (f32[18,768]{1,0:T(8,128)S(1)}, f32[18,768]{1,0:T(8,128)S(1)}, u32[]{:S(2)}, u32[]{:S(2)}) collective-permute-start(f32[18,768]{1,0:T(8,128)S(1)} %add_add_fusion.1), channel_id=1, source_target_pairs={{0,6},{2,4},{4,2},{6,0},{1,7},{3,5},{5,3},{7,1},{8,14},{10,12},{12... | collective-permute-start | bytes 165896 | tf_op jit(solution)/shard_map/ppermute | solution.py:505
  576.1 13.8 %collective-permute-start.36 = (f32[18,768]{1,0:T(8,128)S(1)}, f32[18,768]{1,0:T(8,128)S(1)}, u32[]{:S(2)}, u32[]{:S(2)}) collective-permute-start(f32[18,768]{1,0:T(8,128)S(1)} %add_add_fusion.1), channel_id=1, source_target_pairs={{0,4},{2,6},{4,0},{6,2},{1,5},{3,7},{5,1},{7,3},{8,12},{10,14},{12... | collective-permute-start | bytes 165896 | tf_op jit(solution)/shard_map/ppermute | solution.py:505
  576.2 13.7 %collective-permute-start.35 = (f32[18,768]{1,0:T(8,128)S(1)}, f32[18,768]{1,0:T(8,128)S(1)}, u32[]{:S(2)}, u32[]{:S(2)}) collective-permute-start(f32[18,768]{1,0:T(8,128)S(1)} %add_add_fusion.1), channel_id=1, source_target_pairs={{0,2},{2,0},{4,6},{6,4},{1,3},{3,1},{5,7},{7,5},{8,10},{10,8},{12,... | collective-permute-start | bytes 165896 | tf_op jit(solution)/shard_map/ppermute | solution.py:505
  576.9 15.5 %collective-permute-start.32 = (bf16[24,3840]{1,0:T(8,128)(2,1)S(1)}, bf16[24,3840]{1,0:T(8,128)(2,1)S(1)}, u32[]{:S(2)}, u32[]{:S(2)}) collective-permute-start(bf16[24,3840]{1,0:T(8,128)(2,1)S(1)} %get-tuple-element.268), channel_id=1, source_target_pairs={{0,2},{2,0},{4,6},{6,4},{1,3},{3,1},{5,7},{7,5},{8,10},{10,8},{12,... | collective-permute-start | bytes 552968 | tf_op jit(solution)/shard_map/ppermute | solution.py:505
  578.3 14.1 %collective-permute-start.33 = (bf16[24,3840]{1,0:T(8,128)(2,1)S(1)}, bf16[24,3840]{1,0:T(8,128)(2,1)S(1)}, u32[]{:S(2)}, u32[]{:S(2)}) collective-permute-start(bf16[24,3840]{1,0:T(8,128)(2,1)S(1)} %get-tuple-element.269), channel_id=1, source_target_pairs={{0,4},{2,6},{4,0},{6,2},{1,5},{3,7},{5,1},{7,3},{8,12},{10,14},{12... | collective-permute-start | bytes 552968 | tf_op jit(solution)/shard_map/ppermute | solution.py:505
  589.8 7.3 %collective-permute-start.34 = (bf16[24,3840]{1,0:T(8,128)(2,1)S(1)}, bf16[24,3840]{1,0:T(8,128)(2,1)S(1)}, u32[]{:S(2)}, u32[]{:S(2)}) collective-permute-start(bf16[24,3840]{1,0:T(8,128)(2,1)S(1)} %get-tuple-element.270), channel_id=1, source_target_pairs={{0,6},{2,4},{4,2},{6,0},{1,7},{3,5},{5,3},{7,1},{8,14},{10,12},{12... | collective-permute-start | bytes 552968 | tf_op jit(solution)/shard_map/ppermute | solution.py:505
  (40 other events, 383.7 us)
Sparse Core Ops, SparseCore 0:
  90.4 112.8 all-gather.1
  318.7 178.6 reduce-scatter.1
